TPU v7x, 32 devices: a whole 2x2x4 slice. The times are simulated.
32 devices in a mesh: groups: 2 (over x), blk: 16 (over z, y, core).
Axes of the slice: x: 2, y: 2, z: 4, core: 2. Of those that a mesh axis runs over, the one named last changes fastest.
Arguments:
- embeddings: float32 [8192, 768], P(('groups', 'blk')), parts along dimension 0, may hold values from -6 to 6
- dest_pos: int32 [8192], P(('groups', 'blk')), parts along dimension 0, may hold values from 0 to 4095, as said below
- cluster_lengths: int32 [8], P('groups'), parts along dimension 0, may hold values from 1 to 2048, 4096 in all
- block_mask: int32 [32, 16], P('groups'), parts along dimension 0, may hold values 0 or 1
Outputs:
- top_cosine: float32 [8192], P(('groups', 'blk')), parts along dimension 0
- dup_direction: bfloat16 [8192, 768], P(('groups', 'blk')), parts along dimension 0
There are 2 independent parts, one for each index of `groups`. A program takes and returns all parts, laid end to end along the dimension named above; each array names one. Nothing has to cross between parts.
Inputs may be any that keep to these rules, and one draw needn't show every extreme that they name: `dest_pos`: a permutation of the positions; at most 32 rows of one device's 256 rows have positions in one aligned block of 256 positions, and this bound is reached in every draw.
All inputs are finite; a program needn't handle non-finite values.
Results may differ from a plain program's by a relative error of at most 0.0055.
Values may be sent and summed in bfloat16 or wider, within the bound.
No kernel may reach another device: no remote copies, remote signals or barrier semaphores. Data moves between devices by JAX's collectives and lax.ppermute only.
A program may use at most 64 MiB of HBM per device.

v0:
```python
import jax
import jax.numpy as jnp
from jax import lax
from jax.sharding import PartitionSpec as P

EPS = 1e-06
TEMP = 4.0


def cluster_of(positions, cluster_lengths):
    ends = jnp.cumsum(cluster_lengths)
    return jnp.sum((positions[:, None] >= ends[None, :-1]).astype(jnp.int32), axis=1)


def fold_pair(
    carry, queries, query_pos, query_cl, query_mask, piece, key_pos, cluster_lengths, rows, count
):
    key_cl = cluster_of(key_pos, cluster_lengths)
    scores = lax.dot_general(
        queries, piece, (((1,), (1,)), ((), ())), preferred_element_type=jnp.float32
    )
    same = query_cl[:, None] == key_cl[None, :]
    earlier = same & (key_pos[None, :] < query_pos[:, None])
    top = jnp.maximum(carry[0], jnp.max(jnp.where(earlier, scores, jnp.float32(-1.0)), axis=1))
    key_onehot = ((key_pos // rows)[:, None] == jnp.arange(count, dtype=jnp.int32)[None, :]).astype(
        jnp.float32
    )
    key_mask = lax.dot_general(
        query_mask, key_onehot, (((1,), (1,)), ((), ())), preferred_element_type=jnp.float32
    )
    allowed = same & ((key_mask > 0.5) | (key_pos[None, :] == query_pos[:, None]))
    weights = jnp.where(allowed, jnp.exp(TEMP * scores), jnp.float32(0.0)).astype(jnp.bfloat16)
    total = jnp.dot(weights, piece, preferred_element_type=jnp.float32)
    return (top, total)


def per_device(embeddings, dest_pos, cluster_lengths, block_mask):
    rows = embeddings.shape[0]
    width = embeddings.shape[1]
    count = lax.axis_size("blk")
    normed = embeddings * lax.rsqrt(jnp.sum(embeddings * embeddings, axis=1, keepdims=True) + EPS)
    unit = normed.astype(jnp.bfloat16)
    mask_float = block_mask.astype(jnp.float32)
    top_init = jnp.full((rows,), -1.0, jnp.float32)
    total_init = jnp.zeros((rows, width), jnp.float32)
    cap = 2 * rows // count
    me = lax.axis_index("blk")
    dest_dev = dest_pos // rows
    local = dest_pos % rows
    onehot = (dest_dev[:, None] == jnp.arange(count, dtype=jnp.int32)[None, :]).astype(jnp.int32)
    before = jnp.cumsum(onehot, axis=0) - onehot
    slot = jnp.sum(before * onehot, axis=1)
    where_to = dest_dev * cap + slot
    send_rows = jnp.zeros((count * cap, width), jnp.bfloat16).at[where_to].set(unit)
    send_pos = jnp.full((count * cap,), -1, jnp.int32).at[where_to].set(local)
    got_rows, got_pos = (
        lax.all_to_all(
            send_rows.reshape(count, cap, width), "blk", split_axis=0, concat_axis=0, tiled=True
        ),
        lax.all_to_all(
            send_pos.reshape(count, cap), "blk", split_axis=0, concat_axis=0, tiled=True
        ),
    )
    flat_pos = got_pos.reshape(count * cap)
    placed = jnp.where(flat_pos >= 0, flat_pos, rows)
    block = (
        jnp.zeros((rows, width), jnp.bfloat16)
        .at[placed]
        .set(got_rows.reshape(count * cap, width), mode="drop")
    )
    my_pos = me * rows + jnp.arange(rows, dtype=jnp.int32)
    my_cl = cluster_of(my_pos, cluster_lengths)
    my_onehot = ((my_pos // rows)[:, None] == jnp.arange(count, dtype=jnp.int32)[None, :]).astype(
        jnp.float32
    )
    my_mask = jnp.dot(my_onehot, mask_float, preferred_element_type=jnp.float32)
    piece = lax.all_gather(block, "blk", axis=0, tiled=True)
    key_pos = jnp.arange(piece.shape[0], dtype=jnp.int32)
    top, total = fold_pair(
        (top_init, total_init),
        block,
        my_pos,
        my_cl,
        my_mask,
        piece,
        key_pos,
        cluster_lengths,
        rows,
        count,
    )
    scale = jnp.sqrt(jnp.float32(width)) * lax.rsqrt(
        jnp.sum(total * total, axis=1, keepdims=True) + EPS
    )
    direction = (total * scale).astype(jnp.bfloat16)
    fetch = jnp.clip(flat_pos, 0, rows - 1)
    back_dir = direction[fetch].reshape(count, cap, width)
    back_top = top[fetch].reshape(count, cap)
    home_dir, home_top = (
        lax.all_to_all(back_dir, "blk", split_axis=0, concat_axis=0, tiled=True),
        lax.all_to_all(
            back_top.astype(jnp.bfloat16), "blk", split_axis=0, concat_axis=0, tiled=True
        ).astype(back_top.dtype),
    )
    out_dir = home_dir.reshape(count * cap, width)[where_to]
    out_top = home_top.reshape(count * cap)[where_to]
    return (out_top, out_dir)


def solution(mesh):
    placed = (P(("groups", "blk"), None), P(("groups", "blk")), P("groups"), P("groups", None))
    return jax.shard_map(
        per_device,
        mesh=mesh,
        in_specs=placed,
        out_specs=(P(("groups", "blk")), P(("groups", "blk"), None)),
        check_vma=False,
    )
```

profile of v0, /device:TPU:0, one launch (start us, length us, event | category | flops | bytes accessed | tf_op | source)
XLA Modules:
  0.0 172.6 jit_solution(14815166338834683179)
XLA Ops:
  7.2 0.7 and_select_fusion.1
  7.9 0.6 reduce-window.11
  8.5 0.2 slice_reduce_fusion
  8.7 0.1 fusion.23
  8.8 1.4 scatter_custom_fusion
  10.2 0.7 all_to_all.16
  10.9 7.4 %all-to-all-start = ((s32[16,1,32]{2,1,0:T(1,128)}), s32[16,1,32]{2,1,0:T(1,128)S(1)}, u32[]{:S(2)}, u32[]{:S(2)}) async-start(s32[16,1,32]{2,1,0:T(1,128)} %all_to_all.16), calls=%async_computation | async-start | bytes 16384 | tf_op jit(solution)/shard_map/all_to_all | solution.py:60
  18.3 1.3 multiply_reduce_fusion.1
  19.6 3.2 %scatter_custom_fusion.1 = bf16[512,768]{1,0:T(8,128)(2,1)} fusion(s32[256]{0:T(256)S(1)} %compare_select_fusion.3, f32[256,768]{1,0:T(8,128)} %param.4, f32[256]{0:T(256)S(1)} %add_rsqrt_fusion, bf16[]{:T(256)} %constant.72.clone.1), kind=kCustom, calls=%fused_computation.27 | custom fusion | flops 393216 | bytes 1573890 | tf_op jit(solution)/shard_map/scatter | solution.py:54
  22.8 1.8 %all-to-all-done = s32[16,1,32]{2,1,0:T(1,128)S(1)} async-done(((s32[16,1,32]{2,1,0:T(1,128)}), s32[16,1,32]{2,1,0:T(1,128)S(1)}, u32[]{:S(2)}, u32[]{:S(2)}) %all-to-all-start) | async-done | bytes 2080 | tf_op jit(solution)/shard_map/all_to_all | solution.py:60
  24.6 4.2 %all-to-all-start.1 = ((bf16[16,32,768]{2,1,0:T(8,128)(2,1)}), bf16[16,32,768]{2,1,0:T(8,128)(2,1)S(1)}, u32[]{:S(2)}, u32[]{:S(2)}) async-start(bf16[16,32,768]{2,1,0:T(8,128)(2,1)} %bitcast.5), calls=%async_computation.1 | async-start | bytes 1572864 | tf_op jit(solution)/shard_map/all_to_all | solution.py:57
  28.9 0.5 broadcast.231
  29.4 0.7 reduce.9
  30.2 17.4 %all-to-all-done.1 = bf16[16,32,768]{2,1,0:T(8,128)(2,1)S(1)} async-done(((bf16[16,32,768]{2,1,0:T(8,128)(2,1)}), bf16[16,32,768]{2,1,0:T(8,128)(2,1)S(1)}, u32[]{:S(2)}, u32[]{:S(2)}) %all-to-all-start.1) | async-done | bytes 786464 | tf_op jit(solution)/shard_map/all_to_all | solution.py:57
  47.5 3.3 %scatter_custom_fusion.2 = bf16[256,768]{1,0:T(8,128)(2,1)} fusion(s32[512]{0:T(512)S(1)} %bitcast.37, bf16[512,768]{1,0:T(8,128)(2,1)S(1)} %bitcast.34, bf16[]{:T(256)} %constant.72.clone.1), kind=kCustom, calls=%fused_computation.31 | custom fusion | bytes 393218 | tf_op jit(solution)/shard_map/scatter | solution.py:69
  50.9 0.2 reduce-window.10
  51.1 0.1 convert_reduce_fusion.2
  51.2 0.1 convert_reduce_fusion
  51.3 0.2 fusion.17
  51.6 62.1 %all-gather.2.cloned.1.call-done = bf16[4096,768]{1,0:T(8,128)(2,1)} async-done(((bf16[256,768]{1,0:T(8,128)(2,1)}), bf16[4096,768]{1,0:T(8,128)(2,1)}) %all-gather.2.cloned.1.call-update) | async-done | bytes 6291472 | tf_op jit(solution)/shard_map/all_gather | solution.py:77
  113.7 7.1 %select_reduce_fusion = (bf16[256]{0:T(256)(128)(2,1)S(1)}, f32[256,4096]{1,0:T(8,128)}) fusion(s32[256]{0:T(256)S(1)} %get-tuple-element.11, s32[4096]{0:T(1024)S(1)} %convert_reduce_fusion, s32[256]{0:T(256)S(1)} %convert_reduce_fusion.2, bf16[256,768]{1,0:T(8,128)(2,1)} %scatter_custom_fusion.2, bf16[4096,768]{1,0:T(8,128)(2,1)} %all-gather.2.cloned.1.call-done), kind=kOutput, calls=%fused_computation.14 | convolution fusion | flops 1615855360 | bytes 10897920 | tf_op jit(solution)/shard_map/dot_general | solution.py:19
  120.8 6.9 %multiply_reduce_fusion = (f32[256]{0:T(256)S(1)}, f32[256,768]{1,0:T(8,128)S(1)}) fusion(bf16[4096,768]{1,0:T(8,128)(2,1)} %all-gather.2.cloned.1.call-done, bf16[256,16]{0,1:T(8,128)(2,1)S(1)} %fusion.17, f32[256,4096]{1,0:T(8,128)} %get-tuple-element.7, s32[256]{0:T(256)S(1)} %get-tuple-element.11, s32[4096]{0:T(1024)S(1)} %convert_reduce_fusion, ...), kind=kOutput, calls=%fused_computation.24 | convolution fusion | flops 1653014272 | bytes 11316224 | tf_op jit(solution)/shard_map/dot_general | solution.py:33
  127.7 3.4 %gather_fusion = bf16[512]{0:T(512)(128)(2,1)S(1)} fusion(bf16[256]{0:T(256)(128)(2,1)S(1)} %broadcast_maximum_fusion, s32[1024]{0:T(1024)S(1)} %pad_clamp_fusion.1), kind=kCustom, calls=%fused_computation | custom fusion | bytes 4096 | tf_op jit(solution)/shard_map/gather | solution.py:97
  131.1 0.7 convert_element_type.60
  131.7 3.5 %all-to-all-start.2 = ((bf16[16,1,32]{2,1,0:T(2,128)(2,1)}), bf16[16,1,32]{2,1,0:T(2,128)(2,1)S(1)}, u32[]{:S(2)}, u32[]{:S(2)}) async-start(bf16[16,1,32]{2,1,0:T(2,128)(2,1)} %convert_element_type.60), calls=%async_computation.2 | async-start | bytes 16384 | tf_op jit(solution)/shard_map/all_to_all | solution.py:100
  135.2 0.1 multiply_convert_fusion
  135.3 2.7 %gather_fusion.2 = bf16[512,768]{1,0:T(8,128)(2,1)} fusion(bf16[256,768]{1,0:T(8,128)(2,1)S(1)} %multiply_convert_fusion, s32[1024]{0:T(1024)S(1)} %pad_clamp_fusion.1), kind=kCustom, calls=%fused_computation.2 | custom fusion | bytes 1574912 | tf_op jit(solution)/shard_map/gather | solution.py:96
  138.1 3.5 %all-to-all-done.2 = bf16[16,1,32]{2,1,0:T(2,128)(2,1)S(1)} async-done(((bf16[16,1,32]{2,1,0:T(2,128)(2,1)}), bf16[16,1,32]{2,1,0:T(2,128)(2,1)S(1)}, u32[]{:S(2)}, u32[]{:S(2)}) %all-to-all-start.2) | async-done | bytes 1056 | tf_op jit(solution)/shard_map/all_to_all | solution.py:100
  141.5 3.6 %all-to-all-start.3 = ((bf16[16,32,768]{2,1,0:T(8,128)(2,1)}), bf16[16,32,768]{2,1,0:T(8,128)(2,1)S(1)}, u32[]{:S(2)}, u32[]{:S(2)}) async-start(bf16[16,32,768]{2,1,0:T(8,128)(2,1)} %bitcast.8), calls=%async_computation.3 | async-start | bytes 1572864 | tf_op jit(solution)/shard_map/all_to_all | solution.py:99
  145.3 2.5 %gather_fusion.1 = f32[256]{0:T(256)} fusion(f32[512]{0:T(512)S(1)} %reshape.170, s32[1024]{0:T(1024)S(1)} %pad_clamp_fusion), kind=kCustom, calls=%fused_computation.1 | custom fusion | bytes 3072 | tf_op jit(solution)/shard_map/gather | solution.py:105
  147.8 16.0 %all-to-all-done.3 = bf16[16,32,768]{2,1,0:T(8,128)(2,1)S(1)} async-done(((bf16[16,32,768]{2,1,0:T(8,128)(2,1)}), bf16[16,32,768]{2,1,0:T(8,128)(2,1)S(1)}, u32[]{:S(2)}, u32[]{:S(2)}) %all-to-all-start.3) | async-done | bytes 786464 | tf_op jit(solution)/shard_map/all_to_all | solution.py:99
  163.8 1.9 %gather_fusion.3 = bf16[256,768]{1,0:T(8,128)(2,1)} fusion(bf16[512,768]{1,0:T(8,128)(2,1)S(1)} %bitcast.33, s32[1024]{0:T(1024)S(1)} %pad_clamp_fusion), kind=kCustom, calls=%fused_computation.3 | custom fusion | bytes 787456 | tf_op jit(solution)/shard_map/gather | solution.py:104
  (22 shorter events, 0.4 us)
Async XLA Ops:
  7.2 43.7 %copy-start.1 = (s32[4]{0:T(128)S(1)}, s32[4]{0:T(128)}, u32[]{:S(2)}) copy-start(s32[4]{0:T(128)} %param.6) | copy-start | bytes 52
  7.2 44.1 %copy-start = (s32[16,16]{1,0:T(8,128)S(1)}, s32[16,16]{1,0:T(8,128)}, u32[]{:S(2)}) copy-start(s32[16,16]{1,0:T(8,128)} %param.7) | copy-start | bytes 3076
  10.9 13.7 %all-to-all-start = ((s32[16,1,32]{2,1,0:T(1,128)}), s32[16,1,32]{2,1,0:T(1,128)S(1)}, u32[]{:S(2)}, u32[]{:S(2)}) async-start(s32[16,1,32]{2,1,0:T(1,128)} %all_to_all.16), calls=%async_computation | async-start | bytes 16384 | tf_op jit(solution)/shard_map/all_to_all | solution.py:60
  24.6 22.9 %all-to-all-start.1 = ((bf16[16,32,768]{2,1,0:T(8,128)(2,1)}), bf16[16,32,768]{2,1,0:T(8,128)(2,1)S(1)}, u32[]{:S(2)}, u32[]{:S(2)}) async-start(bf16[16,32,768]{2,1,0:T(8,128)(2,1)} %bitcast.5), calls=%async_computation.1 | async-start | bytes 1572864 | tf_op jit(solution)/shard_map/all_to_all | solution.py:57
  28.8 84.9 %all-gather.2.cloned.1.call-start = ((), (), s32[]{:S(2)}) async-start(), calls=%async_computation.4 | async-start | bytes 6684672 | tf_op jit(solution)/shard_map/all_gather | solution.py:77
  131.7 9.8 %all-to-all-start.2 = ((bf16[16,1,32]{2,1,0:T(2,128)(2,1)}), bf16[16,1,32]{2,1,0:T(2,128)(2,1)S(1)}, u32[]{:S(2)}, u32[]{:S(2)}) async-start(bf16[16,1,32]{2,1,0:T(2,128)(2,1)} %convert_element_type.60), calls=%async_computation.2 | async-start | bytes 16384 | tf_op jit(solution)/shard_map/all_to_all | solution.py:100
  141.5 22.3 %all-to-all-start.3 = ((bf16[16,32,768]{2,1,0:T(8,128)(2,1)}), bf16[16,32,768]{2,1,0:T(8,128)(2,1)S(1)}, u32[]{:S(2)}, u32[]{:S(2)}) async-start(bf16[16,32,768]{2,1,0:T(8,128)(2,1)} %bitcast.8), calls=%async_computation.3 | async-start | bytes 1572864 | tf_op jit(solution)/shard_map/all_to_all | solution.py:99
Sparse Core Ops, SparseCore 0:
  51.0 62.6 all-gather.1
where the time goes:
time: 173 us
  waiting for transfers between devices  101 us (58%)
  starting transfers between devices  18.7 us (11%)
  local copies, waits for them, and re-layouts  17.5 us (10%)
  matrix products  14.2 us (8%)
  between operations  14.2 us (8%)
  other arithmetic  7.17 us (4%)
    all_gather x1, waiting for transfers between devices, per_device(): piece = lax.all_gather(block, 'blk', axis=0, tiled=True)  62.1 us
    all_to_all x1, waiting for transfers between devices, per_device(): lax.all_to_all(send_rows.reshape(count, cap, width), 'blk', split_axis=0,...  17.4 us
    all_to_all x1, waiting for transfers between devices, per_device(): lax.all_to_all(back_dir, 'blk', split_axis=0, concat_axis=0, tiled=True)  16 us
    all_to_all x1, starting transfers between devices, per_device(): lax.all_to_all(send_pos.reshape(count, cap), 'blk', split_axis=0, concat_...  7.39 us
    dot_general x1, matrix products, fold_pair(): lax.dot_general(queries, piece, (((1,), (1,)), ((), ())), preferred_eleme...  7.08 us
    dot_general x1, matrix products, fold_pair(): total = jnp.dot(weights, piece, preferred_element_type=jnp.float32)  6.91 us
    all_to_all x1, starting transfers between devices, per_device(): lax.all_to_all(send_rows.reshape(count, cap, width), 'blk', split_axis=0,...  4.19 us
    all_to_all x1, starting transfers between devices, per_device(): lax.all_to_all(back_dir, 'blk', split_axis=0, concat_axis=0, tiled=True)  3.61 us
  transfers between devices with their start and end apart: 5, of which 5 were waited for; matrix products, arithmetic and copies ran while one was open for 7% of the time, Pallas kernels for 0%

commit v1 on v0

v1 whole, which is shorter than its diff:
```python
import functools
import math

import jax
import jax.numpy as jnp
from jax import lax
from jax.experimental import pallas as pl
from jax.experimental.pallas import tpu as pltpu
from jax.sharding import PartitionSpec as P

EPS = 1e-06
TEMP = 4.0
LANES = 128
SPLIT = 128.0
TAIL = 8
VMEM_LIMIT = 48 * 1024 * 1024


def ring_order(chips):
    if chips <= 8:
        return list(range(0, chips, 2)) + list(range(1, chips, 2))[::-1]
    return list(range(chips))


def ring_perm(count, shift):
    order = ring_order(count // 2)
    pairs = []
    for at, chip in enumerate(order):
        to = order[(at + shift) % len(order)]
        pairs += [(2 * chip + core, 2 * to + core) for core in range(2)]
    return pairs


def call(body, out_shape, in_specs, flops, nbytes):
    many = isinstance(out_shape, (tuple, list))
    vmem = pl.BlockSpec(memory_space=pltpu.VMEM)
    return pl.pallas_call(
        body,
        out_shape=out_shape,
        in_specs=in_specs,
        out_specs=[vmem] * len(out_shape) if many else vmem,
        compiler_params=pltpu.CompilerParams(vmem_limit_bytes=VMEM_LIMIT),
        cost_estimate=pl.CostEstimate(flops=flops, bytes_accessed=nbytes, transcendentals=0),
    )


VM = pl.BlockSpec(memory_space=pltpu.VMEM)
SM = pl.BlockSpec(memory_space=pltpu.SMEM)


def prep_body(emb_ref, pos_ref, a_ref, b_ref, ah_ref, bh_ref):
    half = ah_ref.shape[0]
    pos = pos_ref[...].astype(jnp.float32)
    high = jnp.floor(pos * (1.0 / SPLIT))
    low = pos - high * SPLIT
    width = emb_ref.shape[1]
    row = jnp.concatenate(
        [high[0:1], low[0:1], high[1:2], low[1:2], jnp.zeros((1, width - 4 * half), jnp.float32)],
        axis=1,
    )
    tail = jnp.broadcast_to(row, (TAIL, width)).astype(jnp.bfloat16)
    for at, whole, alone in ((0, a_ref, ah_ref), (half, b_ref, bh_ref)):
        emb = emb_ref[at : at + half, :]
        unit = emb * lax.rsqrt(jnp.sum(emb * emb, axis=1, keepdims=True) + EPS)
        unit = unit.astype(jnp.bfloat16)
        alone[...] = unit
        whole[...] = jnp.concatenate([unit, tail], axis=0)


def rows_of(ref, half):
    return ref[...][:half]


def positions_of(ref, half):
    tail = ref[...][half:].astype(jnp.float32)
    return [
        tail[0:1, 2 * i * half : (2 * i + 1) * half] * SPLIT
        + tail[0:1, (2 * i + 1) * half : (2 * i + 2) * half]
        for i in range(2)
    ]


def column(row):
    size = row.shape[1]
    eye = lax.broadcasted_iota(jnp.int32, (size, size), 0) == lax.broadcasted_iota(
        jnp.int32, (size, size), 1
    )
    return jnp.sum(jnp.where(eye, row, 0.0), axis=1, keepdims=True)


def cluster_parts(pos, ends, clusters):
    index = jnp.zeros(pos.shape, jnp.int32)
    start = jnp.zeros(pos.shape, jnp.float32)
    for c in range(clusters - 1):
        past = pos >= ends[c]
        index = index + past.astype(jnp.int32)
        start = jnp.where(past, ends[c], start)
    return index, start


def ends_of(len_ref, clusters):
    ends, total = [], jnp.int32(0)
    for c in range(clusters - 1):
        total = total + len_ref[c]
        ends.append(total.astype(jnp.float32))
    return ends


def attend(
    rows, query, pos_b, start_b, feat, acc, top, keys, key_pos, ends, clusters, diagonal
):
    index, _ = cluster_parts(key_pos, ends, clusters)
    block = jnp.floor(key_pos * (1.0 / rows)).astype(jnp.int32)
    wanted = block * clusters + index
    size = key_pos.shape[1]
    onehot = (
        lax.broadcasted_iota(jnp.int32, (feat.shape[1], size), 0) == wanted
    ).astype(jnp.bfloat16)
    allowed = jnp.dot(feat, onehot, preferred_element_type=jnp.float32)
    scores = lax.dot_general(
        query, keys, (((1,), (1,)), ((), ())), preferred_element_type=jnp.float32
    )
    weights = []
    for at in range(0, size, LANES):
        part = scores[:, at : at + LANES]
        pos = key_pos[:, at : at + LANES]
        earlier = (pos < pos_b) & (pos >= start_b)
        top = jnp.maximum(top, jnp.where(earlier, part, -1.0))
        weight = jnp.exp2(part * (TEMP * math.log2(math.e)))
        masked = weight * allowed[:, at : at + LANES]
        if diagonal:
            masked = jnp.where(pos == pos_b, weight, masked)
        weights.append(masked.astype(jnp.bfloat16))
    acc = acc + jnp.dot(
        jnp.concatenate(weights, axis=1), keys, preferred_element_type=jnp.float32
    )
    return acc, top


def first_body(half, clusters, len_ref, mask_ref, a_ref, b_ref, sa_ref, sb_ref,
               acc_ref, top_ref, info_ref, feat_ref):
    ends = ends_of(len_ref, clusters)
    own = positions_of(a_ref, half)
    sib = positions_of(sa_ref, half)
    pos = jnp.concatenate([column(r) for r in own + sib], axis=0)
    index, start = cluster_parts(pos, ends, clusters)
    count = mask_ref.shape[0]
    block = jnp.floor(pos * (1.0 / (2 * half))).astype(jnp.int32)
    total = pos.shape[0]
    onehot = (block == lax.broadcasted_iota(jnp.int32, (total, count), 1)).astype(jnp.bfloat16)
    wide = count * clusters
    spread = (
        lax.broadcasted_iota(jnp.int32, (count, wide), 1) // clusters
        == lax.broadcasted_iota(jnp.int32, (count, wide), 0)
    ).astype(jnp.bfloat16)
    picked = jnp.dot(
        onehot, mask_ref[...].astype(jnp.bfloat16), preferred_element_type=jnp.float32
    ).astype(jnp.bfloat16)
    picked = jnp.dot(picked, spread, preferred_element_type=jnp.float32)
    lane_cluster = lax.broadcasted_iota(jnp.int32, (total, wide), 1) % clusters
    feat = jnp.where(lane_cluster == index, picked, 0.0).astype(jnp.bfloat16)
    feat_ref[...] = feat
    pos_b = jnp.broadcast_to(pos, (total, LANES))
    start_b = jnp.broadcast_to(start, (total, LANES))
    info_ref[0] = pos_b
    info_ref[1] = start_b
    query = jnp.concatenate([rows_of(r, half) for r in (a_ref, b_ref, sa_ref, sb_ref)], axis=0)
    acc, top = attend(
        2 * half, query, pos_b, start_b, feat,
        jnp.zeros((total, query.shape[1]), jnp.float32),
        jnp.full((total, LANES), -1.0, jnp.float32),
        query[: 2 * half], jnp.concatenate(own, axis=1), ends, clusters, True,
    )
    acc_ref[...] = acc
    top_ref[...] = top


def middle_body(half, clusters, groups, *refs):
    len_ref, info_ref, feat_ref, a_ref, b_ref, sa_ref, sb_ref, acc_in, top_in = refs[:9]
    key_refs = refs[9:-2]
    acc_ref, top_ref = refs[-2:]
    ends = ends_of(len_ref, clusters)
    query = jnp.concatenate([rows_of(r, half) for r in (a_ref, b_ref, sa_ref, sb_ref)], axis=0)
    acc, top = acc_in[...], top_in[...]
    for keys, pos in gather_keys(key_refs, groups, half):
        acc, top = attend(
            2 * half, query, info_ref[0], info_ref[1], feat_ref[...], acc, top, keys, pos,
            ends, clusters, False,
        )
    acc_ref[...] = acc
    top_ref[...] = top


def gather_keys(key_refs, groups, half):
    out = []
    for group in groups:
        keys = jnp.concatenate([rows_of(key_refs[r], half) for r, _, _ in group], axis=0)
        pos = jnp.concatenate(
            [positions_of(key_refs[p], half)[w] for _, p, w in group], axis=1
        )
        out.append((keys, pos))
    return out


def last_body(half, clusters, groups, *refs):
    len_ref, info_ref, feat_ref, a_ref, b_ref, acc_in, top_in, racc, rtop = refs[:9]
    key_refs = refs[9:-2]
    dir_ref, out_top = refs[-2:]
    ends = ends_of(len_ref, clusters)
    rows = 2 * half
    query = jnp.concatenate([rows_of(r, half) for r in (a_ref, b_ref)], axis=0)
    acc = acc_in[:rows] + racc[...]
    top = jnp.maximum(top_in[:rows], rtop[...])
    for keys, pos in gather_keys(key_refs, groups, half):
        acc, top = attend(
            2 * half, query, info_ref[0, :rows], info_ref[1, :rows], feat_ref[:rows], acc, top, keys, pos,
            ends, clusters, False,
        )
    width = acc.shape[1]
    scale = math.sqrt(width) * lax.rsqrt(jnp.sum(acc * acc, axis=1, keepdims=True) + EPS)
    dir_ref[...] = (acc * scale).astype(jnp.bfloat16)
    best = jnp.max(top, axis=1, keepdims=True)
    eye = lax.broadcasted_iota(jnp.int32, (half, half), 0) == lax.broadcasted_iota(
        jnp.int32, (half, half), 1
    )
    lines = [
        jnp.max(jnp.where(eye, best[at : at + half], -1.0), axis=0, keepdims=True)
        for at in (0, half)
    ]
    out_top[...] = jnp.concatenate(lines, axis=0)


def per_device(embeddings, dest_pos, cluster_lengths, block_mask):
    rows, width = embeddings.shape
    half = rows // 2
    count = lax.axis_size("blk")
    clusters = cluster_lengths.shape[0]
    chips = count // 2
    ahead, back = ring_perm(count, 1), ring_perm(count, -1)
    sibling = [(i, i ^ 1) for i in range(count)]

    def move(x, perm):
        return lax.ppermute(x, "blk", perm)

    def bf(n):
        return jax.ShapeDtypeStruct((n, width), jnp.bfloat16)

    def f32(*s):
        return jax.ShapeDtypeStruct(s, jnp.float32)

    full = half + TAIL
    a, b, ah, bh = call(
        prep_body, [bf(full), bf(full), bf(half), bf(half)], [VM, VM], rows * width * 4,
        rows * width * 8,
    )(embeddings, dest_pos.reshape(2, half))

    lead_f, lead_b, follow_f, follow_b = a, b, bh, ah
    rounds = []
    for step in range(chips // 2):
        lead_f, lead_b = move(lead_f, ahead), move(lead_b, back)
        if step < chips // 2 - 1:
            follow_f, follow_b = move(follow_f, ahead), move(follow_b, back)
            rounds.append((lead_f, lead_b, follow_f, follow_b))
        else:
            rounds.append((lead_f, lead_b))

    sa, sb = move(a, sibling), move(b, sibling)
    total = 2 * rows
    wide = count * clusters

    acc, top, info, feat = call(
        functools.partial(first_body, half, clusters),
        [f32(total, width), f32(total, LANES), f32(2, total, LANES),
         jax.ShapeDtypeStruct((total, wide), jnp.bfloat16)],
        [SM] + [VM] * 5, 4 * total * rows * width, 4 * 2**20,
    )(cluster_lengths, block_mask, a, b, sa, sb)

    pair = ((0, 0, 0), (1, 1, 1))

    def middle(acc, top, keys, groups):
        n = sum(len(g) for g in groups)
        return call(
            functools.partial(middle_body, half, clusters, groups),
            [f32(total, width), f32(total, LANES)],
            [SM] + [VM] * (8 + len(keys)), 4 * total * half * n * width, 5 * 2**20,
        )(cluster_lengths, info, feat, a, b, sa, sb, acc, top, *keys)

    for step in range(chips // 2 - 1):
        lf, lb = rounds[step][:2]
        if step == 0:
            acc, top = middle(acc, top, (lf, lb), (((0, 0, 0), (1, 1, 1)),))
        else:
            plf, plb, pff, pfb = rounds[step - 1]
            acc, top = middle(
                acc, top, (lf, lb, pff, pfb, plf, plb),
                (((0, 0, 0), (1, 1, 1)), ((2, 4, 1), (3, 5, 0))),
            )
    racc, rtop = move(acc[rows:], sibling), move(top[rows:], sibling)
    plf, plb, pff, pfb = rounds[-2]
    lf, lb = rounds[-1]
    late = [lf, lb, pff, pfb]
    others = [move(x, sibling) for x in late]
    splf, splb = move(plf, sibling), move(plb, sibling)
    keys = late + [plf, plb] + others + [splf, splb]
    groups = (
        ((2, 4, 1), (3, 5, 0)),
        ((8, 10, 1), (9, 11, 0)),
        ((0, 0, 0), (1, 1, 1)),
        ((6, 6, 0), (7, 7, 1)),
    )
    out_dir, out_top = call(
        functools.partial(last_body, half, clusters, groups),
        [jax.ShapeDtypeStruct((rows, width), jnp.bfloat16), f32(2, half)],
        [SM] + [VM] * (8 + len(keys)), 4 * rows * 8 * half * width, 5 * 2**20,
    )(cluster_lengths, info, feat, a, b, acc, top, racc, rtop, *keys)
    return out_top.reshape(rows), out_dir


def solution(mesh):
    placed = (P(("groups", "blk"), None), P(("groups", "blk")), P("groups"), P("groups", None))
    return jax.shard_map(
        per_device,
        mesh=mesh,
        in_specs=placed,
        out_specs=(P(("groups", "blk")), P(("groups", "blk"), None)),
        check_vma=False,
    )
```

time: 173 us -> 60.1 us (0.35)
  waiting for transfers between devices: 101 us -> 21.1 us
  matrix products: 14.2 us -> 0 us
  Pallas kernels: 0 us -> 13.8 us
  between operations: 14.2 us -> 0.76 us
  local copies, waits for them, and re-layouts: 17.5 us -> 5.55 us
  other arithmetic: 7.17 us -> 0 us
    all_gather x1 -> x0, waiting for transfers between devices: 62.1 us -> none  [per_device(): piece = lax.all_gather(block, 'blk', axis=0, tiled=True)]
    all_to_all x4 -> x0, waiting for transfers between devices: 38.7 us -> none  [the longest x1 17.4 us: per_device(): lax.all_to_all(send_rows.reshape(count, cap, width), 'blk', split_axis=0,...]
    ppermute x0 -> x24, waiting for transfers between devices: none -> 21.1 us  [move(): return lax.ppermute(x, 'blk', perm)]
    all_to_all x4 -> x0, starting transfers between devices: 18.7 us -> none  [the longest x1 7.39 us: per_device(): lax.all_to_all(send_pos.reshape(count, cap), 'blk', split_axis=0, concat_...]
    ppermute x0 -> x24, starting transfers between devices: none -> 18.6 us  [move(): return lax.ppermute(x, 'blk', perm)]
    dot_general x3 -> x0, matrix products: 14.2 us -> none  [the longest x1 7.08 us: fold_pair(): lax.dot_general(queries, piece, (((1,), (1,)), ((), ())), preferred_eleme...]
    pallas_call x0 -> x6, Pallas kernels: none -> 13.8 us  [the longest x3 7.73 us: middle(): call(functools.partial(middle_body, half, clusters, groups), [f32(total,...]
    gather x4 -> x0, local copies, waits for them, and re-layouts: 10.5 us -> none  [the longest x1 3.36 us: per_device(): back_top = top[fetch].reshape(count, cap)]
  transfers between devices with their start and end apart: 5 -> 24, of which waited for: 5 -> 12; matrix products, arithmetic and copies ran while one was open for 7% -> 0% of each run, Pallas kernels for 0% -> 11%
where the time goes in v1:
time: 60.1 us; the launch traced here: 59.8 us
  waiting for transfers between devices  21.1 us (35%)
  starting transfers between devices  18.6 us (31%)
  Pallas kernels  13.8 us (23%)
  local copies, waits for them, and re-layouts  5.55 us (9%)
  between operations  0.76 us (1%)
    ppermute x24, waiting for transfers between devices, move(): return lax.ppermute(x, 'blk', perm)  21.1 us
    ppermute x24, starting transfers between devices, move(): return lax.ppermute(x, 'blk', perm)  18.6 us
    pallas_call x3, Pallas kernels, middle(): call(functools.partial(middle_body, half, clusters, groups), [f32(total,...  7.73 us
    unnamed x14, local copies, waits for them, and re-layouts  5.49 us
    pallas_call x1, Pallas kernels, per_device(): call(functools.partial(last_body, half, clusters, groups), [jax.ShapeDtyp...  3.84 us
    pallas_call x1, Pallas kernels, per_device(): call(functools.partial(first_body, half, clusters), [f32(total, width), f...  2.07 us
  transfers between devices with their start and end apart: 24, of which 12 were waited for; matrix products, arithmetic and copies ran while one was open for 0% of the time, Pallas kernels for 11%

profile of v1, /device:TPU:0, one launch (start us, length us, event | category | flops | bytes accessed | tf_op | source)
XLA Modules:
  0.0 59.8 jit_solution(11134738610305704931)
XLA Ops:
  0.6 1.1 %copy-done.3 = f32[256,768]{1,0:T(8,128)S(1)} copy-done((f32[256,768]{1,0:T(8,128)S(1)}, f32[256,768]{1,0:T(8,128)}, u32[]{:S(2)}) %copy-start.3) | copy-done | bytes 786456
  1.8 0.7 %copy-done.5 = s32[256]{0:T(256)S(1)} copy-done((s32[256]{0:T(256)S(1)}, s32[256]{0:T(256)}, u32[]{:S(2)}) %copy-start.5) | copy-done | bytes 1048
  2.6 3.1 %collective-permute-start.2 = (bf16[136,768]{1,0:T(8,128)(2,1)S(1)}, bf16[136,768]{1,0:T(8,128)(2,1)S(1)}, u32[]{:S(2)}, u32[]{:S(2)}) collective-permute-start(bf16[136,768]{1,0:T(8,128)(2,1)S(1)} %get-tuple-element.18.a_ref.refs_3_), channel_id=1, source_target_pairs={{0,4},{1,5},{4,8},{5,9},{8,12},{9,13},{12,14},{13,15},{14,10},{15,... | collective-permute-start | bytes 626696 | tf_op jit(solution)/shard_map/ppermute | solution.py:243
  5.7 2.0 %collective-permute-start.6 = (bf16[128,768]{1,0:T(8,128)(2,1)S(1)}, bf16[128,768]{1,0:T(8,128)(2,1)S(1)}, u32[]{:S(2)}, u32[]{:S(2)}) collective-permute-start(bf16[128,768]{1,0:T(8,128)(2,1)S(1)} %get-tuple-element.26), channel_id=1, source_target_pairs={{0,4},{1,5},{4,8},{5,9},{8,12},{9,13},{12,14},{13,15},{14,10},{15,... | collective-permute-start | bytes 589832 | tf_op jit(solution)/shard_map/ppermute | solution.py:243
  7.7 3.9 %collective-permute-done.2.refs_9_.refs_13_ = bf16[136,768]{1,0:T(8,128)(2,1)S(1)} collective-permute-done((bf16[136,768]{1,0:T(8,128)(2,1)S(1)}, bf16[136,768]{1,0:T(8,128)(2,1)S(1)}, u32[]{:S(2)}, u32[]{:S(2)}) %collective-permute-start.2) | collective-permute-done | bytes 208928 | tf_op jit(solution)/shard_map/ppermute | solution.py:243
  11.6 2.1 %collective-permute-start.4 = (bf16[136,768]{1,0:T(8,128)(2,1)S(1)}, bf16[136,768]{1,0:T(8,128)(2,1)S(1)}, u32[]{:S(2)}, u32[]{:S(2)}) collective-permute-start(bf16[136,768]{1,0:T(8,128)(2,1)S(1)} %collective-permute-done.2.refs_9_.refs_13_), channel_id=1, source_target_pairs={{0,4},{1,5},{4,8},{5,9},{8,12},{9,13},{12,14},{13,15},{14,10},{15,... | collective-permute-start | bytes 626696 | tf_op jit(solution)/shard_map/ppermute | solution.py:243
  13.7 2.0 %collective-permute-start.7 = (bf16[128,768]{1,0:T(8,128)(2,1)S(1)}, bf16[128,768]{1,0:T(8,128)(2,1)S(1)}, u32[]{:S(2)}, u32[]{:S(2)}) collective-permute-start(bf16[128,768]{1,0:T(8,128)(2,1)S(1)} %get-tuple-element.27), channel_id=1, source_target_pairs={{0,2},{1,3},{4,0},{5,1},{8,4},{9,5},{12,8},{13,9},{14,12},{15,13},... | collective-permute-start | bytes 589832 | tf_op jit(solution)/shard_map/ppermute | solution.py:243
  15.9 3.5 %collective-permute-done.4.refs_9_.refs_13_ = bf16[136,768]{1,0:T(8,128)(2,1)S(1)} collective-permute-done((bf16[136,768]{1,0:T(8,128)(2,1)S(1)}, bf16[136,768]{1,0:T(8,128)(2,1)S(1)}, u32[]{:S(2)}, u32[]{:S(2)}) %collective-permute-start.4) | collective-permute-done | bytes 208928 | tf_op jit(solution)/shard_map/ppermute | solution.py:243
  19.5 1.8 %collective-permute-start.8 = (bf16[136,768]{1,0:T(8,128)(2,1)S(1)}, bf16[136,768]{1,0:T(8,128)(2,1)S(1)}, u32[]{:S(2)}, u32[]{:S(2)}) collective-permute-start(bf16[136,768]{1,0:T(8,128)(2,1)S(1)} %collective-permute-done.4.refs_9_.refs_13_), channel_id=1, source_target_pairs={{0,4},{1,5},{4,8},{5,9},{8,12},{9,13},{12,14},{13,15},{14,10},{15,... | collective-permute-start | bytes 626696 | tf_op jit(solution)/shard_map/ppermute | solution.py:243
  21.3 0.2 collective-permute-done.5.refs_10_.refs_14_
  21.5 3.0 %collective-permute-done.7.refs_12_ = bf16[128,768]{1,0:T(8,128)(2,1)S(1)} collective-permute-done((bf16[128,768]{1,0:T(8,128)(2,1)S(1)}, bf16[128,768]{1,0:T(8,128)(2,1)S(1)}, u32[]{:S(2)}, u32[]{:S(2)}) %collective-permute-start.7) | collective-permute-done | bytes 196640 | tf_op jit(solution)/shard_map/ppermute | solution.py:243
  24.5 1.9 %collective-permute-start.10 = (bf16[128,768]{1,0:T(8,128)(2,1)S(1)}, bf16[128,768]{1,0:T(8,128)(2,1)S(1)}, u32[]{:S(2)}, u32[]{:S(2)}) collective-permute-start(bf16[128,768]{1,0:T(8,128)(2,1)S(1)} %collective-permute-done.6.refs_11_), channel_id=1, source_target_pairs={{0,4},{1,5},{4,8},{5,9},{8,12},{9,13},{12,14},{13,15},{14,10},{15,... | collective-permute-start | bytes 589832 | tf_op jit(solution)/shard_map/ppermute | solution.py:243
  26.5 0.7 %copy-done.4 = s32[4]{0:T(128)S(1)} copy-done((s32[4]{0:T(128)S(1)}, s32[4]{0:T(128)}, u32[]{:S(2)}) %copy-start.4) | copy-done | bytes 40
  27.2 0.7 %copy-done.6 = s32[16,16]{1,0:T(8,128)S(1)} copy-done((s32[16,16]{1,0:T(8,128)S(1)}, s32[16,16]{1,0:T(8,128)}, u32[]{:S(2)}) %copy-start.6) | copy-done | bytes 1048
  27.9 2.1 %shard_map.60 = (f32[512,768]{1,0:T(8,128)S(1)}, f32[512,128]{1,0:T(8,128)S(1)}, f32[2,512,128]{2,1,0:T(8,128)S(1)}, bf16[512,64]{1,0:T(8,128)(2,1)S(1)}) custom-call(s32[4]{0:T(128)S(1)} %copy-done.4, s32[16,16]{1,0:T(8,128)S(1)} %copy-done.6, bf16[136,768]{1,0:T(8,128)(2,1)S(1)} %get-tuple-element.18.a_ref.refs_3_, ...), custom_call_target="tpu_custom_call" | custom-call | flops 402653184 | bytes 4194304 | tf_op jit(solution)/shard_map/pallas_call | solution.py:271
  30.0 1.6 %shard_map.61 = (f32[512,768]{1,0:T(8,128)S(1)}, f32[512,128]{1,0:T(8,128)S(1)}) custom-call(s32[4]{0:T(128)S(1)} %copy-done.4, f32[2,512,128]{2,1,0:T(8,128)S(1)} %get-tuple-element.20.refs_1_, bf16[512,64]{1,0:T(8,128)(2,1)S(1)} %get-tuple-element.21.refs_2_, bf16[136,768]{1,0:T(8,128)(2,1)S(1)} %get-tuple-element.18.a_ref.refs_3_, ...), custom_call_target="tpu_custom_call" | custom-call | flops 402653184 | bytes 5242880 | tf_op jit(solution)/shard_map/pallas_call | solution.py:282
  31.6 1.2 %copy-done.2 = f32[512,768]{1,0:T(8,128)} copy-done((f32[512,768]{1,0:T(8,128)}, f32[512,768]{1,0:T(8,128)S(1)}, u32[]{:S(2)}) %copy-start.2) | copy-done | bytes 1572888
  32.7 3.1 %shard_map.62 = (f32[512,768]{1,0:T(8,128)S(1)}, f32[512,128]{1,0:T(8,128)S(1)}) custom-call(s32[4]{0:T(128)S(1)} %copy-done.4, f32[2,512,128]{2,1,0:T(8,128)S(1)} %get-tuple-element.20.refs_1_, bf16[512,64]{1,0:T(8,128)(2,1)S(1)} %get-tuple-element.21.refs_2_, bf16[136,768]{1,0:T(8,128)(2,1)S(1)} %get-tuple-element.18.a_ref.refs_3_, ...), custom_call_target="tpu_custom_call" | custom-call | flops 805306368 | bytes 5242880 | tf_op jit(solution)/shard_map/pallas_call | solution.py:282
  35.8 1.2 %copy-done.1 = f32[512,768]{1,0:T(8,128)} copy-done((f32[512,768]{1,0:T(8,128)}, f32[512,768]{1,0:T(8,128)S(1)}, u32[]{:S(2)}) %copy-start.1) | copy-done | bytes 1572888
  37.0 3.1 %shard_map.63 = (f32[512,768]{1,0:T(8,128)S(1)}, f32[512,128]{1,0:T(8,128)S(1)}) custom-call(s32[4]{0:T(128)S(1)} %copy-done.4, f32[2,512,128]{2,1,0:T(8,128)S(1)} %get-tuple-element.20.refs_1_, bf16[512,64]{1,0:T(8,128)(2,1)S(1)} %get-tuple-element.21.refs_2_, bf16[136,768]{1,0:T(8,128)(2,1)S(1)} %get-tuple-element.18.a_ref.refs_3_, ...), custom_call_target="tpu_custom_call" | custom-call | flops 805306368 | bytes 5242880 | tf_op jit(solution)/shard_map/pallas_call | solution.py:282
  40.2 2.0 %collective-permute-start.16 = (bf16[128,768]{1,0:T(8,128)(2,1)S(1)}, bf16[128,768]{1,0:T(8,128)(2,1)S(1)}, u32[]{:S(2)}, u32[]{:S(2)}) collective-permute-start(bf16[128,768]{1,0:T(8,128)(2,1)S(1)} %collective-permute-done.10.refs_11_), channel_id=1, source_target_pairs={{0,4},{1,5},{4,8},{5,9},{8,12},{9,13},{12,14},{13,15},{14,10},{15,... | collective-permute-start | bytes 589832 | tf_op jit(solution)/shard_map/ppermute | solution.py:243
  42.5 1.9 %collective-permute-start.14 = (bf16[136,768]{1,0:T(8,128)(2,1)S(1)}, bf16[136,768]{1,0:T(8,128)(2,1)S(1)}, u32[]{:S(2)}, u32[]{:S(2)}) collective-permute-start(bf16[136,768]{1,0:T(8,128)(2,1)S(1)} %collective-permute-done.8.refs_9_.refs_13_), channel_id=1, source_target_pairs={{0,4},{1,5},{4,8},{5,9},{8,12},{9,13},{12,14},{13,15},{14,10},{15,... | collective-permute-start | bytes 626696 | tf_op jit(solution)/shard_map/ppermute | solution.py:243
  44.4 3.6 %collective-permute-done.16.refs_11_ = bf16[128,768]{1,0:T(8,128)(2,1)S(1)} collective-permute-done((bf16[128,768]{1,0:T(8,128)(2,1)S(1)}, bf16[128,768]{1,0:T(8,128)(2,1)S(1)}, u32[]{:S(2)}, u32[]{:S(2)}) %collective-permute-start.16) | collective-permute-done | bytes 196640 | tf_op jit(solution)/shard_map/ppermute | solution.py:243
  48.0 0.4 collective-permute-start.15
  48.3 0.8 %collective-permute-done.17.refs_12_ = bf16[128,768]{1,0:T(8,128)(2,1)S(1)} collective-permute-done((bf16[128,768]{1,0:T(8,128)(2,1)S(1)}, bf16[128,768]{1,0:T(8,128)(2,1)S(1)}, u32[]{:S(2)}, u32[]{:S(2)}) %collective-permute-start.17) | collective-permute-done | bytes 196640 | tf_op jit(solution)/shard_map/ppermute | solution.py:243
  49.2 0.5 collective-permute-start.21
  49.7 0.9 %collective-permute-done.20.refs_17_ = bf16[128,768]{1,0:T(8,128)(2,1)S(1)} collective-permute-done((bf16[128,768]{1,0:T(8,128)(2,1)S(1)}, bf16[128,768]{1,0:T(8,128)(2,1)S(1)}, u32[]{:S(2)}, u32[]{:S(2)}) %collective-permute-start.20) | collective-permute-done | bytes 196640 | tf_op jit(solution)/shard_map/ppermute | solution.py:243
  50.9 0.2 collective-permute-start.23
  51.1 0.9 %collective-permute-done.14.refs_9_ = bf16[136,768]{1,0:T(8,128)(2,1)S(1)} collective-permute-done((bf16[136,768]{1,0:T(8,128)(2,1)S(1)}, bf16[136,768]{1,0:T(8,128)(2,1)S(1)}, u32[]{:S(2)}, u32[]{:S(2)}) %collective-permute-start.14) | collective-permute-done | bytes 208928 | tf_op jit(solution)/shard_map/ppermute | solution.py:243
  52.0 2.4 %collective-permute-done.15.refs_10_ = bf16[136,768]{1,0:T(8,128)(2,1)S(1)} collective-permute-done((bf16[136,768]{1,0:T(8,128)(2,1)S(1)}, bf16[136,768]{1,0:T(8,128)(2,1)S(1)}, u32[]{:S(2)}, u32[]{:S(2)}) %collective-permute-start.15) | collective-permute-done | bytes 208928 | tf_op jit(solution)/shard_map/ppermute | solution.py:243
  54.5 1.4 %collective-permute-done.19.refs_16_ = bf16[136,768]{1,0:T(8,128)(2,1)S(1)} collective-permute-done((bf16[136,768]{1,0:T(8,128)(2,1)S(1)}, bf16[136,768]{1,0:T(8,128)(2,1)S(1)}, u32[]{:S(2)}, u32[]{:S(2)}) %collective-permute-start.19) | collective-permute-done | bytes 208928 | tf_op jit(solution)/shard_map/ppermute | solution.py:243
  55.9 3.8 %shard_map.64 = (bf16[256,768]{1,0:T(8,128)(2,1)}, f32[2,128]{1,0:T(2,128)}) custom-call(s32[4]{0:T(128)S(1)} %copy-done.4, f32[2,512,128]{2,1,0:T(8,128)S(1)} %get-tuple-element.20.refs_1_, bf16[512,64]{1,0:T(8,128)(2,1)S(1)} %get-tuple-element.21.refs_2_, bf16[136,768]{1,0:T(8,128)(2,1)S(1)} %get-tuple-element.18.a_ref.refs_3_, ...), custom_call_target="tpu_custom_call" | custom-call | flops 805306368 | bytes 5242880 | tf_op jit(solution)/shard_map/pallas_call | solution.py:311
  (38 shorter events, 1.2 us)
Async XLA Ops:
  0.6 1.1 %copy-start.3 = (f32[256,768]{1,0:T(8,128)S(1)}, f32[256,768]{1,0:T(8,128)}, u32[]{:S(2)}) copy-start(f32[256,768]{1,0:T(8,128)} %emb_ref.1) | copy-start | bytes 2359300
  1.8 0.7 %copy-start.5 = (s32[256]{0:T(256)S(1)}, s32[256]{0:T(256)}, u32[]{:S(2)}) copy-start(s32[256]{0:T(256)} %param.5) | copy-start | bytes 3076
  2.6 9.0 %collective-permute-start.2 = (bf16[136,768]{1,0:T(8,128)(2,1)S(1)}, bf16[136,768]{1,0:T(8,128)(2,1)S(1)}, u32[]{:S(2)}, u32[]{:S(2)}) collective-permute-start(bf16[136,768]{1,0:T(8,128)(2,1)S(1)} %get-tuple-element.18.a_ref.refs_3_), channel_id=1, source_target_pairs={{0,4},{1,5},{4,8},{5,9},{8,12},{9,13},{12,14},{13,15},{14,10},{15,... | collective-permute-start | bytes 626696 | tf_op jit(solution)/shard_map/ppermute | solution.py:243
  5.7 8.1 %collective-permute-start.3 = (bf16[136,768]{1,0:T(8,128)(2,1)S(1)}, bf16[136,768]{1,0:T(8,128)(2,1)S(1)}, u32[]{:S(2)}, u32[]{:S(2)}) collective-permute-start(bf16[136,768]{1,0:T(8,128)(2,1)S(1)} %get-tuple-element.19.b_ref.refs_4_), channel_id=1, source_target_pairs={{0,2},{1,3},{4,0},{5,1},{8,4},{9,5},{12,8},{13,9},{14,12},{15,13},... | collective-permute-start | bytes 626696 | tf_op jit(solution)/shard_map/ppermute | solution.py:243
  5.7 10.1 %collective-permute-start.6 = (bf16[128,768]{1,0:T(8,128)(2,1)S(1)}, bf16[128,768]{1,0:T(8,128)(2,1)S(1)}, u32[]{:S(2)}, u32[]{:S(2)}) collective-permute-start(bf16[128,768]{1,0:T(8,128)(2,1)S(1)} %get-tuple-element.26), channel_id=1, source_target_pairs={{0,4},{1,5},{4,8},{5,9},{8,12},{9,13},{12,14},{13,15},{14,10},{15,... | collective-permute-start | bytes 589832 | tf_op jit(solution)/shard_map/ppermute | solution.py:243
  11.6 7.9 %collective-permute-start.4 = (bf16[136,768]{1,0:T(8,128)(2,1)S(1)}, bf16[136,768]{1,0:T(8,128)(2,1)S(1)}, u32[]{:S(2)}, u32[]{:S(2)}) collective-permute-start(bf16[136,768]{1,0:T(8,128)(2,1)S(1)} %collective-permute-done.2.refs_9_.refs_13_), channel_id=1, source_target_pairs={{0,4},{1,5},{4,8},{5,9},{8,12},{9,13},{12,14},{13,15},{14,10},{15,... | collective-permute-start | bytes 626696 | tf_op jit(solution)/shard_map/ppermute | solution.py:243
  13.7 7.7 %collective-permute-start.5 = (bf16[136,768]{1,0:T(8,128)(2,1)S(1)}, bf16[136,768]{1,0:T(8,128)(2,1)S(1)}, u32[]{:S(2)}, u32[]{:S(2)}) collective-permute-start(bf16[136,768]{1,0:T(8,128)(2,1)S(1)} %collective-permute-done.3.refs_10_.refs_14_), channel_id=1, source_target_pairs={{0,2},{1,3},{4,0},{5,1},{8,4},{9,5},{12,8},{13,9},{14,12},{15,13},... | collective-permute-start | bytes 626696 | tf_op jit(solution)/shard_map/ppermute | solution.py:243
  13.7 12.7 %collective-permute-start = (bf16[136,768]{1,0:T(8,128)(2,1)S(1)}, bf16[136,768]{1,0:T(8,128)(2,1)S(1)}, u32[]{:S(2)}, u32[]{:S(2)}) collective-permute-start(bf16[136,768]{1,0:T(8,128)(2,1)S(1)} %get-tuple-element.18.a_ref.refs_3_), channel_id=1, source_target_pairs={{0,1},{1,0},{2,3},{3,2},{4,5},{5,4},{6,7},{7,6},{8,9},{9,8},{10,11... | collective-permute-start | bytes 626696 | tf_op jit(solution)/shard_map/ppermute | solution.py:243
  13.7 10.8 %collective-permute-start.7 = (bf16[128,768]{1,0:T(8,128)(2,1)S(1)}, bf16[128,768]{1,0:T(8,128)(2,1)S(1)}, u32[]{:S(2)}, u32[]{:S(2)}) collective-permute-start(bf16[128,768]{1,0:T(8,128)(2,1)S(1)} %get-tuple-element.27), channel_id=1, source_target_pairs={{0,2},{1,3},{4,0},{5,1},{8,4},{9,5},{12,8},{13,9},{14,12},{15,13},... | collective-permute-start | bytes 589832 | tf_op jit(solution)/shard_map/ppermute | solution.py:243
  15.8 10.7 %collective-permute-start.1 = (bf16[136,768]{1,0:T(8,128)(2,1)S(1)}, bf16[136,768]{1,0:T(8,128)(2,1)S(1)}, u32[]{:S(2)}, u32[]{:S(2)}) collective-permute-start(bf16[136,768]{1,0:T(8,128)(2,1)S(1)} %get-tuple-element.19.b_ref.refs_4_), channel_id=1, source_target_pairs={{0,1},{1,0},{2,3},{3,2},{4,5},{5,4},{6,7},{7,6},{8,9},{9,8},{10,11... | collective-permute-start | bytes 626696 | tf_op jit(solution)/shard_map/ppermute | solution.py:243
  19.5 17.5 %collective-permute-start.8 = (bf16[136,768]{1,0:T(8,128)(2,1)S(1)}, bf16[136,768]{1,0:T(8,128)(2,1)S(1)}, u32[]{:S(2)}, u32[]{:S(2)}) collective-permute-start(bf16[136,768]{1,0:T(8,128)(2,1)S(1)} %collective-permute-done.4.refs_9_.refs_13_), channel_id=1, source_target_pairs={{0,4},{1,5},{4,8},{5,9},{8,12},{9,13},{12,14},{13,15},{14,10},{15,... | collective-permute-start | bytes 626696 | tf_op jit(solution)/shard_map/ppermute | solution.py:243
  21.5 15.6 %collective-permute-start.9 = (bf16[136,768]{1,0:T(8,128)(2,1)S(1)}, bf16[136,768]{1,0:T(8,128)(2,1)S(1)}, u32[]{:S(2)}, u32[]{:S(2)}) collective-permute-start(bf16[136,768]{1,0:T(8,128)(2,1)S(1)} %collective-permute-done.5.refs_10_.refs_14_), channel_id=1, source_target_pairs={{0,2},{1,3},{4,0},{5,1},{8,4},{9,5},{12,8},{13,9},{14,12},{15,13},... | collective-permute-start | bytes 626696 | tf_op jit(solution)/shard_map/ppermute | solution.py:243
  24.5 12.5 %collective-permute-start.10 = (bf16[128,768]{1,0:T(8,128)(2,1)S(1)}, bf16[128,768]{1,0:T(8,128)(2,1)S(1)}, u32[]{:S(2)}, u32[]{:S(2)}) collective-permute-start(bf16[128,768]{1,0:T(8,128)(2,1)S(1)} %collective-permute-done.6.refs_11_), channel_id=1, source_target_pairs={{0,4},{1,5},{4,8},{5,9},{8,12},{9,13},{12,14},{13,15},{14,10},{15,... | collective-permute-start | bytes 589832 | tf_op jit(solution)/shard_map/ppermute | solution.py:243
  26.4 10.6 %collective-permute-start.11 = (bf16[128,768]{1,0:T(8,128)(2,1)S(1)}, bf16[128,768]{1,0:T(8,128)(2,1)S(1)}, u32[]{:S(2)}, u32[]{:S(2)}) collective-permute-start(bf16[128,768]{1,0:T(8,128)(2,1)S(1)} %collective-permute-done.7.refs_12_), channel_id=1, source_target_pairs={{0,2},{1,3},{4,0},{5,1},{8,4},{9,5},{12,8},{13,9},{14,12},{15,13},... | collective-permute-start | bytes 589832 | tf_op jit(solution)/shard_map/ppermute | solution.py:243
  26.5 0.7 %copy-start.4 = (s32[4]{0:T(128)S(1)}, s32[4]{0:T(128)}, u32[]{:S(2)}) copy-start(s32[4]{0:T(128)} %refs_0_.7) | copy-start | bytes 52
  27.2 0.7 %copy-start.6 = (s32[16,16]{1,0:T(8,128)S(1)}, s32[16,16]{1,0:T(8,128)}, u32[]{:S(2)}) copy-start(s32[16,16]{1,0:T(8,128)} %mask_ref.1) | copy-start | bytes 3076
  31.6 1.2 %copy-start.2 = (f32[512,768]{1,0:T(8,128)}, f32[512,768]{1,0:T(8,128)S(1)}, u32[]{:S(2)}) copy-start(f32[512,768]{1,0:T(8,128)S(1)} %get-tuple-element.24.refs_7_) | copy-start | bytes 4718596
  35.8 1.2 %copy-start.1 = (f32[512,768]{1,0:T(8,128)}, f32[512,768]{1,0:T(8,128)S(1)}, u32[]{:S(2)}) copy-start(f32[512,768]{1,0:T(8,128)S(1)} %get-tuple-element.28.refs_7_) | copy-start | bytes 4718596
  40.1 15.8 %copy-start = (f32[512,768]{1,0:T(8,128)}, f32[512,768]{1,0:T(8,128)S(1)}, u32[]{:S(2)}) copy-start(f32[512,768]{1,0:T(8,128)S(1)} %get-tuple-element.30.refs_5_) | copy-start | bytes 4718596
  40.2 15.7 %collective-permute-start.12 = (f32[256,768]{1,0:T(8,128)S(1)}, f32[256,768]{1,0:T(8,128)S(1)}, u32[]{:S(2)}, u32[]{:S(2)}) collective-permute-start(f32[256,768]{1,0:T(8,128)S(1)} %slice.6), channel_id=1, source_target_pairs={{0,1},{1,0},{2,3},{3,2},{4,5},{5,4},{6,7},{7,6},{8,9},{9,8},{10,11... | collective-permute-start | bytes 2359304 | tf_op jit(solution)/shard_map/ppermute | solution.py:243
  40.2 7.8 %collective-permute-start.16 = (bf16[128,768]{1,0:T(8,128)(2,1)S(1)}, bf16[128,768]{1,0:T(8,128)(2,1)S(1)}, u32[]{:S(2)}, u32[]{:S(2)}) collective-permute-start(bf16[128,768]{1,0:T(8,128)(2,1)S(1)} %collective-permute-done.10.refs_11_), channel_id=1, source_target_pairs={{0,4},{1,5},{4,8},{5,9},{8,12},{9,13},{12,14},{13,15},{14,10},{15,... | collective-permute-start | bytes 589832 | tf_op jit(solution)/shard_map/ppermute | solution.py:243
  42.2 7.0 %collective-permute-start.17 = (bf16[128,768]{1,0:T(8,128)(2,1)S(1)}, bf16[128,768]{1,0:T(8,128)(2,1)S(1)}, u32[]{:S(2)}, u32[]{:S(2)}) collective-permute-start(bf16[128,768]{1,0:T(8,128)(2,1)S(1)} %collective-permute-done.11.refs_12_), channel_id=1, source_target_pairs={{0,2},{1,3},{4,0},{5,1},{8,4},{9,5},{12,8},{13,9},{14,12},{15,13},... | collective-permute-start | bytes 589832 | tf_op jit(solution)/shard_map/ppermute | solution.py:243
  42.3 6.9 %collective-permute-start.13 = (f32[256,128]{1,0:T(8,128)S(1)}, f32[256,128]{1,0:T(8,128)S(1)}, u32[]{:S(2)}, u32[]{:S(2)}) collective-permute-start(f32[256,128]{1,0:T(8,128)S(1)} %slice.7), channel_id=1, source_target_pairs={{0,1},{1,0},{2,3},{3,2},{4,5},{5,4},{6,7},{7,6},{8,9},{9,8},{10,11... | collective-permute-start | bytes 393224 | tf_op jit(solution)/shard_map/ppermute | solution.py:243
  42.5 9.6 %collective-permute-start.14 = (bf16[136,768]{1,0:T(8,128)(2,1)S(1)}, bf16[136,768]{1,0:T(8,128)(2,1)S(1)}, u32[]{:S(2)}, u32[]{:S(2)}) collective-permute-start(bf16[136,768]{1,0:T(8,128)(2,1)S(1)} %collective-permute-done.8.refs_9_.refs_13_), channel_id=1, source_target_pairs={{0,4},{1,5},{4,8},{5,9},{8,12},{9,13},{12,14},{13,15},{14,10},{15,... | collective-permute-start | bytes 626696 | tf_op jit(solution)/shard_map/ppermute | solution.py:243
  48.0 6.5 %collective-permute-start.15 = (bf16[136,768]{1,0:T(8,128)(2,1)S(1)}, bf16[136,768]{1,0:T(8,128)(2,1)S(1)}, u32[]{:S(2)}, u32[]{:S(2)}) collective-permute-start(bf16[136,768]{1,0:T(8,128)(2,1)S(1)} %collective-permute-done.9.refs_10_.refs_14_), channel_id=1, source_target_pairs={{0,2},{1,3},{4,0},{5,1},{8,4},{9,5},{12,8},{13,9},{14,12},{15,13},... | collective-permute-start | bytes 626696 | tf_op jit(solution)/shard_map/ppermute | solution.py:243
  49.2 1.4 %collective-permute-start.20 = (bf16[128,768]{1,0:T(8,128)(2,1)S(1)}, bf16[128,768]{1,0:T(8,128)(2,1)S(1)}, u32[]{:S(2)}, u32[]{:S(2)}) collective-permute-start(bf16[128,768]{1,0:T(8,128)(2,1)S(1)} %collective-permute-done.16.refs_11_), channel_id=1, source_target_pairs={{0,1},{1,0},{2,3},{3,2},{4,5},{5,4},{6,7},{7,6},{8,9},{9,8},{10,11... | collective-permute-start | bytes 589832 | tf_op jit(solution)/shard_map/ppermute | solution.py:243
  49.2 1.7 %collective-permute-start.21 = (bf16[128,768]{1,0:T(8,128)(2,1)S(1)}, bf16[128,768]{1,0:T(8,128)(2,1)S(1)}, u32[]{:S(2)}, u32[]{:S(2)}) collective-permute-start(bf16[128,768]{1,0:T(8,128)(2,1)S(1)} %collective-permute-done.17.refs_12_), channel_id=1, source_target_pairs={{0,1},{1,0},{2,3},{3,2},{4,5},{5,4},{6,7},{7,6},{8,9},{9,8},{10,11... | collective-permute-start | bytes 589832 | tf_op jit(solution)/shard_map/ppermute | solution.py:243
  50.6 3.8 %collective-permute-start.22 = (bf16[136,768]{1,0:T(8,128)(2,1)S(1)}, bf16[136,768]{1,0:T(8,128)(2,1)S(1)}, u32[]{:S(2)}, u32[]{:S(2)}) collective-permute-start(bf16[136,768]{1,0:T(8,128)(2,1)S(1)} %collective-permute-done.8.refs_9_.refs_13_), channel_id=1, source_target_pairs={{0,1},{1,0},{2,3},{3,2},{4,5},{5,4},{6,7},{7,6},{8,9},{9,8},{10,11... | collective-permute-start | bytes 626696 | tf_op jit(solution)/shard_map/ppermute | solution.py:243
  50.9 3.6 %collective-permute-start.23 = (bf16[136,768]{1,0:T(8,128)(2,1)S(1)}, bf16[136,768]{1,0:T(8,128)(2,1)S(1)}, u32[]{:S(2)}, u32[]{:S(2)}) collective-permute-start(bf16[136,768]{1,0:T(8,128)(2,1)S(1)} %collective-permute-done.9.refs_10_.refs_14_), channel_id=1, source_target_pairs={{0,1},{1,0},{2,3},{3,2},{4,5},{5,4},{6,7},{7,6},{8,9},{9,8},{10,11... | collective-permute-start | bytes 626696 | tf_op jit(solution)/shard_map/ppermute | solution.py:243
  52.0 2.4 %collective-permute-start.18 = (bf16[136,768]{1,0:T(8,128)(2,1)S(1)}, bf16[136,768]{1,0:T(8,128)(2,1)S(1)}, u32[]{:S(2)}, u32[]{:S(2)}) collective-permute-start(bf16[136,768]{1,0:T(8,128)(2,1)S(1)} %collective-permute-done.14.refs_9_), channel_id=1, source_target_pairs={{0,1},{1,0},{2,3},{3,2},{4,5},{5,4},{6,7},{7,6},{8,9},{9,8},{10,11... | collective-permute-start | bytes 626696 | tf_op jit(solution)/shard_map/ppermute | solution.py:243
  54.4 1.5 %collective-permute-start.19 = (bf16[136,768]{1,0:T(8,128)(2,1)S(1)}, bf16[136,768]{1,0:T(8,128)(2,1)S(1)}, u32[]{:S(2)}, u32[]{:S(2)}) collective-permute-start(bf16[136,768]{1,0:T(8,128)(2,1)S(1)} %collective-permute-done.15.refs_10_), channel_id=1, source_target_pairs={{0,1},{1,0},{2,3},{3,2},{4,5},{5,4},{6,7},{7,6},{8,9},{9,8},{10,11... | collective-permute-start | bytes 626696 | tf_op jit(solution)/shard_map/ppermute | solution.py:243

commit v2 on v1

v2 whole, which is shorter than its diff:
```python
import functools
import math

import jax
import jax.numpy as jnp
from jax import lax
from jax.experimental import pallas as pl
from jax.experimental.pallas import tpu as pltpu
from jax.sharding import PartitionSpec as P

EPS = 1e-06
TEMP = 4.0
LANES = 128
SPLIT = 128.0
TAIL = 8
VMEM_LIMIT = 16 * 1024 * 1024
WEIGHT = 20


def ring_order(chips):
    if chips <= 8:
        return list(range(0, chips, 2)) + list(range(1, chips, 2))[::-1]
    return list(range(chips))


def ring_perm(count, shift):
    order = ring_order(count // 2)
    pairs = []
    for at, chip in enumerate(order):
        to = order[(at + shift) % len(order)]
        pairs += [(2 * chip + core, 2 * to + core) for core in range(2)]
    return pairs


VM = pl.BlockSpec(memory_space=pltpu.VMEM)
SM = pl.BlockSpec(memory_space=pltpu.SMEM)
HB = pl.BlockSpec(memory_space=pltpu.HBM)


def call(body, out_shape, in_specs, flops=1, out_specs=None, scratch=(), aliases=None,
         limit=VMEM_LIMIT):
    return pl.pallas_call(
        body,
        out_shape=out_shape,
        in_specs=in_specs,
        out_specs=out_specs or [VM] * len(out_shape),
        scratch_shapes=list(scratch),
        input_output_aliases=aliases or {},
        compiler_params=pltpu.CompilerParams(vmem_limit_bytes=limit),
        cost_estimate=pl.CostEstimate(flops=flops, bytes_accessed=1, transcendentals=0),
    )


def prep_body(emb_ref, pos_ref, a_ref, b_ref, ah_ref, bh_ref):
    half = ah_ref.shape[0]
    width = emb_ref.shape[1]
    pos = pos_ref[...]
    high = jnp.floor(pos * (1.0 / SPLIT))
    low = pos - high * SPLIT
    row = jnp.concatenate(
        [high[0:1], low[0:1], high[1:2], low[1:2], jnp.zeros((1, width - 4 * half), jnp.float32)],
        axis=1,
    )
    tail = jnp.broadcast_to(row, (TAIL, width)).astype(jnp.bfloat16)
    for i, whole, alone in ((0, a_ref, ah_ref), (1, b_ref, bh_ref)):
        emb = emb_ref[i * half : (i + 1) * half, :]
        unit = emb * lax.rsqrt(jnp.sum(emb * emb, axis=1, keepdims=True) + EPS)
        unit = unit.astype(jnp.bfloat16)
        alone[...] = unit
        whole[...] = jnp.concatenate([unit, tail], axis=0)


def rows_of(ref, half):
    return ref[...][:half]


def positions_of(ref, half):
    tail = ref[...][half:].astype(jnp.float32)
    return [
        tail[0:1, 2 * i * half : (2 * i + 1) * half] * SPLIT
        + tail[0:1, (2 * i + 1) * half : (2 * i + 2) * half]
        for i in range(2)
    ]


def column(row):
    size = row.shape[1]
    eye = lax.broadcasted_iota(jnp.int32, (size, size), 0) == lax.broadcasted_iota(
        jnp.int32, (size, size), 1
    )
    return jnp.sum(jnp.where(eye, row, 0.0), axis=1, keepdims=True)


def cluster_parts(pos, ends, clusters):
    index = jnp.zeros(pos.shape, jnp.int32)
    start = jnp.zeros(pos.shape, jnp.float32)
    for c in range(clusters - 1):
        past = pos >= ends[c]
        index = index + past.astype(jnp.int32)
        start = jnp.where(past, ends[c], start)
    return index, start


def ends_of(len_ref, clusters):
    ends, total = [], jnp.int32(0)
    for c in range(clusters - 1):
        total = total + len_ref[c]
        ends.append(total.astype(jnp.float32))
    return ends


def attend(
    rows, query, pos_b, start_b, feat, acc, top, keys, key_pos, ends, clusters, diagonal
):
    index, _ = cluster_parts(key_pos, ends, clusters)
    block = jnp.floor(key_pos * (1.0 / rows)).astype(jnp.int32)
    wanted = block * clusters + index
    size = key_pos.shape[1]
    onehot = (
        lax.broadcasted_iota(jnp.int32, (feat.shape[1], size), 0) == wanted
    ).astype(jnp.bfloat16)
    allowed = jnp.dot(feat, onehot, preferred_element_type=jnp.float32)
    scores = lax.dot_general(
        query, keys, (((1,), (1,)), ((), ())), preferred_element_type=jnp.float32
    )
    weights = []
    for at in range(0, size, LANES):
        part = scores[:, at : at + LANES]
        pos = key_pos[:, at : at + LANES]
        earlier = (pos < pos_b) & (pos >= start_b)
        top = jnp.maximum(top, jnp.where(earlier, part, -1.0))
        weight = jnp.exp2(part * (TEMP * math.log2(math.e)))
        masked = weight * allowed[:, at : at + LANES]
        if diagonal:
            masked = jnp.where(pos == pos_b, weight, masked)
        weights.append(masked.astype(jnp.bfloat16))
    acc = acc + jnp.dot(
        jnp.concatenate(weights, axis=1), keys, preferred_element_type=jnp.float32
    )
    return acc, top


def fold(rows, width, state, out_ref, query, info, feat, blocks, ends, clusters, diagonal=False):
    acc, top = state[:, :width], state[:, width:]
    for i, (keys, pos) in enumerate(blocks):
        acc, top = attend(
            rows, query, info[0], info[1], feat, acc, top, keys, pos, ends, clusters,
            diagonal and i == 0,
        )
    out_ref[:rows, :width] = acc
    out_ref[:rows, width:] = top


def first_body(half, clusters, len_ref, mask_hbm, a_ref, b_ref, sa_ref, sb_ref,
               f_ref, g_ref, own_ref, sib_ref, info_ref, feat_ref, mask_ref, sem):
    fetch = pltpu.make_async_copy(mask_hbm, mask_ref, sem.at[0])
    fetch.start()
    ends = ends_of(len_ref, clusters)
    own = positions_of(a_ref, half)
    sib = positions_of(sa_ref, half)
    pos = jnp.concatenate([column(r) for r in own + sib], axis=0)
    index, start = cluster_parts(pos, ends, clusters)
    count = mask_ref.shape[0]
    rows = 2 * half
    width = a_ref.shape[1]
    block = jnp.floor(pos * (1.0 / rows)).astype(jnp.int32)
    total = pos.shape[0]
    onehot = (block == lax.broadcasted_iota(jnp.int32, (total, count), 1)).astype(jnp.bfloat16)
    wide = count * clusters
    spread = (
        lax.broadcasted_iota(jnp.int32, (count, wide), 1) // clusters
        == lax.broadcasted_iota(jnp.int32, (count, wide), 0)
    ).astype(jnp.bfloat16)
    fetch.wait()
    picked = jnp.dot(
        onehot, mask_ref[...].astype(jnp.bfloat16), preferred_element_type=jnp.float32
    ).astype(jnp.bfloat16)
    picked = jnp.dot(picked, spread, preferred_element_type=jnp.float32)
    lane_cluster = lax.broadcasted_iota(jnp.int32, (total, wide), 1) % clusters
    feat = jnp.where(lane_cluster == index, picked, 0.0).astype(jnp.bfloat16)
    feat_ref[...] = feat
    info_ref[0] = jnp.broadcast_to(pos, (total, LANES))
    info_ref[1] = jnp.broadcast_to(start, (total, LANES))
    keys = jnp.concatenate([rows_of(r, half) for r in (a_ref, b_ref)], axis=0)
    blocks = [(keys, jnp.concatenate(own, axis=1))]
    blocks += gather_keys((f_ref, g_ref), (((0, 0, 0), (1, 1, 1)),), half)
    state = jnp.concatenate(
        [jnp.zeros((rows, width), jnp.float32), jnp.full((rows, LANES), -1.0, jnp.float32)],
        axis=1,
    )
    fold(rows, width, state, own_ref, keys, info_ref[:, :rows], feat[:rows], blocks, ends,
         clusters, True)
    other = jnp.concatenate([rows_of(r, half) for r in (sa_ref, sb_ref)], axis=0)
    fold(rows, width, state, sib_ref, other, info_ref[:, rows:], feat[rows:], blocks, ends,
         clusters)


def gather_keys(key_refs, groups, half):
    out = []
    for group in groups:
        keys = jnp.concatenate([rows_of(key_refs[r], half) for r, _, _ in group], axis=0)
        pos = jnp.concatenate(
            [positions_of(key_refs[p], half)[w] for _, p, w in group], axis=1
        )
        out.append((keys, pos))
    return out


def middle_body(half, clusters, groups, len_ref, info_ref, feat_ref, a_ref, b_ref, sa_ref,
                sb_ref, own_in, sib_in, *refs):
    key_refs, (own_ref, sib_ref) = refs[:-2], refs[-2:]
    ends = ends_of(len_ref, clusters)
    rows, width = 2 * half, a_ref.shape[1]
    blocks = gather_keys(key_refs, groups, half)
    for i, state_in, state_out, pair in (
        (0, own_in, own_ref, (a_ref, b_ref)), (1, sib_in, sib_ref, (sa_ref, sb_ref))
    ):
        query = jnp.concatenate([rows_of(r, half) for r in pair], axis=0)
        part = slice(i * rows, (i + 1) * rows)
        fold(rows, width, state_in[...], state_out, query, info_ref[:, part], feat_ref[part],
             blocks, ends, clusters)


def late_body(half, clusters, len_ref, info_ref, feat_ref, a_ref, b_ref, own_in, *refs):
    key_refs, own_ref = refs[:-1], refs[-1]
    ends = ends_of(len_ref, clusters)
    rows, width = 2 * half, a_ref.shape[1]
    blocks = gather_keys(key_refs, (((0, 0, 0), (1, 1, 1)),), half)
    query = jnp.concatenate([rows_of(r, half) for r in (a_ref, b_ref)], axis=0)
    fold(rows, width, own_in[...], own_ref, query, info_ref[:, :rows], feat_ref[:rows],
         blocks, ends, clusters)


def last_body(half, clusters, groups, len_ref, info_ref, feat_ref, a_ref, b_ref, own_in, got_ref,
              *refs):
    key_refs, (dir_ref, out_top) = refs[:-2], refs[-2:]
    ends = ends_of(len_ref, clusters)
    rows, width = 2 * half, a_ref.shape[1]
    query = jnp.concatenate([rows_of(r, half) for r in (a_ref, b_ref)], axis=0)
    acc = own_in[:, :width] + got_ref[:, :width]
    top = jnp.maximum(own_in[:, width:], got_ref[:, width:])
    for keys, pos in gather_keys(key_refs, groups, half):
        acc, top = attend(
            rows, query, info_ref[0, :rows], info_ref[1, :rows], feat_ref[:rows], acc, top, keys,
            pos, ends, clusters, False,
        )
    scale = math.sqrt(width) * lax.rsqrt(jnp.sum(acc * acc, axis=1, keepdims=True) + EPS)
    dir_ref[...] = (acc * scale).astype(jnp.bfloat16)
    best = jnp.max(top, axis=1, keepdims=True)
    eye = lax.broadcasted_iota(jnp.int32, (half, half), 0) == lax.broadcasted_iota(
        jnp.int32, (half, half), 1
    )
    lines = [
        jnp.max(jnp.where(eye, best[at : at + half], -1.0), axis=0, keepdims=True)
        for at in (0, half)
    ]
    out_top[...] = jnp.concatenate(lines, axis=0)


def after(x, *before):
    return lax.optimization_barrier((x, *before))[0]


def per_device(embeddings, dest_pos, cluster_lengths, block_mask):
    rows, width = embeddings.shape
    half = rows // 2
    count = lax.axis_size("blk")
    clusters = cluster_lengths.shape[0]
    steps = count // 4
    ahead, back = ring_perm(count, 1), ring_perm(count, -1)
    sibling = [(i, i ^ 1) for i in range(count)]

    def move(x, perm):
        return lax.ppermute(x, "blk", perm)

    def bf(n, w=width):
        return jax.ShapeDtypeStruct((n, w), jnp.bfloat16)

    def f32(*s):
        return jax.ShapeDtypeStruct(s, jnp.float32)

    full = half + TAIL
    wide = width + LANES
    state = f32(rows, wide)
    a, b, ah, bh = call(
        prep_body, [bf(full), bf(full), bf(half), bf(half)], [VM, VM],
    )(embeddings, dest_pos.reshape(2, half).astype(jnp.float32))

    lead = [(move(a, ahead), move(b, back))]
    follow = [(move(bh, ahead), move(ah, back))]
    sa, sb = move(a, sibling), move(b, sibling)
    work = 8 * rows * rows * width * WEIGHT
    own, sib, info, feat = call(
        functools.partial(first_body, half, clusters),
        [state, state, f32(2, 2 * rows, LANES), bf(2 * rows, count * clusters)],
        [SM, HB] + [VM] * 6, work,
        scratch=[pltpu.VMEM(block_mask.shape, jnp.int32), pltpu.SemaphoreType.DMA((1,))],
    )(cluster_lengths, block_mask, a, b, sa, sb, *lead[0])

    def middle(own, sib, keys, groups, work):
        return call(
            functools.partial(middle_body, half, clusters, groups), [state, state],
            [SM] + [VM] * (8 + len(keys)), work, aliases={7: 0, 8: 1},
        )(cluster_lengths, info, feat, a, b, sa, sb, own, sib, *keys)

    both = ((0, 0, 0), (1, 1, 1))
    for step in range(1, steps):
        f, g = lead[-1]
        lead.append((move(after(f, sa), ahead), move(after(g, sb), back)))
        if step > 1:
            own, sib = middle(
                own, sib, (*lead[-2], *follow[-2], *lead[-3]), (((2, 4, 1), (3, 5, 0)), both),
                work,
            )
        if step < steps - 1:
            f, g = follow[-1]
            follow.append((move(after(f, own), ahead), move(after(g, own), back)))
    own, sib = middle(own, sib, (*lead[-2], *follow[-1]), (((2, 0, 1), (3, 1, 0)),), 1)
    got = move(sib, sibling)
    far = [move(after(x, own), sibling) for x in lead[-1]]
    shared = (cluster_lengths, info, feat, a, b)
    own = call(
        functools.partial(late_body, half, clusters), [state], [SM] + [VM] * 7, work, aliases={5: 0},
    )(*shared, own, *lead[-1])[0]
    out_dir, out_top = call(
        functools.partial(last_body, half, clusters, (both,)),
        [bf(rows), f32(2, half)], [SM] + [VM] * 8,
    )(*shared, own, got, *far)
    return out_top.reshape(rows), out_dir


def solution(mesh):
    placed = (P(("groups", "blk"), None), P(("groups", "blk")), P("groups"), P("groups", None))
    return jax.shard_map(
        per_device,
        mesh=mesh,
        in_specs=placed,
        out_specs=(P(("groups", "blk")), P(("groups", "blk"), None)),
        check_vma=False,
    )
```

time: 60.1 us -> 44.2 us (0.74)
  waiting for transfers between devices: 21.1 us -> 11.7 us
  local copies, waits for them, and re-layouts: 5.55 us -> 1.14 us
  starting transfers between devices: 18.6 us -> 17.1 us
  Pallas kernels: 13.8 us -> 12.7 us
  other arithmetic: 0 us -> 0.68 us
    ppermute x24 -> x19, waiting for transfers between devices: 21.1 us -> 11.7 us  [move(): return lax.ppermute(x, 'blk', perm)]
    unnamed x14 -> x6, local copies, waits for them, and re-layouts: 5.49 us -> 1.14 us
    ppermute x24 -> x19, starting transfers between devices: 18.6 us -> 17.1 us  [move(): return lax.ppermute(x, 'blk', perm)]
    pallas_call x6 -> x7, Pallas kernels: 13.8 us -> 12.7 us  [the longest x3 6.41 us: middle(): call(functools.partial(middle_body, half, clusters, groups), [state, stat...]
    convert_element_type x0 -> x1, other arithmetic: none -> 0.68 us  [per_device(): dest_pos.reshape(2, half).astype(jnp.float32)]
  transfers between devices with their start and end apart: 24 -> 19, of which waited for: 12 -> 13; matrix products, arithmetic and copies ran while one was open for 0% -> 0% of each run, Pallas kernels for 11% -> 24%
where the time goes in v2:
time: 44.2 us; the launch traced here: 44 us
  starting transfers between devices  17.1 us (39%)
  Pallas kernels  12.7 us (29%)
  waiting for transfers between devices  11.7 us (26%)
  local copies, waits for them, and re-layouts  1.14 us (3%)
  between operations  0.71 us (2%)
  other arithmetic  0.68 us (2%)
    ppermute x19, starting transfers between devices, move(): return lax.ppermute(x, 'blk', perm)  17.1 us
    ppermute x19, waiting for transfers between devices, move(): return lax.ppermute(x, 'blk', perm)  11.7 us
    pallas_call x3, Pallas kernels, middle(): call(functools.partial(middle_body, half, clusters, groups), [state, stat...  6.41 us
    pallas_call x1, Pallas kernels, per_device(): call(functools.partial(first_body, half, clusters), [state, state, f32(2,...  2.78 us
    pallas_call x1, Pallas kernels, per_device(): call(functools.partial(last_body, half, clusters, (both,)), [bf(rows), f3...  2.09 us
    pallas_call x1, Pallas kernels, per_device(): call(functools.partial(late_body, half, clusters), [state], [SM] + [VM] *...  1.25 us
    unnamed x6, local copies, waits for them, and re-layouts  1.14 us
  transfers between devices with their start and end apart: 19, of which 13 were waited for; matrix products, arithmetic and copies ran while one was open for 0% of the time, Pallas kernels for 24%

profile of v2, /device:TPU:0, one launch (start us, length us, event | category | flops | bytes accessed | tf_op | source)
XLA Modules:
  0.0 44.0 jit_solution(7637711251887470107)
XLA Ops:
  0.6 0.7 %convert_bitcast_fusion.pos_ref = f32[2,128]{1,0:T(2,128)S(1)} fusion(s32[256]{0:T(256)} %param.5), kind=kLoop, calls=%fused_computation | loop fusion | flops 256 | bytes 2048 | tf_op jit(solution)/shard_map/convert_element_type | solution.py:287
  1.3 1.1 %copy-done = f32[256,768]{1,0:T(8,128)S(1)} copy-done((f32[256,768]{1,0:T(8,128)S(1)}, f32[256,768]{1,0:T(8,128)}, u32[]{:S(2)}) %copy-start) | copy-done | bytes 786456
  2.6 0.5 %collective-permute-start = (bf16[136,768]{1,0:T(8,128)(2,1)S(1)}, bf16[136,768]{1,0:T(8,128)(2,1)S(1)}, u32[]{:S(2)}, u32[]{:S(2)}) collective-permute-start(bf16[136,768]{1,0:T(8,128)(2,1)S(1)} %get-tuple-element.30.a_ref), channel_id=1, source_target_pairs={{0,1},{1,0},{2,3},{3,2},{4,5},{5,4},{6,7},{7,6},{8,9},{9,8},{10,11... | collective-permute-start | bytes 626696 | tf_op jit(solution)/shard_map/ppermute | solution.py:274
  3.1 2.6 %collective-permute-start.2 = (bf16[136,768]{1,0:T(8,128)(2,1)S(1)}, bf16[136,768]{1,0:T(8,128)(2,1)S(1)}, u32[]{:S(2)}, u32[]{:S(2)}) collective-permute-start(bf16[136,768]{1,0:T(8,128)(2,1)S(1)} %get-tuple-element.30.a_ref), channel_id=1, source_target_pairs={{0,4},{1,5},{4,8},{5,9},{8,12},{9,13},{12,14},{13,15},{14,10},{15,... | collective-permute-start | bytes 626696 | tf_op jit(solution)/shard_map/ppermute | solution.py:274
  6.1 1.7 %collective-permute-start.7 = (bf16[128,768]{1,0:T(8,128)(2,1)S(1)}, bf16[128,768]{1,0:T(8,128)(2,1)S(1)}, u32[]{:S(2)}, u32[]{:S(2)}) collective-permute-start(bf16[128,768]{1,0:T(8,128)(2,1)S(1)} %get-tuple-element.39), channel_id=1, source_target_pairs={{0,2},{1,3},{4,0},{5,1},{8,4},{9,5},{12,8},{13,9},{14,12},{15,13},... | collective-permute-start | bytes 589832 | tf_op jit(solution)/shard_map/ppermute | solution.py:274
  7.9 0.3 collective-permute-start.6
  8.2 3.5 %collective-permute-done.2.f_ref.refs_4_ = bf16[136,768]{1,0:T(8,128)(2,1)S(1)} collective-permute-done((bf16[136,768]{1,0:T(8,128)(2,1)S(1)}, bf16[136,768]{1,0:T(8,128)(2,1)S(1)}, u32[]{:S(2)}, u32[]{:S(2)}) %collective-permute-start.2) | collective-permute-done | bytes 208928 | tf_op jit(solution)/shard_map/ppermute | solution.py:274
  11.7 2.0 %collective-permute-start.4 = (bf16[136,768]{1,0:T(8,128)(2,1)S(1)}, bf16[136,768]{1,0:T(8,128)(2,1)S(1)}, u32[]{:S(2)}, u32[]{:S(2)}) collective-permute-start(bf16[136,768]{1,0:T(8,128)(2,1)S(1)} %collective-permute-done.2.f_ref.refs_4_), channel_id=1, source_target_pairs={{0,4},{1,5},{4,8},{5,9},{8,12},{9,13},{12,14},{13,15},{14,10},{15,... | collective-permute-start | bytes 626696 | tf_op jit(solution)/shard_map/ppermute | solution.py:274
  14.1 2.8 %shard_map.60 = (f32[256,896]{1,0:T(8,128)S(1)}, f32[256,896]{1,0:T(8,128)S(1)}, f32[2,512,128]{2,1,0:T(8,128)S(1)}, bf16[512,64]{1,0:T(8,128)(2,1)S(1)}) custom-call(s32[4]{0:T(128)S(1)} %copy-done.1, s32[16,16]{1,0:T(8,128)S(1)} %copy-done.2, bf16[136,768]{1,0:T(8,128)(2,1)S(1)} %get-tuple-element.30.a_ref, bf16[136,768]{1,0:T(8,128)(2,1)S(1)} %get-tuple-element.31.b_ref, ...), custom_call_target="tpu_custom_call" | custom-call | flops 8053063680 | bytes 1 | tf_op jit(solution)/shard_map/pallas_call | solution.py:293
  16.9 1.2 %collective-permute-done.7.refs_3_ = bf16[128,768]{1,0:T(8,128)(2,1)S(1)} collective-permute-done((bf16[128,768]{1,0:T(8,128)(2,1)S(1)}, bf16[128,768]{1,0:T(8,128)(2,1)S(1)}, u32[]{:S(2)}, u32[]{:S(2)}) %collective-permute-start.7) | collective-permute-done | bytes 196640 | tf_op jit(solution)/shard_map/ppermute | solution.py:274
  18.1 1.6 %collective-permute-start.10 = (bf16[128,768]{1,0:T(8,128)(2,1)S(1)}, bf16[128,768]{1,0:T(8,128)(2,1)S(1)}, u32[]{:S(2)}, u32[]{:S(2)}) collective-permute-start(bf16[128,768]{1,0:T(8,128)(2,1)S(1)} %collective-permute-done.6.refs_2_), channel_id=1, source_target_pairs={{0,4},{1,5},{4,8},{5,9},{8,12},{9,13},{12,14},{13,15},{14,10},{15,... | collective-permute-start | bytes 589832 | tf_op jit(solution)/shard_map/ppermute | solution.py:274
  19.7 0.5 %collective-permute-start.11 = (bf16[128,768]{1,0:T(8,128)(2,1)S(1)}, bf16[128,768]{1,0:T(8,128)(2,1)S(1)}, u32[]{:S(2)}, u32[]{:S(2)}) collective-permute-start(bf16[128,768]{1,0:T(8,128)(2,1)S(1)} %collective-permute-done.7.refs_3_), channel_id=1, source_target_pairs={{0,2},{1,3},{4,0},{5,1},{8,4},{9,5},{12,8},{13,9},{14,12},{15,13},... | collective-permute-start | bytes 589832 | tf_op jit(solution)/shard_map/ppermute | solution.py:274
  20.2 0.2 collective-permute-done.4.refs_0_.refs_4_
  20.4 2.0 %collective-permute-start.8 = (bf16[136,768]{1,0:T(8,128)(2,1)S(1)}, bf16[136,768]{1,0:T(8,128)(2,1)S(1)}, u32[]{:S(2)}, u32[]{:S(2)}) collective-permute-start(bf16[136,768]{1,0:T(8,128)(2,1)S(1)} %collective-permute-done.4.refs_0_.refs_4_), channel_id=1, source_target_pairs={{0,4},{1,5},{4,8},{5,9},{8,12},{9,13},{12,14},{13,15},{14,10},{15,... | collective-permute-start | bytes 626696 | tf_op jit(solution)/shard_map/ppermute | solution.py:274
  22.8 2.3 %shard_map.61 = (f32[256,896]{1,0:T(8,128)S(1)}, f32[256,896]{1,0:T(8,128)S(1)}) custom-call(s32[4]{0:T(128)S(1)} %copy-done.1, f32[2,512,128]{2,1,0:T(8,128)S(1)} %get-tuple-element.32.info_ref, bf16[512,64]{1,0:T(8,128)(2,1)S(1)} %get-tuple-element.33.feat_ref, ...), custom_call_target="tpu_custom_call", output_to_operand_aliasing={{0}: (7, {}), {1}: (8, {})} | custom-call | flops 8053063680 | bytes 1 | tf_op jit(solution)/shard_map/pallas_call | solution.py:301
  25.1 0.9 %collective-permute-done.10.refs_2_ = bf16[128,768]{1,0:T(8,128)(2,1)S(1)} collective-permute-done((bf16[128,768]{1,0:T(8,128)(2,1)S(1)}, bf16[128,768]{1,0:T(8,128)(2,1)S(1)}, u32[]{:S(2)}, u32[]{:S(2)}) %collective-permute-start.10) | collective-permute-done | bytes 196640 | tf_op jit(solution)/shard_map/ppermute | solution.py:274
  26.0 1.6 %collective-permute-done.11.refs_3_ = bf16[128,768]{1,0:T(8,128)(2,1)S(1)} collective-permute-done((bf16[128,768]{1,0:T(8,128)(2,1)S(1)}, bf16[128,768]{1,0:T(8,128)(2,1)S(1)}, u32[]{:S(2)}, u32[]{:S(2)}) %collective-permute-start.11) | collective-permute-done | bytes 196640 | tf_op jit(solution)/shard_map/ppermute | solution.py:274
  27.5 1.6 %collective-permute-start.12 = (bf16[128,768]{1,0:T(8,128)(2,1)S(1)}, bf16[128,768]{1,0:T(8,128)(2,1)S(1)}, u32[]{:S(2)}, u32[]{:S(2)}) collective-permute-start(bf16[128,768]{1,0:T(8,128)(2,1)S(1)} %collective-permute-done.10.refs_2_), channel_id=1, source_target_pairs={{0,4},{1,5},{4,8},{5,9},{8,12},{9,13},{12,14},{13,15},{14,10},{15,... | collective-permute-start | bytes 589832 | tf_op jit(solution)/shard_map/ppermute | solution.py:274
  29.1 0.4 %collective-permute-start.13 = (bf16[128,768]{1,0:T(8,128)(2,1)S(1)}, bf16[128,768]{1,0:T(8,128)(2,1)S(1)}, u32[]{:S(2)}, u32[]{:S(2)}) collective-permute-start(bf16[128,768]{1,0:T(8,128)(2,1)S(1)} %collective-permute-done.11.refs_3_), channel_id=1, source_target_pairs={{0,2},{1,3},{4,0},{5,1},{8,4},{9,5},{12,8},{13,9},{14,12},{15,13},... | collective-permute-start | bytes 589832 | tf_op jit(solution)/shard_map/ppermute | solution.py:274
  29.6 0.4 collective-permute-done.8.refs_0_
  30.0 2.0 %collective-permute-start.14 = (bf16[136,768]{1,0:T(8,128)(2,1)S(1)}, bf16[136,768]{1,0:T(8,128)(2,1)S(1)}, u32[]{:S(2)}, u32[]{:S(2)}) collective-permute-start(bf16[136,768]{1,0:T(8,128)(2,1)S(1)} %collective-permute-done.8.refs_0_), channel_id=1, source_target_pairs={{0,4},{1,5},{4,8},{5,9},{8,12},{9,13},{12,14},{13,15},{14,10},{15,... | collective-permute-start | bytes 626696 | tf_op jit(solution)/shard_map/ppermute | solution.py:274
  32.0 0.5 %collective-permute-start.15 = (bf16[136,768]{1,0:T(8,128)(2,1)S(1)}, bf16[136,768]{1,0:T(8,128)(2,1)S(1)}, u32[]{:S(2)}, u32[]{:S(2)}) collective-permute-start(bf16[136,768]{1,0:T(8,128)(2,1)S(1)} %collective-permute-done.9.refs_1_), channel_id=1, source_target_pairs={{0,2},{1,3},{4,0},{5,1},{8,4},{9,5},{12,8},{13,9},{14,12},{15,13},... | collective-permute-start | bytes 626696 | tf_op jit(solution)/shard_map/ppermute | solution.py:274
  32.5 2.3 %shard_map.62 = (f32[256,896]{1,0:T(8,128)S(1)}, f32[256,896]{1,0:T(8,128)S(1)}) custom-call(s32[4]{0:T(128)S(1)} %copy-done.1, f32[2,512,128]{2,1,0:T(8,128)S(1)} %get-tuple-element.32.info_ref, bf16[512,64]{1,0:T(8,128)(2,1)S(1)} %get-tuple-element.33.feat_ref, ...), custom_call_target="tpu_custom_call", output_to_operand_aliasing={{0}: (7, {}), {1}: (8, {})} | custom-call | flops 8053063680 | bytes 1 | tf_op jit(solution)/shard_map/pallas_call | solution.py:301
  34.8 0.5 %collective-permute-done.12.refs_2_ = bf16[128,768]{1,0:T(8,128)(2,1)S(1)} collective-permute-done((bf16[128,768]{1,0:T(8,128)(2,1)S(1)}, bf16[128,768]{1,0:T(8,128)(2,1)S(1)}, u32[]{:S(2)}, u32[]{:S(2)}) %collective-permute-start.12) | collective-permute-done | bytes 196640 | tf_op jit(solution)/shard_map/ppermute | solution.py:274
  35.3 1.7 %collective-permute-done.13.refs_3_ = bf16[128,768]{1,0:T(8,128)(2,1)S(1)} collective-permute-done((bf16[128,768]{1,0:T(8,128)(2,1)S(1)}, bf16[128,768]{1,0:T(8,128)(2,1)S(1)}, u32[]{:S(2)}, u32[]{:S(2)}) %collective-permute-start.13) | collective-permute-done | bytes 196640 | tf_op jit(solution)/shard_map/ppermute | solution.py:274
  36.9 1.8 %shard_map.63 = (f32[256,896]{1,0:T(8,128)S(1)}, f32[256,896]{1,0:T(8,128)S(1)}) custom-call(s32[4]{0:T(128)S(1)} %copy-done.1, f32[2,512,128]{2,1,0:T(8,128)S(1)} %get-tuple-element.32.info_ref, bf16[512,64]{1,0:T(8,128)(2,1)S(1)} %get-tuple-element.33.feat_ref, ...), custom_call_target="tpu_custom_call", output_to_operand_aliasing={{0}: (7, {}), {1}: (8, {})} | custom-call | flops 1 | bytes 1 | tf_op jit(solution)/shard_map/pallas_call | solution.py:301
  38.8 0.6 %collective-permute-done.15.refs_1_ = bf16[136,768]{1,0:T(8,128)(2,1)S(1)} collective-permute-done((bf16[136,768]{1,0:T(8,128)(2,1)S(1)}, bf16[136,768]{1,0:T(8,128)(2,1)S(1)}, u32[]{:S(2)}, u32[]{:S(2)}) %collective-permute-start.15) | collective-permute-done | bytes 208928 | tf_op jit(solution)/shard_map/ppermute | solution.py:274
  39.4 0.5 %collective-permute-start.18 = (bf16[136,768]{1,0:T(8,128)(2,1)S(1)}, bf16[136,768]{1,0:T(8,128)(2,1)S(1)}, u32[]{:S(2)}, u32[]{:S(2)}) collective-permute-start(bf16[136,768]{1,0:T(8,128)(2,1)S(1)} %collective-permute-done.15.refs_1_), channel_id=1, source_target_pairs={{0,1},{1,0},{2,3},{3,2},{4,5},{5,4},{6,7},{7,6},{8,9},{9,8},{10,11... | collective-permute-start | bytes 626696 | tf_op jit(solution)/shard_map/ppermute | solution.py:274
  39.9 1.3 %shard_map.64.own_in = f32[256,896]{1,0:T(8,128)S(1)} custom-call(s32[4]{0:T(128)S(1)} %copy-done.1, f32[2,512,128]{2,1,0:T(8,128)S(1)} %get-tuple-element.32.info_ref, bf16[512,64]{1,0:T(8,128)(2,1)S(1)} %get-tuple-element.33.feat_ref, bf16[136,768]{1,0:T(8,128)(2,1)S(1)} %get-tuple-element.30.a_ref, ...), custom_call_target="tpu_custom_call", output_to_operand_aliasing={{}: (5, {})} | custom-call | flops 8053063680 | bytes 1 | tf_op jit(solution)/shard_map/pallas_call | solution.py:322
  41.2 0.4 collective-permute-done.17.refs_0_
  41.6 0.3 collective-permute-done.18.refs_1_
  41.9 2.1 %shard_map.65 = (bf16[256,768]{1,0:T(8,128)(2,1)}, f32[2,128]{1,0:T(2,128)}) custom-call(s32[4]{0:T(128)S(1)} %copy-done.1, f32[2,512,128]{2,1,0:T(8,128)S(1)} %get-tuple-element.32.info_ref, bf16[512,64]{1,0:T(8,128)(2,1)S(1)} %get-tuple-element.33.feat_ref, bf16[136,768]{1,0:T(8,128)(2,1)S(1)} %get-tuple-element.30.a_ref, ...), custom_call_target="tpu_custom_call" | custom-call | flops 1 | bytes 1 | tf_op jit(solution)/shard_map/pallas_call | solution.py:325
  (20 shorter events, 1.4 us)
Async XLA Ops:
  1.3 1.1 %copy-start = (f32[256,768]{1,0:T(8,128)S(1)}, f32[256,768]{1,0:T(8,128)}, u32[]{:S(2)}) copy-start(f32[256,768]{1,0:T(8,128)} %emb_ref.1) | copy-start | bytes 2359300
  2.4 11.7 %copy-start.2 = (s32[16,16]{1,0:T(8,128)S(1)}, s32[16,16]{1,0:T(8,128)}, u32[]{:S(2)}) copy-start(s32[16,16]{1,0:T(8,128)} %mask_hbm.1) | copy-start | bytes 3076
  2.6 5.3 %collective-permute-start = (bf16[136,768]{1,0:T(8,128)(2,1)S(1)}, bf16[136,768]{1,0:T(8,128)(2,1)S(1)}, u32[]{:S(2)}, u32[]{:S(2)}) collective-permute-start(bf16[136,768]{1,0:T(8,128)(2,1)S(1)} %get-tuple-element.30.a_ref), channel_id=1, source_target_pairs={{0,1},{1,0},{2,3},{3,2},{4,5},{5,4},{6,7},{7,6},{8,9},{9,8},{10,11... | collective-permute-start | bytes 626696 | tf_op jit(solution)/shard_map/ppermute | solution.py:274
  3.1 8.6 %collective-permute-start.2 = (bf16[136,768]{1,0:T(8,128)(2,1)S(1)}, bf16[136,768]{1,0:T(8,128)(2,1)S(1)}, u32[]{:S(2)}, u32[]{:S(2)}) collective-permute-start(bf16[136,768]{1,0:T(8,128)(2,1)S(1)} %get-tuple-element.30.a_ref), channel_id=1, source_target_pairs={{0,4},{1,5},{4,8},{5,9},{8,12},{9,13},{12,14},{13,15},{14,10},{15,... | collective-permute-start | bytes 626696 | tf_op jit(solution)/shard_map/ppermute | solution.py:274
  5.7 8.0 %collective-permute-start.1 = (bf16[136,768]{1,0:T(8,128)(2,1)S(1)}, bf16[136,768]{1,0:T(8,128)(2,1)S(1)}, u32[]{:S(2)}, u32[]{:S(2)}) collective-permute-start(bf16[136,768]{1,0:T(8,128)(2,1)S(1)} %get-tuple-element.31.b_ref), channel_id=1, source_target_pairs={{0,1},{1,0},{2,3},{3,2},{4,5},{5,4},{6,7},{7,6},{8,9},{9,8},{10,11... | collective-permute-start | bytes 626696 | tf_op jit(solution)/shard_map/ppermute | solution.py:274
  5.9 8.0 %collective-permute-start.3 = (bf16[136,768]{1,0:T(8,128)(2,1)S(1)}, bf16[136,768]{1,0:T(8,128)(2,1)S(1)}, u32[]{:S(2)}, u32[]{:S(2)}) collective-permute-start(bf16[136,768]{1,0:T(8,128)(2,1)S(1)} %get-tuple-element.31.b_ref), channel_id=1, source_target_pairs={{0,2},{1,3},{4,0},{5,1},{8,4},{9,5},{12,8},{13,9},{14,12},{15,13},... | collective-permute-start | bytes 626696 | tf_op jit(solution)/shard_map/ppermute | solution.py:274
  6.1 8.0 %copy-start.1 = (s32[4]{0:T(128)S(1)}, s32[4]{0:T(128)}, u32[]{:S(2)}) copy-start(s32[4]{0:T(128)} %len_ref.11) | copy-start | bytes 52
  6.1 12.0 %collective-permute-start.7 = (bf16[128,768]{1,0:T(8,128)(2,1)S(1)}, bf16[128,768]{1,0:T(8,128)(2,1)S(1)}, u32[]{:S(2)}, u32[]{:S(2)}) collective-permute-start(bf16[128,768]{1,0:T(8,128)(2,1)S(1)} %get-tuple-element.39), channel_id=1, source_target_pairs={{0,2},{1,3},{4,0},{5,1},{8,4},{9,5},{12,8},{13,9},{14,12},{15,13},... | collective-permute-start | bytes 589832 | tf_op jit(solution)/shard_map/ppermute | solution.py:274
  7.9 10.2 %collective-permute-start.6 = (bf16[128,768]{1,0:T(8,128)(2,1)S(1)}, bf16[128,768]{1,0:T(8,128)(2,1)S(1)}, u32[]{:S(2)}, u32[]{:S(2)}) collective-permute-start(bf16[128,768]{1,0:T(8,128)(2,1)S(1)} %get-tuple-element.38), channel_id=1, source_target_pairs={{0,4},{1,5},{4,8},{5,9},{8,12},{9,13},{12,14},{13,15},{14,10},{15,... | collective-permute-start | bytes 589832 | tf_op jit(solution)/shard_map/ppermute | solution.py:274
  11.7 8.7 %collective-permute-start.4 = (bf16[136,768]{1,0:T(8,128)(2,1)S(1)}, bf16[136,768]{1,0:T(8,128)(2,1)S(1)}, u32[]{:S(2)}, u32[]{:S(2)}) collective-permute-start(bf16[136,768]{1,0:T(8,128)(2,1)S(1)} %collective-permute-done.2.f_ref.refs_4_), channel_id=1, source_target_pairs={{0,4},{1,5},{4,8},{5,9},{8,12},{9,13},{12,14},{13,15},{14,10},{15,... | collective-permute-start | bytes 626696 | tf_op jit(solution)/shard_map/ppermute | solution.py:274
  13.9 8.7 %collective-permute-start.5 = (bf16[136,768]{1,0:T(8,128)(2,1)S(1)}, bf16[136,768]{1,0:T(8,128)(2,1)S(1)}, u32[]{:S(2)}, u32[]{:S(2)}) collective-permute-start(bf16[136,768]{1,0:T(8,128)(2,1)S(1)} %collective-permute-done.3.g_ref.refs_5_), channel_id=1, source_target_pairs={{0,2},{1,3},{4,0},{5,1},{8,4},{9,5},{12,8},{13,9},{14,12},{15,13},... | collective-permute-start | bytes 626696 | tf_op jit(solution)/shard_map/ppermute | solution.py:274
  18.1 7.8 %collective-permute-start.10 = (bf16[128,768]{1,0:T(8,128)(2,1)S(1)}, bf16[128,768]{1,0:T(8,128)(2,1)S(1)}, u32[]{:S(2)}, u32[]{:S(2)}) collective-permute-start(bf16[128,768]{1,0:T(8,128)(2,1)S(1)} %collective-permute-done.6.refs_2_), channel_id=1, source_target_pairs={{0,4},{1,5},{4,8},{5,9},{8,12},{9,13},{12,14},{13,15},{14,10},{15,... | collective-permute-start | bytes 589832 | tf_op jit(solution)/shard_map/ppermute | solution.py:274
  19.7 7.8 %collective-permute-start.11 = (bf16[128,768]{1,0:T(8,128)(2,1)S(1)}, bf16[128,768]{1,0:T(8,128)(2,1)S(1)}, u32[]{:S(2)}, u32[]{:S(2)}) collective-permute-start(bf16[128,768]{1,0:T(8,128)(2,1)S(1)} %collective-permute-done.7.refs_3_), channel_id=1, source_target_pairs={{0,2},{1,3},{4,0},{5,1},{8,4},{9,5},{12,8},{13,9},{14,12},{15,13},... | collective-permute-start | bytes 589832 | tf_op jit(solution)/shard_map/ppermute | solution.py:274
  20.4 9.6 %collective-permute-start.8 = (bf16[136,768]{1,0:T(8,128)(2,1)S(1)}, bf16[136,768]{1,0:T(8,128)(2,1)S(1)}, u32[]{:S(2)}, u32[]{:S(2)}) collective-permute-start(bf16[136,768]{1,0:T(8,128)(2,1)S(1)} %collective-permute-done.4.refs_0_.refs_4_), channel_id=1, source_target_pairs={{0,4},{1,5},{4,8},{5,9},{8,12},{9,13},{12,14},{13,15},{14,10},{15,... | collective-permute-start | bytes 626696 | tf_op jit(solution)/shard_map/ppermute | solution.py:274
  22.6 9.4 %collective-permute-start.9 = (bf16[136,768]{1,0:T(8,128)(2,1)S(1)}, bf16[136,768]{1,0:T(8,128)(2,1)S(1)}, u32[]{:S(2)}, u32[]{:S(2)}) collective-permute-start(bf16[136,768]{1,0:T(8,128)(2,1)S(1)} %collective-permute-done.5.refs_1_.refs_5_), channel_id=1, source_target_pairs={{0,2},{1,3},{4,0},{5,1},{8,4},{9,5},{12,8},{13,9},{14,12},{15,13},... | collective-permute-start | bytes 626696 | tf_op jit(solution)/shard_map/ppermute | solution.py:274
  27.5 7.8 %collective-permute-start.12 = (bf16[128,768]{1,0:T(8,128)(2,1)S(1)}, bf16[128,768]{1,0:T(8,128)(2,1)S(1)}, u32[]{:S(2)}, u32[]{:S(2)}) collective-permute-start(bf16[128,768]{1,0:T(8,128)(2,1)S(1)} %collective-permute-done.10.refs_2_), channel_id=1, source_target_pairs={{0,4},{1,5},{4,8},{5,9},{8,12},{9,13},{12,14},{13,15},{14,10},{15,... | collective-permute-start | bytes 589832 | tf_op jit(solution)/shard_map/ppermute | solution.py:274
  29.1 7.8 %collective-permute-start.13 = (bf16[128,768]{1,0:T(8,128)(2,1)S(1)}, bf16[128,768]{1,0:T(8,128)(2,1)S(1)}, u32[]{:S(2)}, u32[]{:S(2)}) collective-permute-start(bf16[128,768]{1,0:T(8,128)(2,1)S(1)} %collective-permute-done.11.refs_3_), channel_id=1, source_target_pairs={{0,2},{1,3},{4,0},{5,1},{8,4},{9,5},{12,8},{13,9},{14,12},{15,13},... | collective-permute-start | bytes 589832 | tf_op jit(solution)/shard_map/ppermute | solution.py:274
  30.0 8.9 %collective-permute-start.14 = (bf16[136,768]{1,0:T(8,128)(2,1)S(1)}, bf16[136,768]{1,0:T(8,128)(2,1)S(1)}, u32[]{:S(2)}, u32[]{:S(2)}) collective-permute-start(bf16[136,768]{1,0:T(8,128)(2,1)S(1)} %collective-permute-done.8.refs_0_), channel_id=1, source_target_pairs={{0,4},{1,5},{4,8},{5,9},{8,12},{9,13},{12,14},{13,15},{14,10},{15,... | collective-permute-start | bytes 626696 | tf_op jit(solution)/shard_map/ppermute | solution.py:274
  32.0 7.4 %collective-permute-start.15 = (bf16[136,768]{1,0:T(8,128)(2,1)S(1)}, bf16[136,768]{1,0:T(8,128)(2,1)S(1)}, u32[]{:S(2)}, u32[]{:S(2)}) collective-permute-start(bf16[136,768]{1,0:T(8,128)(2,1)S(1)} %collective-permute-done.9.refs_1_), channel_id=1, source_target_pairs={{0,2},{1,3},{4,0},{5,1},{8,4},{9,5},{12,8},{13,9},{14,12},{15,13},... | collective-permute-start | bytes 626696 | tf_op jit(solution)/shard_map/ppermute | solution.py:274
  38.8 3.1 %collective-permute-start.16 = (f32[256,896]{1,0:T(8,128)S(1)}, f32[256,896]{1,0:T(8,128)S(1)}, u32[]{:S(2)}, u32[]{:S(2)}) collective-permute-start(f32[256,896]{1,0:T(8,128)S(1)} %get-tuple-element.53), channel_id=1, source_target_pairs={{0,1},{1,0},{2,3},{3,2},{4,5},{5,4},{6,7},{7,6},{8,9},{9,8},{10,11... | collective-permute-start | bytes 2752520 | tf_op jit(solution)/shard_map/ppermute | solution.py:274
  39.4 2.2 %collective-permute-start.17 = (bf16[136,768]{1,0:T(8,128)(2,1)S(1)}, bf16[136,768]{1,0:T(8,128)(2,1)S(1)}, u32[]{:S(2)}, u32[]{:S(2)}) collective-permute-start(bf16[136,768]{1,0:T(8,128)(2,1)S(1)} %collective-permute-done.14.refs_0_), channel_id=1, source_target_pairs={{0,1},{1,0},{2,3},{3,2},{4,5},{5,4},{6,7},{7,6},{8,9},{9,8},{10,11... | collective-permute-start | bytes 626696 | tf_op jit(solution)/shard_map/ppermute | solution.py:274
  39.4 2.5 %collective-permute-start.18 = (bf16[136,768]{1,0:T(8,128)(2,1)S(1)}, bf16[136,768]{1,0:T(8,128)(2,1)S(1)}, u32[]{:S(2)}, u32[]{:S(2)}) collective-permute-start(bf16[136,768]{1,0:T(8,128)(2,1)S(1)} %collective-permute-done.15.refs_1_), channel_id=1, source_target_pairs={{0,1},{1,0},{2,3},{3,2},{4,5},{5,4},{6,7},{7,6},{8,9},{9,8},{10,11... | collective-permute-start | bytes 626696 | tf_op jit(solution)/shard_map/ppermute | solution.py:274

commit v3 on v2

--- a/solution.py
+++ b/solution.py
@@ -14,6 +14,7 @@
 SPLIT = 128.0
 TAIL = 8
 VMEM_LIMIT = 16 * 1024 * 1024
+PARTS = 2
 WEIGHT = 20
 
 
@@ -51,36 +52,49 @@
     )
 
 
-def prep_body(emb_ref, pos_ref, a_ref, b_ref, ah_ref, bh_ref):
-    half = ah_ref.shape[0]
-    width = emb_ref.shape[1]
-    pos = pos_ref[...]
+def prep_body(parts, emb_hbm, pos_hbm, a_ref, b_ref, ah_ref, bh_ref, emb_ref, pos_ref, sem):
+    half = pos_ref.shape[1]
+    rows, width = emb_ref.shape
+    size = rows // parts
+    fetch = []
+    for i in range(parts):
+        part = pl.ds(i * size, size)
+        fetch.append(pltpu.make_async_copy(emb_hbm.at[part], emb_ref.at[part], sem.at[i]))
+    last = pltpu.make_async_copy(pos_hbm, pos_ref, sem.at[parts])
+    for copy in (*fetch, last):
+        copy.start()
+    for i, copy in enumerate(fetch):
+        copy.wait()
+        first = i * size
+        whole, alone = (a_ref, ah_ref) if first < half else (b_ref, bh_ref)
+        emb = emb_ref[first : first + size, :]
+        unit = emb * lax.rsqrt(jnp.sum(emb * emb, axis=1, keepdims=True) + EPS)
+        unit = unit.astype(jnp.bfloat16)
+        for at in range(0, width, LANES):
+            panel = unit[:, at : at + LANES]
+            row = at // LANES * half + first % half
+            alone[row : row + size] = panel
+            whole[row : row + size] = panel
+    last.wait()
+    pos = pos_ref[...].astype(jnp.float32)
     high = jnp.floor(pos * (1.0 / SPLIT))
     low = pos - high * SPLIT
-    row = jnp.concatenate(
-        [high[0:1], low[0:1], high[1:2], low[1:2], jnp.zeros((1, width - 4 * half), jnp.float32)],
-        axis=1,
-    )
-    tail = jnp.broadcast_to(row, (TAIL, width)).astype(jnp.bfloat16)
-    for i, whole, alone in ((0, a_ref, ah_ref), (1, b_ref, bh_ref)):
-        emb = emb_ref[i * half : (i + 1) * half, :]
-        unit = emb * lax.rsqrt(jnp.sum(emb * emb, axis=1, keepdims=True) + EPS)
-        unit = unit.astype(jnp.bfloat16)
-        alone[...] = unit
-        whole[...] = jnp.concatenate([unit, tail], axis=0)
+    tail = jnp.concatenate(
+        [high[0:1], low[0:1], high[1:2], low[1:2], jnp.zeros((TAIL - 4, half), jnp.float32)],
+        axis=0,
+    ).astype(jnp.bfloat16)
+    for ref in (a_ref, b_ref):
+        ref[width // LANES * half :] = tail
 
 
 def rows_of(ref, half):
-    return ref[...][:half]
+    panels = ref.shape[0] // half
+    return jnp.concatenate([ref[i * half : (i + 1) * half] for i in range(panels)], axis=1)
 
 
 def positions_of(ref, half):
-    tail = ref[...][half:].astype(jnp.float32)
-    return [
-        tail[0:1, 2 * i * half : (2 * i + 1) * half] * SPLIT
-        + tail[0:1, (2 * i + 1) * half : (2 * i + 2) * half]
-        for i in range(2)
-    ]
+    tail = ref[ref.shape[0] // half * half :].astype(jnp.float32)
+    return [tail[2 * i : 2 * i + 1] * SPLIT + tail[2 * i + 1 : 2 * i + 2] for i in range(2)]
 
 
 def column(row):
@@ -140,6 +154,17 @@
     return acc, top
 
 
+def column_parts(top):
+    rest = jnp.max(top, axis=1, keepdims=True)
+    lane = lax.broadcasted_iota(jnp.int32, top.shape, 1)
+    out = jnp.zeros(top.shape, jnp.float32)
+    for i in range(3):
+        part = rest.astype(jnp.bfloat16).astype(jnp.float32)
+        out = jnp.where(lane == i, part, out)
+        rest = rest - part
+    return out
+
+
 def fold(rows, width, state, out_ref, query, info, feat, blocks, ends, clusters, diagonal=False):
     acc, top = state[:, :width], state[:, width:]
     for i, (keys, pos) in enumerate(blocks):
@@ -147,12 +172,14 @@
             rows, query, info[0], info[1], feat, acc, top, keys, pos, ends, clusters,
             diagonal and i == 0,
         )
-    out_ref[:rows, :width] = acc
-    out_ref[:rows, width:] = top
+    if out_ref.dtype == jnp.bfloat16:
+        top = column_parts(top)
+    out_ref[:, :width] = acc.astype(out_ref.dtype)
+    out_ref[:, width:] = top.astype(out_ref.dtype)
 
 
 def first_body(half, clusters, len_ref, mask_hbm, a_ref, b_ref, sa_ref, sb_ref,
-               f_ref, g_ref, own_ref, sib_ref, info_ref, feat_ref, mask_ref, sem):
+               f_ref, g_ref, own_ref, sib_ref, info_ref, feat_ref, ends_ref, mask_ref, sem):
     fetch = pltpu.make_async_copy(mask_hbm, mask_ref, sem.at[0])
     fetch.start()
     ends = ends_of(len_ref, clusters)
@@ -162,7 +189,7 @@
     index, start = cluster_parts(pos, ends, clusters)
     count = mask_ref.shape[0]
     rows = 2 * half
-    width = a_ref.shape[1]
+    width = a_ref.shape[0] // half * LANES
     block = jnp.floor(pos * (1.0 / rows)).astype(jnp.int32)
     total = pos.shape[0]
     onehot = (block == lax.broadcasted_iota(jnp.int32, (total, count), 1)).astype(jnp.bfloat16)
@@ -188,6 +215,11 @@
         [jnp.zeros((rows, width), jnp.float32), jnp.full((rows, LANES), -1.0, jnp.float32)],
         axis=1,
     )
+    ends_ref[...] = jnp.concatenate(
+        [jnp.full((1, rows), e, jnp.float32) for e in ends]
+        + [jnp.zeros((ends_ref.shape[0] - len(ends), rows), jnp.float32)],
+        axis=0,
+    )
     fold(rows, width, state, own_ref, keys, info_ref[:, :rows], feat[:rows], blocks, ends,
          clusters, True)
     other = jnp.concatenate([rows_of(r, half) for r in (sa_ref, sb_ref)], axis=0)
@@ -206,11 +238,11 @@
     return out
 
 
-def middle_body(half, clusters, groups, len_ref, info_ref, feat_ref, a_ref, b_ref, sa_ref,
+def middle_body(half, clusters, groups, ends_ref, info_ref, feat_ref, a_ref, b_ref, sa_ref,
                 sb_ref, own_in, sib_in, *refs):
     key_refs, (own_ref, sib_ref) = refs[:-2], refs[-2:]
-    ends = ends_of(len_ref, clusters)
-    rows, width = 2 * half, a_ref.shape[1]
+    ends = [ends_ref[c : c + 1, :] for c in range(clusters - 1)]
+    rows, width = 2 * half, a_ref.shape[0] // half * LANES
     blocks = gather_keys(key_refs, groups, half)
     for i, state_in, state_out, pair in (
         (0, own_in, own_ref, (a_ref, b_ref)), (1, sib_in, sib_ref, (sa_ref, sb_ref))
@@ -221,24 +253,25 @@
              blocks, ends, clusters)
 
 
-def late_body(half, clusters, len_ref, info_ref, feat_ref, a_ref, b_ref, own_in, *refs):
+def late_body(half, clusters, ends_ref, info_ref, feat_ref, a_ref, b_ref, own_in, *refs):
     key_refs, own_ref = refs[:-1], refs[-1]
-    ends = ends_of(len_ref, clusters)
-    rows, width = 2 * half, a_ref.shape[1]
+    ends = [ends_ref[c : c + 1, :] for c in range(clusters - 1)]
+    rows, width = 2 * half, a_ref.shape[0] // half * LANES
     blocks = gather_keys(key_refs, (((0, 0, 0), (1, 1, 1)),), half)
     query = jnp.concatenate([rows_of(r, half) for r in (a_ref, b_ref)], axis=0)
     fold(rows, width, own_in[...], own_ref, query, info_ref[:, :rows], feat_ref[:rows],
          blocks, ends, clusters)
 
 
-def last_body(half, clusters, groups, len_ref, info_ref, feat_ref, a_ref, b_ref, own_in, got_ref,
+def last_body(half, clusters, groups, ends_ref, info_ref, feat_ref, a_ref, b_ref, own_in, got_ref,
               *refs):
     key_refs, (dir_ref, out_top) = refs[:-2], refs[-2:]
-    ends = ends_of(len_ref, clusters)
-    rows, width = 2 * half, a_ref.shape[1]
+    ends = [ends_ref[c : c + 1, :] for c in range(clusters - 1)]
+    rows, width = 2 * half, a_ref.shape[0] // half * LANES
     query = jnp.concatenate([rows_of(r, half) for r in (a_ref, b_ref)], axis=0)
-    acc = own_in[:, :width] + got_ref[:, :width]
-    top = jnp.maximum(own_in[:, width:], got_ref[:, width:])
+    acc = own_in[:, :width] + got_ref[:, :width].astype(jnp.float32)
+    parts = got_ref[:, width:].astype(jnp.float32)
+    top = jnp.maximum(own_in[:, width:], jnp.sum(parts, axis=1, keepdims=True))
     for keys, pos in gather_keys(key_refs, groups, half):
         acc, top = attend(
             rows, query, info_ref[0, :rows], info_ref[1, :rows], feat_ref[:rows], acc, top, keys,
@@ -257,6 +290,10 @@
     out_top[...] = jnp.concatenate(lines, axis=0)
 
 
+def in_hbm(x):
+    return pltpu.with_memory_space_constraint(x, pltpu.HBM)
+
+
 def after(x, *before):
     return lax.optimization_barrier((x, *before))[0]
 
@@ -279,34 +316,40 @@
     def f32(*s):
         return jax.ShapeDtypeStruct(s, jnp.float32)
 
-    full = half + TAIL
+    full = width // LANES * half + TAIL
     wide = width + LANES
     state = f32(rows, wide)
     a, b, ah, bh = call(
-        prep_body, [bf(full), bf(full), bf(half), bf(half)], [VM, VM],
-    )(embeddings, dest_pos.reshape(2, half).astype(jnp.float32))
+        functools.partial(prep_body, PARTS),
+        [bf(full, LANES)] * 2 + [bf(full - TAIL, LANES)] * 2, [HB, HB],
+        scratch=[
+            pltpu.VMEM((rows, width), jnp.float32), pltpu.VMEM((2, half), jnp.int32),
+            pltpu.SemaphoreType.DMA((PARTS + 1,)),
+        ],
+    )(in_hbm(embeddings), in_hbm(dest_pos.reshape(2, half)))
 
     lead = [(move(a, ahead), move(b, back))]
     follow = [(move(bh, ahead), move(ah, back))]
     sa, sb = move(a, sibling), move(b, sibling)
     work = 8 * rows * rows * width * WEIGHT
-    own, sib, info, feat = call(
+    own, sib, info, feat, ends = call(
         functools.partial(first_body, half, clusters),
-        [state, state, f32(2, 2 * rows, LANES), bf(2 * rows, count * clusters)],
+        [state, state, f32(2, 2 * rows, LANES), bf(2 * rows, count * clusters),
+         f32(-(-clusters // 8) * 8, rows)],
         [SM, HB] + [VM] * 6, work,
         scratch=[pltpu.VMEM(block_mask.shape, jnp.int32), pltpu.SemaphoreType.DMA((1,))],
     )(cluster_lengths, block_mask, a, b, sa, sb, *lead[0])
 
-    def middle(own, sib, keys, groups, work):
+    def middle(own, sib, keys, groups, work, sent=state):
         return call(
-            functools.partial(middle_body, half, clusters, groups), [state, state],
-            [SM] + [VM] * (8 + len(keys)), work, aliases={7: 0, 8: 1},
-        )(cluster_lengths, info, feat, a, b, sa, sb, own, sib, *keys)
+            functools.partial(middle_body, half, clusters, groups), [state, sent],
+            [VM] * (9 + len(keys)), work, aliases={7: 0, 8: 1} if sent is state else {7: 0},
+        )(ends, info, feat, a, b, sa, sb, own, sib, *keys)
 
     both = ((0, 0, 0), (1, 1, 1))
     for step in range(1, steps):
         f, g = lead[-1]
-        lead.append((move(after(f, sa), ahead), move(after(g, sb), back)))
+        lead.append((move(f, ahead), move(g, back)))
         if step > 1:
             own, sib = middle(
                 own, sib, (*lead[-2], *follow[-2], *lead[-3]), (((2, 4, 1), (3, 5, 0)), both),
@@ -315,16 +358,17 @@
         if step < steps - 1:
             f, g = follow[-1]
             follow.append((move(after(f, own), ahead), move(after(g, own), back)))
-    own, sib = middle(own, sib, (*lead[-2], *follow[-1]), (((2, 0, 1), (3, 1, 0)),), 1)
+    own, sib = middle(own, sib, (*lead[-2], *follow[-1]), (((2, 0, 1), (3, 1, 0)),), 1,
+                      bf(rows, wide))
     got = move(sib, sibling)
     far = [move(after(x, own), sibling) for x in lead[-1]]
-    shared = (cluster_lengths, info, feat, a, b)
+    shared = (ends, info, feat, a, b)
     own = call(
-        functools.partial(late_body, half, clusters), [state], [SM] + [VM] * 7, work, aliases={5: 0},
+        functools.partial(late_body, half, clusters), [state], [VM] * 8, work, aliases={5: 0},
     )(*shared, own, *lead[-1])[0]
     out_dir, out_top = call(
         functools.partial(last_body, half, clusters, (both,)),
-        [bf(rows), f32(2, half)], [SM] + [VM] * 8,
+        [bf(rows), f32(2, half)], [VM] * 9,
     )(*shared, own, got, *far)
     return out_top.reshape(rows), out_dir
 

time: 44.2 us -> 40.9 us (0.925)
  Pallas kernels: 12.7 us -> 11 us
  waiting for transfers between devices: 11.7 us -> 13 us
  local copies, waits for them, and re-layouts: 1.14 us -> 0.01 us
  starting transfers between devices: 17.1 us -> 16.1 us
  other arithmetic: 0.68 us -> 0 us
    ppermute x19, waiting for transfers between devices: 11.7 us -> 13 us  [move(): return lax.ppermute(x, 'blk', perm)]
    unnamed x6 -> x4, local copies, waits for them, and re-layouts: 1.14 us -> 0.01 us
    pallas_call x5, Pallas kernels: 7.81 us -> 6.72 us  [the longest x3 4.72 us: middle(): call(functools.partial(middle_body, half, clusters, groups), [state, sent...]
    ppermute x19, starting transfers between devices: 17.1 us -> 16.1 us  [move(): return lax.ppermute(x, 'blk', perm)]
    convert_element_type x1 -> x0, other arithmetic: 0.68 us -> none  [per_device(): dest_pos.reshape(2, half).astype(jnp.float32)]
    pallas_call x1, Pallas kernels: 2.09 us -> 1.54 us  [per_device(): call(functools.partial(last_body, half, clusters, (both,)), [bf(rows), f3...]
  transfers between devices with their start and end apart: 19 -> 19, of which waited for: 13 -> 11; matrix products, arithmetic and copies ran while one was open for 0% -> 0% of each run, Pallas kernels for 24% -> 20%
where the time goes in v3:
time: 40.9 us; the launch traced here: 40.8 us
  starting transfers between devices  16.1 us (39%)
  waiting for transfers between devices  13 us (32%)
  Pallas kernels  11 us (27%)
  between operations  0.73 us (2%)
    ppermute x19, starting transfers between devices, move(): return lax.ppermute(x, 'blk', perm)  16.1 us
    ppermute x19, waiting for transfers between devices, move(): return lax.ppermute(x, 'blk', perm)  13 us
    pallas_call x3, Pallas kernels, middle(): call(functools.partial(middle_body, half, clusters, groups), [state, sent...  4.72 us
    pallas_call x1, Pallas kernels, per_device(): call(functools.partial(first_body, half, clusters), [state, state, f32(2,...  2.76 us
    pallas_call x1, Pallas kernels, per_device(): call(functools.partial(last_body, half, clusters, (both,)), [bf(rows), f3...  1.54 us
    pallas_call x1, Pallas kernels, per_device(): call(functools.partial(prep_body, PARTS), [bf(full, LANES)] * 2 + [bf(ful...  1.28 us
  transfers between devices with their start and end apart: 19, of which 11 were waited for; matrix products, arithmetic and copies ran while one was open for 0% of the time, Pallas kernels for 20%

profile of v3, /device:TPU:0, one launch (start us, length us, event | category | flops | bytes accessed | tf_op | source)
XLA Modules:
  0.0 40.8 jit_solution(14340731104579720224)
XLA Ops:
  0.6 1.3 %shard_map.59 = (bf16[776,128]{1,0:T(8,128)(2,1)S(1)}, bf16[776,128]{1,0:T(8,128)(2,1)S(1)}, bf16[768,128]{1,0:T(8,128)(2,1)S(1)}, bf16[768,128]{1,0:T(8,128)(2,1)S(1)}) custom-call(f32[256,768]{1,0:T(8,128)} %emb_hbm.1, s32[2,128]{1,0:T(2,128)} %bitcast.2), custom_call_target="tpu_custom_call" | custom-call | flops 1 | bytes 1 | tf_op jit(solution)/shard_map/pallas_call | solution.py:322
  1.9 0.5 %collective-permute-start = (bf16[776,128]{1,0:T(8,128)(2,1)S(1)}, bf16[776,128]{1,0:T(8,128)(2,1)S(1)}, u32[]{:S(2)}, u32[]{:S(2)}) collective-permute-start(bf16[776,128]{1,0:T(8,128)(2,1)S(1)} %get-tuple-element.25.a_ref), channel_id=1, source_target_pairs={{0,1},{1,0},{2,3},{3,2},{4,5},{5,4},{6,7},{7,6},{8,9},{9,8},{10,11... | collective-permute-start | bytes 595976 | tf_op jit(solution)/shard_map/ppermute | solution.py:311
  2.4 2.6 %collective-permute-start.2 = (bf16[776,128]{1,0:T(8,128)(2,1)S(1)}, bf16[776,128]{1,0:T(8,128)(2,1)S(1)}, u32[]{:S(2)}, u32[]{:S(2)}) collective-permute-start(bf16[776,128]{1,0:T(8,128)(2,1)S(1)} %get-tuple-element.25.a_ref), channel_id=1, source_target_pairs={{0,4},{1,5},{4,8},{5,9},{8,12},{9,13},{12,14},{13,15},{14,10},{15,... | collective-permute-start | bytes 595976 | tf_op jit(solution)/shard_map/ppermute | solution.py:311
  5.1 0.1 collective-permute-start.1
  5.3 1.8 %collective-permute-start.7 = (bf16[768,128]{1,0:T(8,128)(2,1)S(1)}, bf16[768,128]{1,0:T(8,128)(2,1)S(1)}, u32[]{:S(2)}, u32[]{:S(2)}) collective-permute-start(bf16[768,128]{1,0:T(8,128)(2,1)S(1)} %get-tuple-element.33), channel_id=1, source_target_pairs={{0,2},{1,3},{4,0},{5,1},{8,4},{9,5},{12,8},{13,9},{14,12},{15,13},... | collective-permute-start | bytes 589832 | tf_op jit(solution)/shard_map/ppermute | solution.py:311
  7.1 0.3 collective-permute-start.6
  7.3 3.5 %collective-permute-done.2.f_ref.refs_4_ = bf16[776,128]{1,0:T(8,128)(2,1)S(1)} collective-permute-done((bf16[776,128]{1,0:T(8,128)(2,1)S(1)}, bf16[776,128]{1,0:T(8,128)(2,1)S(1)}, u32[]{:S(2)}, u32[]{:S(2)}) %collective-permute-start.2) | collective-permute-done | bytes 198688 | tf_op jit(solution)/shard_map/ppermute | solution.py:311
  10.8 2.0 %collective-permute-start.4 = (bf16[776,128]{1,0:T(8,128)(2,1)S(1)}, bf16[776,128]{1,0:T(8,128)(2,1)S(1)}, u32[]{:S(2)}, u32[]{:S(2)}) collective-permute-start(bf16[776,128]{1,0:T(8,128)(2,1)S(1)} %collective-permute-done.2.f_ref.refs_4_), channel_id=1, source_target_pairs={{0,4},{1,5},{4,8},{5,9},{8,12},{9,13},{12,14},{13,15},{14,10},{15,... | collective-permute-start | bytes 595976 | tf_op jit(solution)/shard_map/ppermute | solution.py:311
  12.9 2.8 %shard_map.60 = (f32[256,896]{1,0:T(8,128)S(1)}, f32[256,896]{1,0:T(8,128)S(1)}, f32[2,512,128]{2,1,0:T(8,128)S(1)}, bf16[512,64]{1,0:T(8,128)(2,1)S(1)}, f32[8,256]{1,0:T(8,128)S(1)}) custom-call(s32[4]{0:T(128)S(1)} %copy-done.1, s32[16,16]{1,0:T(8,128)S(1)} %copy-done, bf16[776,128]{1,0:T(8,128)(2,1)S(1)} %get-tuple-element.25.a_ref, ...), custom_call_target="tpu_custom_call" | custom-call | flops 8053063680 | bytes 1 | tf_op jit(solution)/shard_map/pallas_call | solution.py:335
  15.7 1.4 %collective-permute-done.7.refs_3_ = bf16[768,128]{1,0:T(8,128)(2,1)S(1)} collective-permute-done((bf16[768,128]{1,0:T(8,128)(2,1)S(1)}, bf16[768,128]{1,0:T(8,128)(2,1)S(1)}, u32[]{:S(2)}, u32[]{:S(2)}) %collective-permute-start.7) | collective-permute-done | bytes 196640 | tf_op jit(solution)/shard_map/ppermute | solution.py:311
  17.1 1.6 %collective-permute-start.10 = (bf16[768,128]{1,0:T(8,128)(2,1)S(1)}, bf16[768,128]{1,0:T(8,128)(2,1)S(1)}, u32[]{:S(2)}, u32[]{:S(2)}) collective-permute-start(bf16[768,128]{1,0:T(8,128)(2,1)S(1)} %collective-permute-done.6.refs_2_), channel_id=1, source_target_pairs={{0,4},{1,5},{4,8},{5,9},{8,12},{9,13},{12,14},{13,15},{14,10},{15,... | collective-permute-start | bytes 589832 | tf_op jit(solution)/shard_map/ppermute | solution.py:311
  18.7 0.4 %collective-permute-start.11 = (bf16[768,128]{1,0:T(8,128)(2,1)S(1)}, bf16[768,128]{1,0:T(8,128)(2,1)S(1)}, u32[]{:S(2)}, u32[]{:S(2)}) collective-permute-start(bf16[768,128]{1,0:T(8,128)(2,1)S(1)} %collective-permute-done.7.refs_3_), channel_id=1, source_target_pairs={{0,2},{1,3},{4,0},{5,1},{8,4},{9,5},{12,8},{13,9},{14,12},{15,13},... | collective-permute-start | bytes 589832 | tf_op jit(solution)/shard_map/ppermute | solution.py:311
  19.1 0.2 collective-permute-done.4.refs_0_.refs_4_
  19.3 2.0 %collective-permute-start.8 = (bf16[776,128]{1,0:T(8,128)(2,1)S(1)}, bf16[776,128]{1,0:T(8,128)(2,1)S(1)}, u32[]{:S(2)}, u32[]{:S(2)}) collective-permute-start(bf16[776,128]{1,0:T(8,128)(2,1)S(1)} %collective-permute-done.4.refs_0_.refs_4_), channel_id=1, source_target_pairs={{0,4},{1,5},{4,8},{5,9},{8,12},{9,13},{12,14},{13,15},{14,10},{15,... | collective-permute-start | bytes 595976 | tf_op jit(solution)/shard_map/ppermute | solution.py:311
  21.3 1.7 %shard_map.61 = (f32[256,896]{1,0:T(8,128)S(1)}, f32[256,896]{1,0:T(8,128)S(1)}) custom-call(f32[8,256]{1,0:T(8,128)S(1)} %get-tuple-element.27.ends_ref, f32[2,512,128]{2,1,0:T(8,128)S(1)} %get-tuple-element.28.info_ref, bf16[512,64]{1,0:T(8,128)(2,1)S(1)} %get-tuple-element.29.feat_ref, ...), custom_call_target="tpu_custom_call", output_to_operand_aliasing={{0}: (7, {}), {1}: (8, {})} | custom-call | flops 8053063680 | bytes 1 | tf_op jit(solution)/shard_map/pallas_call | solution.py:344
  23.1 1.8 %collective-permute-done.10.refs_2_ = bf16[768,128]{1,0:T(8,128)(2,1)S(1)} collective-permute-done((bf16[768,128]{1,0:T(8,128)(2,1)S(1)}, bf16[768,128]{1,0:T(8,128)(2,1)S(1)}, u32[]{:S(2)}, u32[]{:S(2)}) %collective-permute-start.10) | collective-permute-done | bytes 196640 | tf_op jit(solution)/shard_map/ppermute | solution.py:311
  24.9 1.6 %collective-permute-done.11.refs_3_ = bf16[768,128]{1,0:T(8,128)(2,1)S(1)} collective-permute-done((bf16[768,128]{1,0:T(8,128)(2,1)S(1)}, bf16[768,128]{1,0:T(8,128)(2,1)S(1)}, u32[]{:S(2)}, u32[]{:S(2)}) %collective-permute-start.11) | collective-permute-done | bytes 196640 | tf_op jit(solution)/shard_map/ppermute | solution.py:311
  26.5 1.6 %collective-permute-start.12 = (bf16[768,128]{1,0:T(8,128)(2,1)S(1)}, bf16[768,128]{1,0:T(8,128)(2,1)S(1)}, u32[]{:S(2)}, u32[]{:S(2)}) collective-permute-start(bf16[768,128]{1,0:T(8,128)(2,1)S(1)} %collective-permute-done.10.refs_2_), channel_id=1, source_target_pairs={{0,4},{1,5},{4,8},{5,9},{8,12},{9,13},{12,14},{13,15},{14,10},{15,... | collective-permute-start | bytes 589832 | tf_op jit(solution)/shard_map/ppermute | solution.py:311
  28.1 0.4 %collective-permute-start.13 = (bf16[768,128]{1,0:T(8,128)(2,1)S(1)}, bf16[768,128]{1,0:T(8,128)(2,1)S(1)}, u32[]{:S(2)}, u32[]{:S(2)}) collective-permute-start(bf16[768,128]{1,0:T(8,128)(2,1)S(1)} %collective-permute-done.11.refs_3_), channel_id=1, source_target_pairs={{0,2},{1,3},{4,0},{5,1},{8,4},{9,5},{12,8},{13,9},{14,12},{15,13},... | collective-permute-start | bytes 589832 | tf_op jit(solution)/shard_map/ppermute | solution.py:311
  28.5 0.7 %collective-permute-done.8.refs_0_ = bf16[776,128]{1,0:T(8,128)(2,1)S(1)} collective-permute-done((bf16[776,128]{1,0:T(8,128)(2,1)S(1)}, bf16[776,128]{1,0:T(8,128)(2,1)S(1)}, u32[]{:S(2)}, u32[]{:S(2)}) %collective-permute-start.8) | collective-permute-done | bytes 198688 | tf_op jit(solution)/shard_map/ppermute | solution.py:311
  29.2 1.6 %collective-permute-start.14 = (bf16[776,128]{1,0:T(8,128)(2,1)S(1)}, bf16[776,128]{1,0:T(8,128)(2,1)S(1)}, u32[]{:S(2)}, u32[]{:S(2)}) collective-permute-start(bf16[776,128]{1,0:T(8,128)(2,1)S(1)} %collective-permute-done.8.refs_0_), channel_id=1, source_target_pairs={{0,4},{1,5},{4,8},{5,9},{8,12},{9,13},{12,14},{13,15},{14,10},{15,... | collective-permute-start | bytes 595976 | tf_op jit(solution)/shard_map/ppermute | solution.py:311
  30.8 0.5 %collective-permute-start.15 = (bf16[776,128]{1,0:T(8,128)(2,1)S(1)}, bf16[776,128]{1,0:T(8,128)(2,1)S(1)}, u32[]{:S(2)}, u32[]{:S(2)}) collective-permute-start(bf16[776,128]{1,0:T(8,128)(2,1)S(1)} %collective-permute-done.9.refs_1_), channel_id=1, source_target_pairs={{0,2},{1,3},{4,0},{5,1},{8,4},{9,5},{12,8},{13,9},{14,12},{15,13},... | collective-permute-start | bytes 595976 | tf_op jit(solution)/shard_map/ppermute | solution.py:311
  31.2 1.8 %shard_map.62 = (f32[256,896]{1,0:T(8,128)S(1)}, f32[256,896]{1,0:T(8,128)S(1)}) custom-call(f32[8,256]{1,0:T(8,128)S(1)} %get-tuple-element.27.ends_ref, f32[2,512,128]{2,1,0:T(8,128)S(1)} %get-tuple-element.28.info_ref, bf16[512,64]{1,0:T(8,128)(2,1)S(1)} %get-tuple-element.29.feat_ref, ...), custom_call_target="tpu_custom_call", output_to_operand_aliasing={{0}: (7, {}), {1}: (8, {})} | custom-call | flops 8053063680 | bytes 1 | tf_op jit(solution)/shard_map/pallas_call | solution.py:344
  33.0 1.0 %collective-permute-done.12.refs_2_ = bf16[768,128]{1,0:T(8,128)(2,1)S(1)} collective-permute-done((bf16[768,128]{1,0:T(8,128)(2,1)S(1)}, bf16[768,128]{1,0:T(8,128)(2,1)S(1)}, u32[]{:S(2)}, u32[]{:S(2)}) %collective-permute-start.12) | collective-permute-done | bytes 196640 | tf_op jit(solution)/shard_map/ppermute | solution.py:311
  33.9 1.5 %collective-permute-done.13.refs_3_ = bf16[768,128]{1,0:T(8,128)(2,1)S(1)} collective-permute-done((bf16[768,128]{1,0:T(8,128)(2,1)S(1)}, bf16[768,128]{1,0:T(8,128)(2,1)S(1)}, u32[]{:S(2)}, u32[]{:S(2)}) %collective-permute-start.13) | collective-permute-done | bytes 196640 | tf_op jit(solution)/shard_map/ppermute | solution.py:311
  35.4 1.2 %shard_map.63 = (f32[256,896]{1,0:T(8,128)S(1)}, bf16[256,896]{1,0:T(8,128)(2,1)S(1)}) custom-call(f32[8,256]{1,0:T(8,128)S(1)} %get-tuple-element.27.ends_ref, f32[2,512,128]{2,1,0:T(8,128)S(1)} %get-tuple-element.28.info_ref, bf16[512,64]{1,0:T(8,128)(2,1)S(1)} %get-tuple-element.29.feat_ref, ...), custom_call_target="tpu_custom_call", output_to_operand_aliasing={{0}: (7, {})} | custom-call | flops 1 | bytes 1 | tf_op jit(solution)/shard_map/pallas_call | solution.py:344
  36.7 0.8 %collective-permute-done.15.refs_1_ = bf16[776,128]{1,0:T(8,128)(2,1)S(1)} collective-permute-done((bf16[776,128]{1,0:T(8,128)(2,1)S(1)}, bf16[776,128]{1,0:T(8,128)(2,1)S(1)}, u32[]{:S(2)}, u32[]{:S(2)}) %collective-permute-start.15) | collective-permute-done | bytes 198688 | tf_op jit(solution)/shard_map/ppermute | solution.py:311
  37.5 0.5 %collective-permute-start.18 = (bf16[776,128]{1,0:T(8,128)(2,1)S(1)}, bf16[776,128]{1,0:T(8,128)(2,1)S(1)}, u32[]{:S(2)}, u32[]{:S(2)}) collective-permute-start(bf16[776,128]{1,0:T(8,128)(2,1)S(1)} %collective-permute-done.15.refs_1_), channel_id=1, source_target_pairs={{0,1},{1,0},{2,3},{3,2},{4,5},{5,4},{6,7},{7,6},{8,9},{9,8},{10,11... | collective-permute-start | bytes 595976 | tf_op jit(solution)/shard_map/ppermute | solution.py:311
  38.0 0.7 %shard_map.64.own_in = f32[256,896]{1,0:T(8,128)S(1)} custom-call(f32[8,256]{1,0:T(8,128)S(1)} %get-tuple-element.27.ends_ref, f32[2,512,128]{2,1,0:T(8,128)S(1)} %get-tuple-element.28.info_ref, bf16[512,64]{1,0:T(8,128)(2,1)S(1)} %get-tuple-element.29.feat_ref, bf16[776,128]{1,0:T(8,128)(2,1)S(1)} %get-tuple-element.25.a_ref, ...), custom_call_target="tpu_custom_call", output_to_operand_aliasing={{}: (5, {})} | custom-call | flops 8053063680 | bytes 1 | tf_op jit(solution)/shard_map/pallas_call | solution.py:366
  38.7 0.2 collective-permute-done.17.refs_0_
  39.0 0.3 collective-permute-done.18.refs_1_
  39.2 1.5 %shard_map.65 = (bf16[256,768]{1,0:T(8,128)(2,1)}, f32[2,128]{1,0:T(2,128)}) custom-call(f32[8,256]{1,0:T(8,128)S(1)} %get-tuple-element.27.ends_ref, f32[2,512,128]{2,1,0:T(8,128)S(1)} %get-tuple-element.28.info_ref, bf16[512,64]{1,0:T(8,128)(2,1)S(1)} %get-tuple-element.29.feat_ref, bf16[776,128]{1,0:T(8,128)(2,1)S(1)} %get-tuple-element.25.a_ref, ...), custom_call_target="tpu_custom_call" | custom-call | flops 1 | bytes 1 | tf_op jit(solution)/shard_map/pallas_call | solution.py:369
  (17 shorter events, 0.2 us)
Async XLA Ops:
  0.6 12.3 %copy-start = (s32[16,16]{1,0:T(8,128)S(1)}, s32[16,16]{1,0:T(8,128)}, u32[]{:S(2)}) copy-start(s32[16,16]{1,0:T(8,128)} %mask_hbm.1) | copy-start | bytes 3076
  1.9 5.1 %collective-permute-start = (bf16[776,128]{1,0:T(8,128)(2,1)S(1)}, bf16[776,128]{1,0:T(8,128)(2,1)S(1)}, u32[]{:S(2)}, u32[]{:S(2)}) collective-permute-start(bf16[776,128]{1,0:T(8,128)(2,1)S(1)} %get-tuple-element.25.a_ref), channel_id=1, source_target_pairs={{0,1},{1,0},{2,3},{3,2},{4,5},{5,4},{6,7},{7,6},{8,9},{9,8},{10,11... | collective-permute-start | bytes 595976 | tf_op jit(solution)/shard_map/ppermute | solution.py:311
  2.4 8.4 %collective-permute-start.2 = (bf16[776,128]{1,0:T(8,128)(2,1)S(1)}, bf16[776,128]{1,0:T(8,128)(2,1)S(1)}, u32[]{:S(2)}, u32[]{:S(2)}) collective-permute-start(bf16[776,128]{1,0:T(8,128)(2,1)S(1)} %get-tuple-element.25.a_ref), channel_id=1, source_target_pairs={{0,4},{1,5},{4,8},{5,9},{8,12},{9,13},{12,14},{13,15},{14,10},{15,... | collective-permute-start | bytes 595976 | tf_op jit(solution)/shard_map/ppermute | solution.py:311
  5.1 7.8 %collective-permute-start.3 = (bf16[776,128]{1,0:T(8,128)(2,1)S(1)}, bf16[776,128]{1,0:T(8,128)(2,1)S(1)}, u32[]{:S(2)}, u32[]{:S(2)}) collective-permute-start(bf16[776,128]{1,0:T(8,128)(2,1)S(1)} %get-tuple-element.26.b_ref), channel_id=1, source_target_pairs={{0,2},{1,3},{4,0},{5,1},{8,4},{9,5},{12,8},{13,9},{14,12},{15,13},... | collective-permute-start | bytes 595976 | tf_op jit(solution)/shard_map/ppermute | solution.py:311
  5.1 7.8 %collective-permute-start.1 = (bf16[776,128]{1,0:T(8,128)(2,1)S(1)}, bf16[776,128]{1,0:T(8,128)(2,1)S(1)}, u32[]{:S(2)}, u32[]{:S(2)}) collective-permute-start(bf16[776,128]{1,0:T(8,128)(2,1)S(1)} %get-tuple-element.26.b_ref), channel_id=1, source_target_pairs={{0,1},{1,0},{2,3},{3,2},{4,5},{5,4},{6,7},{7,6},{8,9},{9,8},{10,11... | collective-permute-start | bytes 595976 | tf_op jit(solution)/shard_map/ppermute | solution.py:311
  5.3 7.6 %copy-start.1 = (s32[4]{0:T(128)S(1)}, s32[4]{0:T(128)}, u32[]{:S(2)}) copy-start(s32[4]{0:T(128)} %len_ref.1) | copy-start | bytes 52
  5.3 11.8 %collective-permute-start.7 = (bf16[768,128]{1,0:T(8,128)(2,1)S(1)}, bf16[768,128]{1,0:T(8,128)(2,1)S(1)}, u32[]{:S(2)}, u32[]{:S(2)}) collective-permute-start(bf16[768,128]{1,0:T(8,128)(2,1)S(1)} %get-tuple-element.33), channel_id=1, source_target_pairs={{0,2},{1,3},{4,0},{5,1},{8,4},{9,5},{12,8},{13,9},{14,12},{15,13},... | collective-permute-start | bytes 589832 | tf_op jit(solution)/shard_map/ppermute | solution.py:311
  7.1 10.0 %collective-permute-start.6 = (bf16[768,128]{1,0:T(8,128)(2,1)S(1)}, bf16[768,128]{1,0:T(8,128)(2,1)S(1)}, u32[]{:S(2)}, u32[]{:S(2)}) collective-permute-start(bf16[768,128]{1,0:T(8,128)(2,1)S(1)} %get-tuple-element.32), channel_id=1, source_target_pairs={{0,4},{1,5},{4,8},{5,9},{8,12},{9,13},{12,14},{13,15},{14,10},{15,... | collective-permute-start | bytes 589832 | tf_op jit(solution)/shard_map/ppermute | solution.py:311
  10.8 8.5 %collective-permute-start.4 = (bf16[776,128]{1,0:T(8,128)(2,1)S(1)}, bf16[776,128]{1,0:T(8,128)(2,1)S(1)}, u32[]{:S(2)}, u32[]{:S(2)}) collective-permute-start(bf16[776,128]{1,0:T(8,128)(2,1)S(1)} %collective-permute-done.2.f_ref.refs_4_), channel_id=1, source_target_pairs={{0,4},{1,5},{4,8},{5,9},{8,12},{9,13},{12,14},{13,15},{14,10},{15,... | collective-permute-start | bytes 595976 | tf_op jit(solution)/shard_map/ppermute | solution.py:311
  12.9 8.5 %collective-permute-start.5 = (bf16[776,128]{1,0:T(8,128)(2,1)S(1)}, bf16[776,128]{1,0:T(8,128)(2,1)S(1)}, u32[]{:S(2)}, u32[]{:S(2)}) collective-permute-start(bf16[776,128]{1,0:T(8,128)(2,1)S(1)} %collective-permute-done.3.g_ref.refs_5_), channel_id=1, source_target_pairs={{0,2},{1,3},{4,0},{5,1},{8,4},{9,5},{12,8},{13,9},{14,12},{15,13},... | collective-permute-start | bytes 595976 | tf_op jit(solution)/shard_map/ppermute | solution.py:311
  17.1 7.8 %collective-permute-start.10 = (bf16[768,128]{1,0:T(8,128)(2,1)S(1)}, bf16[768,128]{1,0:T(8,128)(2,1)S(1)}, u32[]{:S(2)}, u32[]{:S(2)}) collective-permute-start(bf16[768,128]{1,0:T(8,128)(2,1)S(1)} %collective-permute-done.6.refs_2_), channel_id=1, source_target_pairs={{0,4},{1,5},{4,8},{5,9},{8,12},{9,13},{12,14},{13,15},{14,10},{15,... | collective-permute-start | bytes 589832 | tf_op jit(solution)/shard_map/ppermute | solution.py:311
  18.7 7.8 %collective-permute-start.11 = (bf16[768,128]{1,0:T(8,128)(2,1)S(1)}, bf16[768,128]{1,0:T(8,128)(2,1)S(1)}, u32[]{:S(2)}, u32[]{:S(2)}) collective-permute-start(bf16[768,128]{1,0:T(8,128)(2,1)S(1)} %collective-permute-done.7.refs_3_), channel_id=1, source_target_pairs={{0,2},{1,3},{4,0},{5,1},{8,4},{9,5},{12,8},{13,9},{14,12},{15,13},... | collective-permute-start | bytes 589832 | tf_op jit(solution)/shard_map/ppermute | solution.py:311
  19.3 9.9 %collective-permute-start.8 = (bf16[776,128]{1,0:T(8,128)(2,1)S(1)}, bf16[776,128]{1,0:T(8,128)(2,1)S(1)}, u32[]{:S(2)}, u32[]{:S(2)}) collective-permute-start(bf16[776,128]{1,0:T(8,128)(2,1)S(1)} %collective-permute-done.4.refs_0_.refs_4_), channel_id=1, source_target_pairs={{0,4},{1,5},{4,8},{5,9},{8,12},{9,13},{12,14},{13,15},{14,10},{15,... | collective-permute-start | bytes 595976 | tf_op jit(solution)/shard_map/ppermute | solution.py:311
  21.3 9.4 %collective-permute-start.9 = (bf16[776,128]{1,0:T(8,128)(2,1)S(1)}, bf16[776,128]{1,0:T(8,128)(2,1)S(1)}, u32[]{:S(2)}, u32[]{:S(2)}) collective-permute-start(bf16[776,128]{1,0:T(8,128)(2,1)S(1)} %collective-permute-done.5.refs_1_.refs_5_), channel_id=1, source_target_pairs={{0,2},{1,3},{4,0},{5,1},{8,4},{9,5},{12,8},{13,9},{14,12},{15,13},... | collective-permute-start | bytes 595976 | tf_op jit(solution)/shard_map/ppermute | solution.py:311
  26.5 7.4 %collective-permute-start.12 = (bf16[768,128]{1,0:T(8,128)(2,1)S(1)}, bf16[768,128]{1,0:T(8,128)(2,1)S(1)}, u32[]{:S(2)}, u32[]{:S(2)}) collective-permute-start(bf16[768,128]{1,0:T(8,128)(2,1)S(1)} %collective-permute-done.10.refs_2_), channel_id=1, source_target_pairs={{0,4},{1,5},{4,8},{5,9},{8,12},{9,13},{12,14},{13,15},{14,10},{15,... | collective-permute-start | bytes 589832 | tf_op jit(solution)/shard_map/ppermute | solution.py:311
  28.1 7.3 %collective-permute-start.13 = (bf16[768,128]{1,0:T(8,128)(2,1)S(1)}, bf16[768,128]{1,0:T(8,128)(2,1)S(1)}, u32[]{:S(2)}, u32[]{:S(2)}) collective-permute-start(bf16[768,128]{1,0:T(8,128)(2,1)S(1)} %collective-permute-done.11.refs_3_), channel_id=1, source_target_pairs={{0,2},{1,3},{4,0},{5,1},{8,4},{9,5},{12,8},{13,9},{14,12},{15,13},... | collective-permute-start | bytes 589832 | tf_op jit(solution)/shard_map/ppermute | solution.py:311
  29.2 7.5 %collective-permute-start.14 = (bf16[776,128]{1,0:T(8,128)(2,1)S(1)}, bf16[776,128]{1,0:T(8,128)(2,1)S(1)}, u32[]{:S(2)}, u32[]{:S(2)}) collective-permute-start(bf16[776,128]{1,0:T(8,128)(2,1)S(1)} %collective-permute-done.8.refs_0_), channel_id=1, source_target_pairs={{0,4},{1,5},{4,8},{5,9},{8,12},{9,13},{12,14},{13,15},{14,10},{15,... | collective-permute-start | bytes 595976 | tf_op jit(solution)/shard_map/ppermute | solution.py:311
  30.8 6.7 %collective-permute-start.15 = (bf16[776,128]{1,0:T(8,128)(2,1)S(1)}, bf16[776,128]{1,0:T(8,128)(2,1)S(1)}, u32[]{:S(2)}, u32[]{:S(2)}) collective-permute-start(bf16[776,128]{1,0:T(8,128)(2,1)S(1)} %collective-permute-done.9.refs_1_), channel_id=1, source_target_pairs={{0,2},{1,3},{4,0},{5,1},{8,4},{9,5},{12,8},{13,9},{14,12},{15,13},... | collective-permute-start | bytes 595976 | tf_op jit(solution)/shard_map/ppermute | solution.py:311
  36.6 2.6 %collective-permute-start.16 = (bf16[256,896]{1,0:T(8,128)(2,1)S(1)}, bf16[256,896]{1,0:T(8,128)(2,1)S(1)}, u32[]{:S(2)}, u32[]{:S(2)}) collective-permute-start(bf16[256,896]{1,0:T(8,128)(2,1)S(1)} %get-tuple-element.43), channel_id=1, source_target_pairs={{0,1},{1,0},{2,3},{3,2},{4,5},{5,4},{6,7},{7,6},{8,9},{9,8},{10,11... | collective-permute-start | bytes 1376264 | tf_op jit(solution)/shard_map/ppermute | solution.py:311
  37.5 1.4 %collective-permute-start.17 = (bf16[776,128]{1,0:T(8,128)(2,1)S(1)}, bf16[776,128]{1,0:T(8,128)(2,1)S(1)}, u32[]{:S(2)}, u32[]{:S(2)}) collective-permute-start(bf16[776,128]{1,0:T(8,128)(2,1)S(1)} %collective-permute-done.14.refs_0_), channel_id=1, source_target_pairs={{0,1},{1,0},{2,3},{3,2},{4,5},{5,4},{6,7},{7,6},{8,9},{9,8},{10,11... | collective-permute-start | bytes 595976 | tf_op jit(solution)/shard_map/ppermute | solution.py:311
  37.5 1.7 %collective-permute-start.18 = (bf16[776,128]{1,0:T(8,128)(2,1)S(1)}, bf16[776,128]{1,0:T(8,128)(2,1)S(1)}, u32[]{:S(2)}, u32[]{:S(2)}) collective-permute-start(bf16[776,128]{1,0:T(8,128)(2,1)S(1)} %collective-permute-done.15.refs_1_), channel_id=1, source_target_pairs={{0,1},{1,0},{2,3},{3,2},{4,5},{5,4},{6,7},{7,6},{8,9},{9,8},{10,11... | collective-permute-start | bytes 595976 | tf_op jit(solution)/shard_map/ppermute | solution.py:311

commit v4 on v3

--- a/solution.py
+++ b/solution.py
@@ -12,7 +12,7 @@
 TEMP = 4.0
 LANES = 128
 SPLIT = 128.0
-TAIL = 8
+TAIL = 16
 VMEM_LIMIT = 16 * 1024 * 1024
 PARTS = 2
 WEIGHT = 20
@@ -263,16 +263,25 @@
          blocks, ends, clusters)
 
 
-def last_body(half, clusters, groups, ends_ref, info_ref, feat_ref, a_ref, b_ref, own_in, got_ref,
-              *refs):
-    key_refs, (dir_ref, out_top) = refs[:-2], refs[-2:]
+def join_body(state_ref, f_ref, out_ref):
+    rows, wide = state_ref.shape
+    panels = wide // LANES
+    for i in range(panels):
+        out_ref[i * rows : (i + 1) * rows] = state_ref[:, i * LANES : (i + 1) * LANES]
+    out_ref[panels * rows : panels * rows + f_ref.shape[0]] = f_ref[...]
+
+
+def last_body(half, clusters, ends_ref, info_ref, feat_ref, a_ref, b_ref, own_in, got_ref,
+              far_ref, dir_ref, out_top):
     ends = [ends_ref[c : c + 1, :] for c in range(clusters - 1)]
     rows, width = 2 * half, a_ref.shape[0] // half * LANES
     query = jnp.concatenate([rows_of(r, half) for r in (a_ref, b_ref)], axis=0)
-    acc = own_in[:, :width] + got_ref[:, :width].astype(jnp.float32)
-    parts = got_ref[:, width:].astype(jnp.float32)
-    top = jnp.maximum(own_in[:, width:], jnp.sum(parts, axis=1, keepdims=True))
-    for keys, pos in gather_keys(key_refs, groups, half):
+    panels = width // LANES
+    parts = [got_ref[i * rows : (i + 1) * rows].astype(jnp.float32) for i in range(panels + 1)]
+    acc = own_in[:, :width] + jnp.concatenate(parts[:panels], axis=1)
+    top = jnp.maximum(own_in[:, width:], jnp.sum(parts[panels], axis=1, keepdims=True))
+    key_refs = [got_ref.at[pl.ds((panels + 1) * rows, a_ref.shape[0])], far_ref]
+    for keys, pos in gather_keys(key_refs, (((0, 0, 0), (1, 1, 1)),), half):
         acc, top = attend(
             rows, query, info_ref[0, :rows], info_ref[1, :rows], feat_ref[:rows], acc, top, keys,
             pos, ends, clusters, False,
@@ -304,7 +313,7 @@
     count = lax.axis_size("blk")
     clusters = cluster_lengths.shape[0]
     steps = count // 4
-    ahead, back = ring_perm(count, 1), ring_perm(count, -1)
+    ahead, back = ring_perm(count, -1), ring_perm(count, 1)
     sibling = [(i, i ^ 1) for i in range(count)]
 
     def move(x, perm):
@@ -360,16 +369,18 @@
             follow.append((move(after(f, own), ahead), move(after(g, own), back)))
     own, sib = middle(own, sib, (*lead[-2], *follow[-1]), (((2, 0, 1), (3, 1, 0)),), 1,
                       bf(rows, wide))
-    got = move(sib, sibling)
-    far = [move(after(x, own), sibling) for x in lead[-1]]
+    stacked = wide // LANES * rows + -(-full // 16) * 16
+    joined = call(join_body, [bf(stacked, LANES)], [VM, VM])(sib, lead[-1][0])[0]
+    got = move(joined, sibling)
+    far = move(after(lead[-1][1], own), sibling)
     shared = (ends, info, feat, a, b)
     own = call(
         functools.partial(late_body, half, clusters), [state], [VM] * 8, work, aliases={5: 0},
     )(*shared, own, *lead[-1])[0]
     out_dir, out_top = call(
-        functools.partial(last_body, half, clusters, (both,)),
-        [bf(rows), f32(2, half)], [VM] * 9,
-    )(*shared, own, got, *far)
+        functools.partial(last_body, half, clusters),
+        [bf(rows), f32(2, half)], [VM] * 8,
+    )(*shared, own, got, far)
     return out_top.reshape(rows), out_dir
 
 

time: 40.9 us -> 40.9 us (level)
  starting transfers between devices: 16.1 us -> 15.5 us
  waiting for transfers between devices: 13 us -> 13.5 us
    ppermute x19 -> x18, starting transfers between devices: 16.1 us -> 15.5 us  [move(): return lax.ppermute(x, 'blk', perm)]
    ppermute x19 -> x18, waiting for transfers between devices: 13 us -> 13.5 us  [move(): return lax.ppermute(x, 'blk', perm)]
    pallas_call x1 -> x2, Pallas kernels: 1.54 us -> 1.61 us  [the longest x1 1.51 us: per_device(): call(functools.partial(last_body, half, clusters), [bf(rows), f32(2, half...]
  transfers between devices with their start and end apart: 19 -> 18, of which waited for: 11 -> 10; matrix products, arithmetic and copies ran while one was open for 0% -> 0% of each run, Pallas kernels for 20% -> 20%
where the time goes in v4:
time: 40.9 us; the launch traced here: 40.8 us
  starting transfers between devices  15.5 us (38%)
  waiting for transfers between devices  13.5 us (33%)
  Pallas kernels  11.1 us (27%)
  between operations  0.73 us (2%)
    ppermute x18, starting transfers between devices, move(): return lax.ppermute(x, 'blk', perm)  15.5 us
    ppermute x18, waiting for transfers between devices, move(): return lax.ppermute(x, 'blk', perm)  13.5 us
    pallas_call x3, Pallas kernels, middle(): call(functools.partial(middle_body, half, clusters, groups), [state, sent...  4.71 us
    pallas_call x1, Pallas kernels, per_device(): call(functools.partial(first_body, half, clusters), [state, state, f32(2,...  2.77 us
    pallas_call x1, Pallas kernels, per_device(): call(functools.partial(last_body, half, clusters), [bf(rows), f32(2, half...  1.51 us
    pallas_call x1, Pallas kernels, per_device(): call(functools.partial(prep_body, PARTS), [bf(full, LANES)] * 2 + [bf(ful...  1.28 us
  transfers between devices with their start and end apart: 18, of which 10 were waited for; matrix products, arithmetic and copies ran while one was open for 0% of the time, Pallas kernels for 20%

profile of v4, /device:TPU:0, one launch (start us, length us, event | category | flops | bytes accessed | tf_op | source)
XLA Modules:
  0.0 40.8 jit_solution(15747182254019507216)
XLA Ops:
  0.6 1.3 %shard_map.59 = (bf16[784,128]{1,0:T(8,128)(2,1)S(1)}, bf16[784,128]{1,0:T(8,128)(2,1)S(1)}, bf16[768,128]{1,0:T(8,128)(2,1)S(1)}, bf16[768,128]{1,0:T(8,128)(2,1)S(1)}) custom-call(f32[256,768]{1,0:T(8,128)} %emb_hbm.1, s32[2,128]{1,0:T(2,128)} %bitcast.2), custom_call_target="tpu_custom_call" | custom-call | flops 1 | bytes 1 | tf_op jit(solution)/shard_map/pallas_call | solution.py:331
  1.9 0.5 %collective-permute-start = (bf16[784,128]{1,0:T(8,128)(2,1)S(1)}, bf16[784,128]{1,0:T(8,128)(2,1)S(1)}, u32[]{:S(2)}, u32[]{:S(2)}) collective-permute-start(bf16[784,128]{1,0:T(8,128)(2,1)S(1)} %get-tuple-element.24.a_ref), channel_id=1, source_target_pairs={{0,1},{1,0},{2,3},{3,2},{4,5},{5,4},{6,7},{7,6},{8,9},{9,8},{10,11... | collective-permute-start | bytes 602120 | tf_op jit(solution)/shard_map/ppermute | solution.py:320
  2.4 2.6 %collective-permute-start.2 = (bf16[784,128]{1,0:T(8,128)(2,1)S(1)}, bf16[784,128]{1,0:T(8,128)(2,1)S(1)}, u32[]{:S(2)}, u32[]{:S(2)}) collective-permute-start(bf16[784,128]{1,0:T(8,128)(2,1)S(1)} %get-tuple-element.24.a_ref), channel_id=1, source_target_pairs={{0,2},{1,3},{4,0},{5,1},{8,4},{9,5},{12,8},{13,9},{14,12},{15,13},... | collective-permute-start | bytes 602120 | tf_op jit(solution)/shard_map/ppermute | solution.py:320
  5.0 0.1 collective-permute-start.3
  5.3 1.9 %collective-permute-start.7 = (bf16[768,128]{1,0:T(8,128)(2,1)S(1)}, bf16[768,128]{1,0:T(8,128)(2,1)S(1)}, u32[]{:S(2)}, u32[]{:S(2)}) collective-permute-start(bf16[768,128]{1,0:T(8,128)(2,1)S(1)} %get-tuple-element.32), channel_id=1, source_target_pairs={{0,4},{1,5},{4,8},{5,9},{8,12},{9,13},{12,14},{13,15},{14,10},{15,... | collective-permute-start | bytes 589832 | tf_op jit(solution)/shard_map/ppermute | solution.py:320
  7.1 0.2 collective-permute-start.6
  7.3 3.6 %collective-permute-done.2.f_ref.refs_4_ = bf16[784,128]{1,0:T(8,128)(2,1)S(1)} collective-permute-done((bf16[784,128]{1,0:T(8,128)(2,1)S(1)}, bf16[784,128]{1,0:T(8,128)(2,1)S(1)}, u32[]{:S(2)}, u32[]{:S(2)}) %collective-permute-start.2) | collective-permute-done | bytes 200736 | tf_op jit(solution)/shard_map/ppermute | solution.py:320
  10.9 1.9 %collective-permute-start.4 = (bf16[784,128]{1,0:T(8,128)(2,1)S(1)}, bf16[784,128]{1,0:T(8,128)(2,1)S(1)}, u32[]{:S(2)}, u32[]{:S(2)}) collective-permute-start(bf16[784,128]{1,0:T(8,128)(2,1)S(1)} %collective-permute-done.2.f_ref.refs_4_), channel_id=1, source_target_pairs={{0,2},{1,3},{4,0},{5,1},{8,4},{9,5},{12,8},{13,9},{14,12},{15,13},... | collective-permute-start | bytes 602120 | tf_op jit(solution)/shard_map/ppermute | solution.py:320
  12.9 0.1 collective-permute-start.5
  13.0 2.8 %shard_map.60 = (f32[256,896]{1,0:T(8,128)S(1)}, f32[256,896]{1,0:T(8,128)S(1)}, f32[2,512,128]{2,1,0:T(8,128)S(1)}, bf16[512,64]{1,0:T(8,128)(2,1)S(1)}, f32[8,256]{1,0:T(8,128)S(1)}) custom-call(s32[4]{0:T(128)S(1)} %copy-done.1, s32[16,16]{1,0:T(8,128)S(1)} %copy-done, bf16[784,128]{1,0:T(8,128)(2,1)S(1)} %get-tuple-element.24.a_ref, ...), custom_call_target="tpu_custom_call" | custom-call | flops 8053063680 | bytes 1 | tf_op jit(solution)/shard_map/pallas_call | solution.py:344
  15.8 1.3 %collective-permute-done.7.refs_3_ = bf16[768,128]{1,0:T(8,128)(2,1)S(1)} collective-permute-done((bf16[768,128]{1,0:T(8,128)(2,1)S(1)}, bf16[768,128]{1,0:T(8,128)(2,1)S(1)}, u32[]{:S(2)}, u32[]{:S(2)}) %collective-permute-start.7) | collective-permute-done | bytes 196640 | tf_op jit(solution)/shard_map/ppermute | solution.py:320
  17.1 1.6 %collective-permute-start.10 = (bf16[768,128]{1,0:T(8,128)(2,1)S(1)}, bf16[768,128]{1,0:T(8,128)(2,1)S(1)}, u32[]{:S(2)}, u32[]{:S(2)}) collective-permute-start(bf16[768,128]{1,0:T(8,128)(2,1)S(1)} %collective-permute-done.6.refs_2_), channel_id=1, source_target_pairs={{0,2},{1,3},{4,0},{5,1},{8,4},{9,5},{12,8},{13,9},{14,12},{15,13},... | collective-permute-start | bytes 589832 | tf_op jit(solution)/shard_map/ppermute | solution.py:320
  18.7 0.4 %collective-permute-start.11 = (bf16[768,128]{1,0:T(8,128)(2,1)S(1)}, bf16[768,128]{1,0:T(8,128)(2,1)S(1)}, u32[]{:S(2)}, u32[]{:S(2)}) collective-permute-start(bf16[768,128]{1,0:T(8,128)(2,1)S(1)} %collective-permute-done.7.refs_3_), channel_id=1, source_target_pairs={{0,4},{1,5},{4,8},{5,9},{8,12},{9,13},{12,14},{13,15},{14,10},{15,... | collective-permute-start | bytes 589832 | tf_op jit(solution)/shard_map/ppermute | solution.py:320
  19.1 0.3 collective-permute-done.4.refs_0_.refs_4_
  19.4 1.9 %collective-permute-start.8 = (bf16[784,128]{1,0:T(8,128)(2,1)S(1)}, bf16[784,128]{1,0:T(8,128)(2,1)S(1)}, u32[]{:S(2)}, u32[]{:S(2)}) collective-permute-start(bf16[784,128]{1,0:T(8,128)(2,1)S(1)} %collective-permute-done.4.refs_0_.refs_4_), channel_id=1, source_target_pairs={{0,2},{1,3},{4,0},{5,1},{8,4},{9,5},{12,8},{13,9},{14,12},{15,13},... | collective-permute-start | bytes 602120 | tf_op jit(solution)/shard_map/ppermute | solution.py:320
  21.4 0.1 collective-permute-start.9
  21.5 1.7 %shard_map.61 = (f32[256,896]{1,0:T(8,128)S(1)}, f32[256,896]{1,0:T(8,128)S(1)}) custom-call(f32[8,256]{1,0:T(8,128)S(1)} %get-tuple-element.26.ends_ref, f32[2,512,128]{2,1,0:T(8,128)S(1)} %get-tuple-element.27.info_ref, bf16[512,64]{1,0:T(8,128)(2,1)S(1)} %get-tuple-element.28.feat_ref, ...), custom_call_target="tpu_custom_call", output_to_operand_aliasing={{0}: (7, {}), {1}: (8, {})} | custom-call | flops 8053063680 | bytes 1 | tf_op jit(solution)/shard_map/pallas_call | solution.py:353
  23.2 1.7 %collective-permute-done.10.refs_2_ = bf16[768,128]{1,0:T(8,128)(2,1)S(1)} collective-permute-done((bf16[768,128]{1,0:T(8,128)(2,1)S(1)}, bf16[768,128]{1,0:T(8,128)(2,1)S(1)}, u32[]{:S(2)}, u32[]{:S(2)}) %collective-permute-start.10) | collective-permute-done | bytes 196640 | tf_op jit(solution)/shard_map/ppermute | solution.py:320
  24.9 1.6 %collective-permute-done.11.refs_3_ = bf16[768,128]{1,0:T(8,128)(2,1)S(1)} collective-permute-done((bf16[768,128]{1,0:T(8,128)(2,1)S(1)}, bf16[768,128]{1,0:T(8,128)(2,1)S(1)}, u32[]{:S(2)}, u32[]{:S(2)}) %collective-permute-start.11) | collective-permute-done | bytes 196640 | tf_op jit(solution)/shard_map/ppermute | solution.py:320
  26.5 1.6 %collective-permute-start.12 = (bf16[768,128]{1,0:T(8,128)(2,1)S(1)}, bf16[768,128]{1,0:T(8,128)(2,1)S(1)}, u32[]{:S(2)}, u32[]{:S(2)}) collective-permute-start(bf16[768,128]{1,0:T(8,128)(2,1)S(1)} %collective-permute-done.10.refs_2_), channel_id=1, source_target_pairs={{0,2},{1,3},{4,0},{5,1},{8,4},{9,5},{12,8},{13,9},{14,12},{15,13},... | collective-permute-start | bytes 589832 | tf_op jit(solution)/shard_map/ppermute | solution.py:320
  28.1 0.4 %collective-permute-start.13 = (bf16[768,128]{1,0:T(8,128)(2,1)S(1)}, bf16[768,128]{1,0:T(8,128)(2,1)S(1)}, u32[]{:S(2)}, u32[]{:S(2)}) collective-permute-start(bf16[768,128]{1,0:T(8,128)(2,1)S(1)} %collective-permute-done.11.refs_3_), channel_id=1, source_target_pairs={{0,4},{1,5},{4,8},{5,9},{8,12},{9,13},{12,14},{13,15},{14,10},{15,... | collective-permute-start | bytes 589832 | tf_op jit(solution)/shard_map/ppermute | solution.py:320
  28.5 0.7 %collective-permute-done.8.refs_0_ = bf16[784,128]{1,0:T(8,128)(2,1)S(1)} collective-permute-done((bf16[784,128]{1,0:T(8,128)(2,1)S(1)}, bf16[784,128]{1,0:T(8,128)(2,1)S(1)}, u32[]{:S(2)}, u32[]{:S(2)}) %collective-permute-start.8) | collective-permute-done | bytes 200736 | tf_op jit(solution)/shard_map/ppermute | solution.py:320
  29.2 1.6 %collective-permute-start.14 = (bf16[784,128]{1,0:T(8,128)(2,1)S(1)}, bf16[784,128]{1,0:T(8,128)(2,1)S(1)}, u32[]{:S(2)}, u32[]{:S(2)}) collective-permute-start(bf16[784,128]{1,0:T(8,128)(2,1)S(1)} %collective-permute-done.8.refs_0_), channel_id=1, source_target_pairs={{0,2},{1,3},{4,0},{5,1},{8,4},{9,5},{12,8},{13,9},{14,12},{15,13},... | collective-permute-start | bytes 602120 | tf_op jit(solution)/shard_map/ppermute | solution.py:320
  30.8 0.4 %collective-permute-start.15 = (bf16[784,128]{1,0:T(8,128)(2,1)S(1)}, bf16[784,128]{1,0:T(8,128)(2,1)S(1)}, u32[]{:S(2)}, u32[]{:S(2)}) collective-permute-start(bf16[784,128]{1,0:T(8,128)(2,1)S(1)} %collective-permute-done.9.refs_1_), channel_id=1, source_target_pairs={{0,4},{1,5},{4,8},{5,9},{8,12},{9,13},{12,14},{13,15},{14,10},{15,... | collective-permute-start | bytes 602120 | tf_op jit(solution)/shard_map/ppermute | solution.py:320
  31.2 1.7 %shard_map.62 = (f32[256,896]{1,0:T(8,128)S(1)}, f32[256,896]{1,0:T(8,128)S(1)}) custom-call(f32[8,256]{1,0:T(8,128)S(1)} %get-tuple-element.26.ends_ref, f32[2,512,128]{2,1,0:T(8,128)S(1)} %get-tuple-element.27.info_ref, bf16[512,64]{1,0:T(8,128)(2,1)S(1)} %get-tuple-element.28.feat_ref, ...), custom_call_target="tpu_custom_call", output_to_operand_aliasing={{0}: (7, {}), {1}: (8, {})} | custom-call | flops 8053063680 | bytes 1 | tf_op jit(solution)/shard_map/pallas_call | solution.py:353
  33.0 1.2 %collective-permute-done.12.refs_2_ = bf16[768,128]{1,0:T(8,128)(2,1)S(1)} collective-permute-done((bf16[768,128]{1,0:T(8,128)(2,1)S(1)}, bf16[768,128]{1,0:T(8,128)(2,1)S(1)}, u32[]{:S(2)}, u32[]{:S(2)}) %collective-permute-start.12) | collective-permute-done | bytes 196640 | tf_op jit(solution)/shard_map/ppermute | solution.py:320
  34.2 1.3 %collective-permute-done.13.refs_3_ = bf16[768,128]{1,0:T(8,128)(2,1)S(1)} collective-permute-done((bf16[768,128]{1,0:T(8,128)(2,1)S(1)}, bf16[768,128]{1,0:T(8,128)(2,1)S(1)}, u32[]{:S(2)}, u32[]{:S(2)}) %collective-permute-start.13) | collective-permute-done | bytes 196640 | tf_op jit(solution)/shard_map/ppermute | solution.py:320
  35.5 1.2 %shard_map.63 = (f32[256,896]{1,0:T(8,128)S(1)}, bf16[256,896]{1,0:T(8,128)(2,1)S(1)}) custom-call(f32[8,256]{1,0:T(8,128)S(1)} %get-tuple-element.26.ends_ref, f32[2,512,128]{2,1,0:T(8,128)S(1)} %get-tuple-element.27.info_ref, bf16[512,64]{1,0:T(8,128)(2,1)S(1)} %get-tuple-element.28.feat_ref, ...), custom_call_target="tpu_custom_call", output_to_operand_aliasing={{0}: (7, {})} | custom-call | flops 1 | bytes 1 | tf_op jit(solution)/shard_map/pallas_call | solution.py:353
  36.9 0.7 %collective-permute-done.15.refs_1_ = bf16[784,128]{1,0:T(8,128)(2,1)S(1)} collective-permute-done((bf16[784,128]{1,0:T(8,128)(2,1)S(1)}, bf16[784,128]{1,0:T(8,128)(2,1)S(1)}, u32[]{:S(2)}, u32[]{:S(2)}) %collective-permute-start.15) | collective-permute-done | bytes 200736 | tf_op jit(solution)/shard_map/ppermute | solution.py:320
  37.6 0.7 %shard_map.64.own_in = f32[256,896]{1,0:T(8,128)S(1)} custom-call(f32[8,256]{1,0:T(8,128)S(1)} %get-tuple-element.26.ends_ref, f32[2,512,128]{2,1,0:T(8,128)S(1)} %get-tuple-element.27.info_ref, bf16[512,64]{1,0:T(8,128)(2,1)S(1)} %get-tuple-element.28.feat_ref, bf16[784,128]{1,0:T(8,128)(2,1)S(1)} %get-tuple-element.24.a_ref, ...), custom_call_target="tpu_custom_call", output_to_operand_aliasing={{}: (5, {})} | custom-call | flops 8053063680 | bytes 1 | tf_op jit(solution)/shard_map/pallas_call | solution.py:377
  38.4 0.9 %collective-permute-done.17.far_ref = bf16[784,128]{1,0:T(8,128)(2,1)S(1)} collective-permute-done((bf16[784,128]{1,0:T(8,128)(2,1)S(1)}, bf16[784,128]{1,0:T(8,128)(2,1)S(1)}, u32[]{:S(2)}, u32[]{:S(2)}) %collective-permute-start.17) | collective-permute-done | bytes 200736 | tf_op jit(solution)/shard_map/ppermute | solution.py:320
  39.3 1.5 %shard_map.66 = (bf16[256,768]{1,0:T(8,128)(2,1)}, f32[2,128]{1,0:T(2,128)}) custom-call(f32[8,256]{1,0:T(8,128)S(1)} %get-tuple-element.26.ends_ref, f32[2,512,128]{2,1,0:T(8,128)S(1)} %get-tuple-element.27.info_ref, bf16[512,64]{1,0:T(8,128)(2,1)S(1)} %get-tuple-element.28.feat_ref, bf16[784,128]{1,0:T(8,128)(2,1)S(1)} %get-tuple-element.24.a_ref, ...), custom_call_target="tpu_custom_call" | custom-call | flops 1 | bytes 1 | tf_op jit(solution)/shard_map/pallas_call | solution.py:380
  (16 shorter events, 0.4 us)
Async XLA Ops:
  0.6 12.4 %copy-start = (s32[16,16]{1,0:T(8,128)S(1)}, s32[16,16]{1,0:T(8,128)}, u32[]{:S(2)}) copy-start(s32[16,16]{1,0:T(8,128)} %mask_hbm.1) | copy-start | bytes 3076
  1.9 5.2 %collective-permute-start = (bf16[784,128]{1,0:T(8,128)(2,1)S(1)}, bf16[784,128]{1,0:T(8,128)(2,1)S(1)}, u32[]{:S(2)}, u32[]{:S(2)}) collective-permute-start(bf16[784,128]{1,0:T(8,128)(2,1)S(1)} %get-tuple-element.24.a_ref), channel_id=1, source_target_pairs={{0,1},{1,0},{2,3},{3,2},{4,5},{5,4},{6,7},{7,6},{8,9},{9,8},{10,11... | collective-permute-start | bytes 602120 | tf_op jit(solution)/shard_map/ppermute | solution.py:320
  2.4 8.5 %collective-permute-start.2 = (bf16[784,128]{1,0:T(8,128)(2,1)S(1)}, bf16[784,128]{1,0:T(8,128)(2,1)S(1)}, u32[]{:S(2)}, u32[]{:S(2)}) collective-permute-start(bf16[784,128]{1,0:T(8,128)(2,1)S(1)} %get-tuple-element.24.a_ref), channel_id=1, source_target_pairs={{0,2},{1,3},{4,0},{5,1},{8,4},{9,5},{12,8},{13,9},{14,12},{15,13},... | collective-permute-start | bytes 602120 | tf_op jit(solution)/shard_map/ppermute | solution.py:320
  5.0 7.8 %collective-permute-start.3 = (bf16[784,128]{1,0:T(8,128)(2,1)S(1)}, bf16[784,128]{1,0:T(8,128)(2,1)S(1)}, u32[]{:S(2)}, u32[]{:S(2)}) collective-permute-start(bf16[784,128]{1,0:T(8,128)(2,1)S(1)} %get-tuple-element.25.b_ref), channel_id=1, source_target_pairs={{0,4},{1,5},{4,8},{5,9},{8,12},{9,13},{12,14},{13,15},{14,10},{15,... | collective-permute-start | bytes 602120 | tf_op jit(solution)/shard_map/ppermute | solution.py:320
  5.2 7.8 %collective-permute-start.1 = (bf16[784,128]{1,0:T(8,128)(2,1)S(1)}, bf16[784,128]{1,0:T(8,128)(2,1)S(1)}, u32[]{:S(2)}, u32[]{:S(2)}) collective-permute-start(bf16[784,128]{1,0:T(8,128)(2,1)S(1)} %get-tuple-element.25.b_ref), channel_id=1, source_target_pairs={{0,1},{1,0},{2,3},{3,2},{4,5},{5,4},{6,7},{7,6},{8,9},{9,8},{10,11... | collective-permute-start | bytes 602120 | tf_op jit(solution)/shard_map/ppermute | solution.py:320
  5.3 7.7 %copy-start.1 = (s32[4]{0:T(128)S(1)}, s32[4]{0:T(128)}, u32[]{:S(2)}) copy-start(s32[4]{0:T(128)} %len_ref.1) | copy-start | bytes 52
  5.3 11.8 %collective-permute-start.7 = (bf16[768,128]{1,0:T(8,128)(2,1)S(1)}, bf16[768,128]{1,0:T(8,128)(2,1)S(1)}, u32[]{:S(2)}, u32[]{:S(2)}) collective-permute-start(bf16[768,128]{1,0:T(8,128)(2,1)S(1)} %get-tuple-element.32), channel_id=1, source_target_pairs={{0,4},{1,5},{4,8},{5,9},{8,12},{9,13},{12,14},{13,15},{14,10},{15,... | collective-permute-start | bytes 589832 | tf_op jit(solution)/shard_map/ppermute | solution.py:320
  7.1 10.0 %collective-permute-start.6 = (bf16[768,128]{1,0:T(8,128)(2,1)S(1)}, bf16[768,128]{1,0:T(8,128)(2,1)S(1)}, u32[]{:S(2)}, u32[]{:S(2)}) collective-permute-start(bf16[768,128]{1,0:T(8,128)(2,1)S(1)} %get-tuple-element.31), channel_id=1, source_target_pairs={{0,2},{1,3},{4,0},{5,1},{8,4},{9,5},{12,8},{13,9},{14,12},{15,13},... | collective-permute-start | bytes 589832 | tf_op jit(solution)/shard_map/ppermute | solution.py:320
  10.9 8.5 %collective-permute-start.4 = (bf16[784,128]{1,0:T(8,128)(2,1)S(1)}, bf16[784,128]{1,0:T(8,128)(2,1)S(1)}, u32[]{:S(2)}, u32[]{:S(2)}) collective-permute-start(bf16[784,128]{1,0:T(8,128)(2,1)S(1)} %collective-permute-done.2.f_ref.refs_4_), channel_id=1, source_target_pairs={{0,2},{1,3},{4,0},{5,1},{8,4},{9,5},{12,8},{13,9},{14,12},{15,13},... | collective-permute-start | bytes 602120 | tf_op jit(solution)/shard_map/ppermute | solution.py:320
  12.9 8.5 %collective-permute-start.5 = (bf16[784,128]{1,0:T(8,128)(2,1)S(1)}, bf16[784,128]{1,0:T(8,128)(2,1)S(1)}, u32[]{:S(2)}, u32[]{:S(2)}) collective-permute-start(bf16[784,128]{1,0:T(8,128)(2,1)S(1)} %collective-permute-done.3.g_ref.refs_5_), channel_id=1, source_target_pairs={{0,4},{1,5},{4,8},{5,9},{8,12},{9,13},{12,14},{13,15},{14,10},{15,... | collective-permute-start | bytes 602120 | tf_op jit(solution)/shard_map/ppermute | solution.py:320
  17.1 7.8 %collective-permute-start.10 = (bf16[768,128]{1,0:T(8,128)(2,1)S(1)}, bf16[768,128]{1,0:T(8,128)(2,1)S(1)}, u32[]{:S(2)}, u32[]{:S(2)}) collective-permute-start(bf16[768,128]{1,0:T(8,128)(2,1)S(1)} %collective-permute-done.6.refs_2_), channel_id=1, source_target_pairs={{0,2},{1,3},{4,0},{5,1},{8,4},{9,5},{12,8},{13,9},{14,12},{15,13},... | collective-permute-start | bytes 589832 | tf_op jit(solution)/shard_map/ppermute | solution.py:320
  18.7 7.8 %collective-permute-start.11 = (bf16[768,128]{1,0:T(8,128)(2,1)S(1)}, bf16[768,128]{1,0:T(8,128)(2,1)S(1)}, u32[]{:S(2)}, u32[]{:S(2)}) collective-permute-start(bf16[768,128]{1,0:T(8,128)(2,1)S(1)} %collective-permute-done.7.refs_3_), channel_id=1, source_target_pairs={{0,4},{1,5},{4,8},{5,9},{8,12},{9,13},{12,14},{13,15},{14,10},{15,... | collective-permute-start | bytes 589832 | tf_op jit(solution)/shard_map/ppermute | solution.py:320
  19.4 9.8 %collective-permute-start.8 = (bf16[784,128]{1,0:T(8,128)(2,1)S(1)}, bf16[784,128]{1,0:T(8,128)(2,1)S(1)}, u32[]{:S(2)}, u32[]{:S(2)}) collective-permute-start(bf16[784,128]{1,0:T(8,128)(2,1)S(1)} %collective-permute-done.4.refs_0_.refs_4_), channel_id=1, source_target_pairs={{0,2},{1,3},{4,0},{5,1},{8,4},{9,5},{12,8},{13,9},{14,12},{15,13},... | collective-permute-start | bytes 602120 | tf_op jit(solution)/shard_map/ppermute | solution.py:320
  21.4 9.4 %collective-permute-start.9 = (bf16[784,128]{1,0:T(8,128)(2,1)S(1)}, bf16[784,128]{1,0:T(8,128)(2,1)S(1)}, u32[]{:S(2)}, u32[]{:S(2)}) collective-permute-start(bf16[784,128]{1,0:T(8,128)(2,1)S(1)} %collective-permute-done.5.refs_1_.refs_5_), channel_id=1, source_target_pairs={{0,4},{1,5},{4,8},{5,9},{8,12},{9,13},{12,14},{13,15},{14,10},{15,... | collective-permute-start | bytes 602120 | tf_op jit(solution)/shard_map/ppermute | solution.py:320
  26.5 7.7 %collective-permute-start.12 = (bf16[768,128]{1,0:T(8,128)(2,1)S(1)}, bf16[768,128]{1,0:T(8,128)(2,1)S(1)}, u32[]{:S(2)}, u32[]{:S(2)}) collective-permute-start(bf16[768,128]{1,0:T(8,128)(2,1)S(1)} %collective-permute-done.10.refs_2_), channel_id=1, source_target_pairs={{0,2},{1,3},{4,0},{5,1},{8,4},{9,5},{12,8},{13,9},{14,12},{15,13},... | collective-permute-start | bytes 589832 | tf_op jit(solution)/shard_map/ppermute | solution.py:320
  28.1 7.4 %collective-permute-start.13 = (bf16[768,128]{1,0:T(8,128)(2,1)S(1)}, bf16[768,128]{1,0:T(8,128)(2,1)S(1)}, u32[]{:S(2)}, u32[]{:S(2)}) collective-permute-start(bf16[768,128]{1,0:T(8,128)(2,1)S(1)} %collective-permute-done.11.refs_3_), channel_id=1, source_target_pairs={{0,4},{1,5},{4,8},{5,9},{8,12},{9,13},{12,14},{13,15},{14,10},{15,... | collective-permute-start | bytes 589832 | tf_op jit(solution)/shard_map/ppermute | solution.py:320
  29.2 7.5 %collective-permute-start.14 = (bf16[784,128]{1,0:T(8,128)(2,1)S(1)}, bf16[784,128]{1,0:T(8,128)(2,1)S(1)}, u32[]{:S(2)}, u32[]{:S(2)}) collective-permute-start(bf16[784,128]{1,0:T(8,128)(2,1)S(1)} %collective-permute-done.8.refs_0_), channel_id=1, source_target_pairs={{0,2},{1,3},{4,0},{5,1},{8,4},{9,5},{12,8},{13,9},{14,12},{15,13},... | collective-permute-start | bytes 602120 | tf_op jit(solution)/shard_map/ppermute | solution.py:320
  30.8 6.8 %collective-permute-start.15 = (bf16[784,128]{1,0:T(8,128)(2,1)S(1)}, bf16[784,128]{1,0:T(8,128)(2,1)S(1)}, u32[]{:S(2)}, u32[]{:S(2)}) collective-permute-start(bf16[784,128]{1,0:T(8,128)(2,1)S(1)} %collective-permute-done.9.refs_1_), channel_id=1, source_target_pairs={{0,4},{1,5},{4,8},{5,9},{8,12},{9,13},{12,14},{13,15},{14,10},{15,... | collective-permute-start | bytes 602120 | tf_op jit(solution)/shard_map/ppermute | solution.py:320
  36.8 2.5 %collective-permute-start.16 = (bf16[2576,128]{1,0:T(8,128)(2,1)S(1)}, bf16[2576,128]{1,0:T(8,128)(2,1)S(1)}, u32[]{:S(2)}, u32[]{:S(2)}) collective-permute-start(bf16[2576,128]{1,0:T(8,128)(2,1)S(1)} %shard_map.65), channel_id=1, source_target_pairs={{0,1},{1,0},{2,3},{3,2},{4,5},{5,4},{6,7},{7,6},{8,9},{9,8},{10,11... | collective-permute-start | bytes 1978376 | tf_op jit(solution)/shard_map/ppermute | solution.py:320
  37.6 1.6 %collective-permute-start.17 = (bf16[784,128]{1,0:T(8,128)(2,1)S(1)}, bf16[784,128]{1,0:T(8,128)(2,1)S(1)}, u32[]{:S(2)}, u32[]{:S(2)}) collective-permute-start(bf16[784,128]{1,0:T(8,128)(2,1)S(1)} %collective-permute-done.15.refs_1_), channel_id=1, source_target_pairs={{0,1},{1,0},{2,3},{3,2},{4,5},{5,4},{6,7},{7,6},{8,9},{9,8},{10,11... | collective-permute-start | bytes 602120 | tf_op jit(solution)/shard_map/ppermute | solution.py:320

commit v5 on v4

--- a/solution.py
+++ b/solution.py
@@ -272,7 +272,7 @@
 
 
 def last_body(half, clusters, ends_ref, info_ref, feat_ref, a_ref, b_ref, own_in, got_ref,
-              far_ref, dir_ref, out_top):
+              far_ref, dir_hbm, top_hbm, dir_ref, top_ref, sem):
     ends = [ends_ref[c : c + 1, :] for c in range(clusters - 1)]
     rows, width = 2 * half, a_ref.shape[0] // half * LANES
     query = jnp.concatenate([rows_of(r, half) for r in (a_ref, b_ref)], axis=0)
@@ -286,8 +286,6 @@
             rows, query, info_ref[0, :rows], info_ref[1, :rows], feat_ref[:rows], acc, top, keys,
             pos, ends, clusters, False,
         )
-    scale = math.sqrt(width) * lax.rsqrt(jnp.sum(acc * acc, axis=1, keepdims=True) + EPS)
-    dir_ref[...] = (acc * scale).astype(jnp.bfloat16)
     best = jnp.max(top, axis=1, keepdims=True)
     eye = lax.broadcasted_iota(jnp.int32, (half, half), 0) == lax.broadcasted_iota(
         jnp.int32, (half, half), 1
@@ -296,7 +294,18 @@
         jnp.max(jnp.where(eye, best[at : at + half], -1.0), axis=0, keepdims=True)
         for at in (0, half)
     ]
-    out_top[...] = jnp.concatenate(lines, axis=0)
+    top_ref[...] = jnp.concatenate(lines, axis=0)
+    sends = [pltpu.make_async_copy(top_ref, top_hbm, sem.at[2])]
+    sends[0].start()
+    for i in range(2):
+        part = acc[i * half : (i + 1) * half]
+        scale = math.sqrt(width) * lax.rsqrt(jnp.sum(part * part, axis=1, keepdims=True) + EPS)
+        dir_ref[i * half : (i + 1) * half] = (part * scale).astype(jnp.bfloat16)
+        place = pl.ds(i * half, half)
+        sends.append(pltpu.make_async_copy(dir_ref.at[place], dir_hbm.at[place], sem.at[i]))
+        sends[-1].start()
+    for copy in sends:
+        copy.wait()
 
 
 def in_hbm(x):
@@ -379,7 +388,11 @@
     )(*shared, own, *lead[-1])[0]
     out_dir, out_top = call(
         functools.partial(last_body, half, clusters),
-        [bf(rows), f32(2, half)], [VM] * 8,
+        [bf(rows), f32(2, half)], [VM] * 8, out_specs=[HB, HB],
+        scratch=[
+            pltpu.VMEM((rows, width), jnp.bfloat16), pltpu.VMEM((2, half), jnp.float32),
+            pltpu.SemaphoreType.DMA((3,)),
+        ],
     )(*shared, own, got, far)
     return out_top.reshape(rows), out_dir
 

time: 40.9 us -> 40.9 us (level)
  no operation moved by 1% of the time
where the time goes in v5:
time: 40.9 us; the launch traced here: 40.8 us
  starting transfers between devices  15.5 us (38%)
  waiting for transfers between devices  13.5 us (33%)
  Pallas kernels  11.1 us (27%)
  between operations  0.73 us (2%)
    ppermute x18, starting transfers between devices, move(): return lax.ppermute(x, 'blk', perm)  15.5 us
    ppermute x18, waiting for transfers between devices, move(): return lax.ppermute(x, 'blk', perm)  13.5 us
    pallas_call x3, Pallas kernels, middle(): call(functools.partial(middle_body, half, clusters, groups), [state, sent...  4.71 us
    pallas_call x1, Pallas kernels, per_device(): call(functools.partial(first_body, half, clusters), [state, state, f32(2,...  2.77 us
    pallas_call x1, Pallas kernels, per_device(): call(functools.partial(last_body, half, clusters), [bf(rows), f32(2, half...  1.49 us
    pallas_call x1, Pallas kernels, per_device(): call(functools.partial(prep_body, PARTS), [bf(full, LANES)] * 2 + [bf(ful...  1.28 us
  transfers between devices with their start and end apart: 18, of which 10 were waited for; matrix products, arithmetic and copies ran while one was open for 0% of the time, Pallas kernels for 20%

profile of v5, /device:TPU:0, one launch (start us, length us, event | category | flops | bytes accessed | tf_op | source)
XLA Modules:
  0.0 40.8 jit_solution(9907716156083967434)
XLA Ops:
  0.6 1.3 %shard_map.59 = (bf16[784,128]{1,0:T(8,128)(2,1)S(1)}, bf16[784,128]{1,0:T(8,128)(2,1)S(1)}, bf16[768,128]{1,0:T(8,128)(2,1)S(1)}, bf16[768,128]{1,0:T(8,128)(2,1)S(1)}) custom-call(f32[256,768]{1,0:T(8,128)} %emb_hbm.1, s32[2,128]{1,0:T(2,128)} %bitcast.2), custom_call_target="tpu_custom_call" | custom-call | flops 1 | bytes 1 | tf_op jit(solution)/shard_map/pallas_call | solution.py:340
  1.9 0.5 %collective-permute-start = (bf16[784,128]{1,0:T(8,128)(2,1)S(1)}, bf16[784,128]{1,0:T(8,128)(2,1)S(1)}, u32[]{:S(2)}, u32[]{:S(2)}) collective-permute-start(bf16[784,128]{1,0:T(8,128)(2,1)S(1)} %get-tuple-element.24.a_ref), channel_id=1, source_target_pairs={{0,1},{1,0},{2,3},{3,2},{4,5},{5,4},{6,7},{7,6},{8,9},{9,8},{10,11... | collective-permute-start | bytes 602120 | tf_op jit(solution)/shard_map/ppermute | solution.py:329
  2.4 2.6 %collective-permute-start.2 = (bf16[784,128]{1,0:T(8,128)(2,1)S(1)}, bf16[784,128]{1,0:T(8,128)(2,1)S(1)}, u32[]{:S(2)}, u32[]{:S(2)}) collective-permute-start(bf16[784,128]{1,0:T(8,128)(2,1)S(1)} %get-tuple-element.24.a_ref), channel_id=1, source_target_pairs={{0,2},{1,3},{4,0},{5,1},{8,4},{9,5},{12,8},{13,9},{14,12},{15,13},... | collective-permute-start | bytes 602120 | tf_op jit(solution)/shard_map/ppermute | solution.py:329
  5.0 0.1 collective-permute-start.3
  5.3 1.9 %collective-permute-start.7 = (bf16[768,128]{1,0:T(8,128)(2,1)S(1)}, bf16[768,128]{1,0:T(8,128)(2,1)S(1)}, u32[]{:S(2)}, u32[]{:S(2)}) collective-permute-start(bf16[768,128]{1,0:T(8,128)(2,1)S(1)} %get-tuple-element.32), channel_id=1, source_target_pairs={{0,4},{1,5},{4,8},{5,9},{8,12},{9,13},{12,14},{13,15},{14,10},{15,... | collective-permute-start | bytes 589832 | tf_op jit(solution)/shard_map/ppermute | solution.py:329
  7.1 0.2 collective-permute-start.6
  7.3 3.6 %collective-permute-done.2.f_ref.refs_4_ = bf16[784,128]{1,0:T(8,128)(2,1)S(1)} collective-permute-done((bf16[784,128]{1,0:T(8,128)(2,1)S(1)}, bf16[784,128]{1,0:T(8,128)(2,1)S(1)}, u32[]{:S(2)}, u32[]{:S(2)}) %collective-permute-start.2) | collective-permute-done | bytes 200736 | tf_op jit(solution)/shard_map/ppermute | solution.py:329
  10.9 1.9 %collective-permute-start.4 = (bf16[784,128]{1,0:T(8,128)(2,1)S(1)}, bf16[784,128]{1,0:T(8,128)(2,1)S(1)}, u32[]{:S(2)}, u32[]{:S(2)}) collective-permute-start(bf16[784,128]{1,0:T(8,128)(2,1)S(1)} %collective-permute-done.2.f_ref.refs_4_), channel_id=1, source_target_pairs={{0,2},{1,3},{4,0},{5,1},{8,4},{9,5},{12,8},{13,9},{14,12},{15,13},... | collective-permute-start | bytes 602120 | tf_op jit(solution)/shard_map/ppermute | solution.py:329
  12.9 0.1 collective-permute-start.5
  13.0 2.8 %shard_map.60 = (f32[256,896]{1,0:T(8,128)S(1)}, f32[256,896]{1,0:T(8,128)S(1)}, f32[2,512,128]{2,1,0:T(8,128)S(1)}, bf16[512,64]{1,0:T(8,128)(2,1)S(1)}, f32[8,256]{1,0:T(8,128)S(1)}) custom-call(s32[4]{0:T(128)S(1)} %copy-done.1, s32[16,16]{1,0:T(8,128)S(1)} %copy-done, bf16[784,128]{1,0:T(8,128)(2,1)S(1)} %get-tuple-element.24.a_ref, ...), custom_call_target="tpu_custom_call" | custom-call | flops 8053063680 | bytes 1 | tf_op jit(solution)/shard_map/pallas_call | solution.py:353
  15.8 1.3 %collective-permute-done.7.refs_3_ = bf16[768,128]{1,0:T(8,128)(2,1)S(1)} collective-permute-done((bf16[768,128]{1,0:T(8,128)(2,1)S(1)}, bf16[768,128]{1,0:T(8,128)(2,1)S(1)}, u32[]{:S(2)}, u32[]{:S(2)}) %collective-permute-start.7) | collective-permute-done | bytes 196640 | tf_op jit(solution)/shard_map/ppermute | solution.py:329
  17.1 1.6 %collective-permute-start.10 = (bf16[768,128]{1,0:T(8,128)(2,1)S(1)}, bf16[768,128]{1,0:T(8,128)(2,1)S(1)}, u32[]{:S(2)}, u32[]{:S(2)}) collective-permute-start(bf16[768,128]{1,0:T(8,128)(2,1)S(1)} %collective-permute-done.6.refs_2_), channel_id=1, source_target_pairs={{0,2},{1,3},{4,0},{5,1},{8,4},{9,5},{12,8},{13,9},{14,12},{15,13},... | collective-permute-start | bytes 589832 | tf_op jit(solution)/shard_map/ppermute | solution.py:329
  18.7 0.4 %collective-permute-start.11 = (bf16[768,128]{1,0:T(8,128)(2,1)S(1)}, bf16[768,128]{1,0:T(8,128)(2,1)S(1)}, u32[]{:S(2)}, u32[]{:S(2)}) collective-permute-start(bf16[768,128]{1,0:T(8,128)(2,1)S(1)} %collective-permute-done.7.refs_3_), channel_id=1, source_target_pairs={{0,4},{1,5},{4,8},{5,9},{8,12},{9,13},{12,14},{13,15},{14,10},{15,... | collective-permute-start | bytes 589832 | tf_op jit(solution)/shard_map/ppermute | solution.py:329
  19.1 0.3 collective-permute-done.4.refs_0_.refs_4_
  19.4 1.9 %collective-permute-start.8 = (bf16[784,128]{1,0:T(8,128)(2,1)S(1)}, bf16[784,128]{1,0:T(8,128)(2,1)S(1)}, u32[]{:S(2)}, u32[]{:S(2)}) collective-permute-start(bf16[784,128]{1,0:T(8,128)(2,1)S(1)} %collective-permute-done.4.refs_0_.refs_4_), channel_id=1, source_target_pairs={{0,2},{1,3},{4,0},{5,1},{8,4},{9,5},{12,8},{13,9},{14,12},{15,13},... | collective-permute-start | bytes 602120 | tf_op jit(solution)/shard_map/ppermute | solution.py:329
  21.4 0.1 collective-permute-start.9
  21.5 1.7 %shard_map.61 = (f32[256,896]{1,0:T(8,128)S(1)}, f32[256,896]{1,0:T(8,128)S(1)}) custom-call(f32[8,256]{1,0:T(8,128)S(1)} %get-tuple-element.26.ends_ref, f32[2,512,128]{2,1,0:T(8,128)S(1)} %get-tuple-element.27.info_ref, bf16[512,64]{1,0:T(8,128)(2,1)S(1)} %get-tuple-element.28.feat_ref, ...), custom_call_target="tpu_custom_call", output_to_operand_aliasing={{0}: (7, {}), {1}: (8, {})} | custom-call | flops 8053063680 | bytes 1 | tf_op jit(solution)/shard_map/pallas_call | solution.py:362
  23.2 1.7 %collective-permute-done.10.refs_2_ = bf16[768,128]{1,0:T(8,128)(2,1)S(1)} collective-permute-done((bf16[768,128]{1,0:T(8,128)(2,1)S(1)}, bf16[768,128]{1,0:T(8,128)(2,1)S(1)}, u32[]{:S(2)}, u32[]{:S(2)}) %collective-permute-start.10) | collective-permute-done | bytes 196640 | tf_op jit(solution)/shard_map/ppermute | solution.py:329
  24.9 1.6 %collective-permute-done.11.refs_3_ = bf16[768,128]{1,0:T(8,128)(2,1)S(1)} collective-permute-done((bf16[768,128]{1,0:T(8,128)(2,1)S(1)}, bf16[768,128]{1,0:T(8,128)(2,1)S(1)}, u32[]{:S(2)}, u32[]{:S(2)}) %collective-permute-start.11) | collective-permute-done | bytes 196640 | tf_op jit(solution)/shard_map/ppermute | solution.py:329
  26.5 1.6 %collective-permute-start.12 = (bf16[768,128]{1,0:T(8,128)(2,1)S(1)}, bf16[768,128]{1,0:T(8,128)(2,1)S(1)}, u32[]{:S(2)}, u32[]{:S(2)}) collective-permute-start(bf16[768,128]{1,0:T(8,128)(2,1)S(1)} %collective-permute-done.10.refs_2_), channel_id=1, source_target_pairs={{0,2},{1,3},{4,0},{5,1},{8,4},{9,5},{12,8},{13,9},{14,12},{15,13},... | collective-permute-start | bytes 589832 | tf_op jit(solution)/shard_map/ppermute | solution.py:329
  28.1 0.4 %collective-permute-start.13 = (bf16[768,128]{1,0:T(8,128)(2,1)S(1)}, bf16[768,128]{1,0:T(8,128)(2,1)S(1)}, u32[]{:S(2)}, u32[]{:S(2)}) collective-permute-start(bf16[768,128]{1,0:T(8,128)(2,1)S(1)} %collective-permute-done.11.refs_3_), channel_id=1, source_target_pairs={{0,4},{1,5},{4,8},{5,9},{8,12},{9,13},{12,14},{13,15},{14,10},{15,... | collective-permute-start | bytes 589832 | tf_op jit(solution)/shard_map/ppermute | solution.py:329
  28.5 0.7 %collective-permute-done.8.refs_0_ = bf16[784,128]{1,0:T(8,128)(2,1)S(1)} collective-permute-done((bf16[784,128]{1,0:T(8,128)(2,1)S(1)}, bf16[784,128]{1,0:T(8,128)(2,1)S(1)}, u32[]{:S(2)}, u32[]{:S(2)}) %collective-permute-start.8) | collective-permute-done | bytes 200736 | tf_op jit(solution)/shard_map/ppermute | solution.py:329
  29.2 1.6 %collective-permute-start.14 = (bf16[784,128]{1,0:T(8,128)(2,1)S(1)}, bf16[784,128]{1,0:T(8,128)(2,1)S(1)}, u32[]{:S(2)}, u32[]{:S(2)}) collective-permute-start(bf16[784,128]{1,0:T(8,128)(2,1)S(1)} %collective-permute-done.8.refs_0_), channel_id=1, source_target_pairs={{0,2},{1,3},{4,0},{5,1},{8,4},{9,5},{12,8},{13,9},{14,12},{15,13},... | collective-permute-start | bytes 602120 | tf_op jit(solution)/shard_map/ppermute | solution.py:329
  30.8 0.4 %collective-permute-start.15 = (bf16[784,128]{1,0:T(8,128)(2,1)S(1)}, bf16[784,128]{1,0:T(8,128)(2,1)S(1)}, u32[]{:S(2)}, u32[]{:S(2)}) collective-permute-start(bf16[784,128]{1,0:T(8,128)(2,1)S(1)} %collective-permute-done.9.refs_1_), channel_id=1, source_target_pairs={{0,4},{1,5},{4,8},{5,9},{8,12},{9,13},{12,14},{13,15},{14,10},{15,... | collective-permute-start | bytes 602120 | tf_op jit(solution)/shard_map/ppermute | solution.py:329
  31.2 1.7 %shard_map.62 = (f32[256,896]{1,0:T(8,128)S(1)}, f32[256,896]{1,0:T(8,128)S(1)}) custom-call(f32[8,256]{1,0:T(8,128)S(1)} %get-tuple-element.26.ends_ref, f32[2,512,128]{2,1,0:T(8,128)S(1)} %get-tuple-element.27.info_ref, bf16[512,64]{1,0:T(8,128)(2,1)S(1)} %get-tuple-element.28.feat_ref, ...), custom_call_target="tpu_custom_call", output_to_operand_aliasing={{0}: (7, {}), {1}: (8, {})} | custom-call | flops 8053063680 | bytes 1 | tf_op jit(solution)/shard_map/pallas_call | solution.py:362
  33.0 1.2 %collective-permute-done.12.refs_2_ = bf16[768,128]{1,0:T(8,128)(2,1)S(1)} collective-permute-done((bf16[768,128]{1,0:T(8,128)(2,1)S(1)}, bf16[768,128]{1,0:T(8,128)(2,1)S(1)}, u32[]{:S(2)}, u32[]{:S(2)}) %collective-permute-start.12) | collective-permute-done | bytes 196640 | tf_op jit(solution)/shard_map/ppermute | solution.py:329
  34.2 1.3 %collective-permute-done.13.refs_3_ = bf16[768,128]{1,0:T(8,128)(2,1)S(1)} collective-permute-done((bf16[768,128]{1,0:T(8,128)(2,1)S(1)}, bf16[768,128]{1,0:T(8,128)(2,1)S(1)}, u32[]{:S(2)}, u32[]{:S(2)}) %collective-permute-start.13) | collective-permute-done | bytes 196640 | tf_op jit(solution)/shard_map/ppermute | solution.py:329
  35.5 1.2 %shard_map.63 = (f32[256,896]{1,0:T(8,128)S(1)}, bf16[256,896]{1,0:T(8,128)(2,1)S(1)}) custom-call(f32[8,256]{1,0:T(8,128)S(1)} %get-tuple-element.26.ends_ref, f32[2,512,128]{2,1,0:T(8,128)S(1)} %get-tuple-element.27.info_ref, bf16[512,64]{1,0:T(8,128)(2,1)S(1)} %get-tuple-element.28.feat_ref, ...), custom_call_target="tpu_custom_call", output_to_operand_aliasing={{0}: (7, {})} | custom-call | flops 1 | bytes 1 | tf_op jit(solution)/shard_map/pallas_call | solution.py:362
  36.9 0.7 %collective-permute-done.15.refs_1_ = bf16[784,128]{1,0:T(8,128)(2,1)S(1)} collective-permute-done((bf16[784,128]{1,0:T(8,128)(2,1)S(1)}, bf16[784,128]{1,0:T(8,128)(2,1)S(1)}, u32[]{:S(2)}, u32[]{:S(2)}) %collective-permute-start.15) | collective-permute-done | bytes 200736 | tf_op jit(solution)/shard_map/ppermute | solution.py:329
  37.6 0.7 %shard_map.64.own_in = f32[256,896]{1,0:T(8,128)S(1)} custom-call(f32[8,256]{1,0:T(8,128)S(1)} %get-tuple-element.26.ends_ref, f32[2,512,128]{2,1,0:T(8,128)S(1)} %get-tuple-element.27.info_ref, bf16[512,64]{1,0:T(8,128)(2,1)S(1)} %get-tuple-element.28.feat_ref, bf16[784,128]{1,0:T(8,128)(2,1)S(1)} %get-tuple-element.24.a_ref, ...), custom_call_target="tpu_custom_call", output_to_operand_aliasing={{}: (5, {})} | custom-call | flops 8053063680 | bytes 1 | tf_op jit(solution)/shard_map/pallas_call | solution.py:386
  38.4 0.9 %collective-permute-done.17.far_ref = bf16[784,128]{1,0:T(8,128)(2,1)S(1)} collective-permute-done((bf16[784,128]{1,0:T(8,128)(2,1)S(1)}, bf16[784,128]{1,0:T(8,128)(2,1)S(1)}, u32[]{:S(2)}, u32[]{:S(2)}) %collective-permute-start.17) | collective-permute-done | bytes 200736 | tf_op jit(solution)/shard_map/ppermute | solution.py:329
  39.3 1.5 %shard_map.66 = (bf16[256,768]{1,0:T(8,128)(2,1)}, f32[2,128]{1,0:T(2,128)}) custom-call(f32[8,256]{1,0:T(8,128)S(1)} %get-tuple-element.26.ends_ref, f32[2,512,128]{2,1,0:T(8,128)S(1)} %get-tuple-element.27.info_ref, bf16[512,64]{1,0:T(8,128)(2,1)S(1)} %get-tuple-element.28.feat_ref, bf16[784,128]{1,0:T(8,128)(2,1)S(1)} %get-tuple-element.24.a_ref, ...), custom_call_target="tpu_custom_call" | custom-call | flops 1 | bytes 1 | tf_op jit(solution)/shard_map/pallas_call | solution.py:389
  (16 shorter events, 0.4 us)
Async XLA Ops:
  0.6 12.4 %copy-start = (s32[16,16]{1,0:T(8,128)S(1)}, s32[16,16]{1,0:T(8,128)}, u32[]{:S(2)}) copy-start(s32[16,16]{1,0:T(8,128)} %mask_hbm.1) | copy-start | bytes 3076
  1.9 5.2 %collective-permute-start = (bf16[784,128]{1,0:T(8,128)(2,1)S(1)}, bf16[784,128]{1,0:T(8,128)(2,1)S(1)}, u32[]{:S(2)}, u32[]{:S(2)}) collective-permute-start(bf16[784,128]{1,0:T(8,128)(2,1)S(1)} %get-tuple-element.24.a_ref), channel_id=1, source_target_pairs={{0,1},{1,0},{2,3},{3,2},{4,5},{5,4},{6,7},{7,6},{8,9},{9,8},{10,11... | collective-permute-start | bytes 602120 | tf_op jit(solution)/shard_map/ppermute | solution.py:329
  2.4 8.5 %collective-permute-start.2 = (bf16[784,128]{1,0:T(8,128)(2,1)S(1)}, bf16[784,128]{1,0:T(8,128)(2,1)S(1)}, u32[]{:S(2)}, u32[]{:S(2)}) collective-permute-start(bf16[784,128]{1,0:T(8,128)(2,1)S(1)} %get-tuple-element.24.a_ref), channel_id=1, source_target_pairs={{0,2},{1,3},{4,0},{5,1},{8,4},{9,5},{12,8},{13,9},{14,12},{15,13},... | collective-permute-start | bytes 602120 | tf_op jit(solution)/shard_map/ppermute | solution.py:329
  5.0 7.8 %collective-permute-start.3 = (bf16[784,128]{1,0:T(8,128)(2,1)S(1)}, bf16[784,128]{1,0:T(8,128)(2,1)S(1)}, u32[]{:S(2)}, u32[]{:S(2)}) collective-permute-start(bf16[784,128]{1,0:T(8,128)(2,1)S(1)} %get-tuple-element.25.b_ref), channel_id=1, source_target_pairs={{0,4},{1,5},{4,8},{5,9},{8,12},{9,13},{12,14},{13,15},{14,10},{15,... | collective-permute-start | bytes 602120 | tf_op jit(solution)/shard_map/ppermute | solution.py:329
  5.2 7.8 %collective-permute-start.1 = (bf16[784,128]{1,0:T(8,128)(2,1)S(1)}, bf16[784,128]{1,0:T(8,128)(2,1)S(1)}, u32[]{:S(2)}, u32[]{:S(2)}) collective-permute-start(bf16[784,128]{1,0:T(8,128)(2,1)S(1)} %get-tuple-element.25.b_ref), channel_id=1, source_target_pairs={{0,1},{1,0},{2,3},{3,2},{4,5},{5,4},{6,7},{7,6},{8,9},{9,8},{10,11... | collective-permute-start | bytes 602120 | tf_op jit(solution)/shard_map/ppermute | solution.py:329
  5.3 7.7 %copy-start.1 = (s32[4]{0:T(128)S(1)}, s32[4]{0:T(128)}, u32[]{:S(2)}) copy-start(s32[4]{0:T(128)} %len_ref.1) | copy-start | bytes 52
  5.3 11.8 %collective-permute-start.7 = (bf16[768,128]{1,0:T(8,128)(2,1)S(1)}, bf16[768,128]{1,0:T(8,128)(2,1)S(1)}, u32[]{:S(2)}, u32[]{:S(2)}) collective-permute-start(bf16[768,128]{1,0:T(8,128)(2,1)S(1)} %get-tuple-element.32), channel_id=1, source_target_pairs={{0,4},{1,5},{4,8},{5,9},{8,12},{9,13},{12,14},{13,15},{14,10},{15,... | collective-permute-start | bytes 589832 | tf_op jit(solution)/shard_map/ppermute | solution.py:329
  7.1 10.0 %collective-permute-start.6 = (bf16[768,128]{1,0:T(8,128)(2,1)S(1)}, bf16[768,128]{1,0:T(8,128)(2,1)S(1)}, u32[]{:S(2)}, u32[]{:S(2)}) collective-permute-start(bf16[768,128]{1,0:T(8,128)(2,1)S(1)} %get-tuple-element.31), channel_id=1, source_target_pairs={{0,2},{1,3},{4,0},{5,1},{8,4},{9,5},{12,8},{13,9},{14,12},{15,13},... | collective-permute-start | bytes 589832 | tf_op jit(solution)/shard_map/ppermute | solution.py:329
  10.9 8.5 %collective-permute-start.4 = (bf16[784,128]{1,0:T(8,128)(2,1)S(1)}, bf16[784,128]{1,0:T(8,128)(2,1)S(1)}, u32[]{:S(2)}, u32[]{:S(2)}) collective-permute-start(bf16[784,128]{1,0:T(8,128)(2,1)S(1)} %collective-permute-done.2.f_ref.refs_4_), channel_id=1, source_target_pairs={{0,2},{1,3},{4,0},{5,1},{8,4},{9,5},{12,8},{13,9},{14,12},{15,13},... | collective-permute-start | bytes 602120 | tf_op jit(solution)/shard_map/ppermute | solution.py:329
  12.9 8.5 %collective-permute-start.5 = (bf16[784,128]{1,0:T(8,128)(2,1)S(1)}, bf16[784,128]{1,0:T(8,128)(2,1)S(1)}, u32[]{:S(2)}, u32[]{:S(2)}) collective-permute-start(bf16[784,128]{1,0:T(8,128)(2,1)S(1)} %collective-permute-done.3.g_ref.refs_5_), channel_id=1, source_target_pairs={{0,4},{1,5},{4,8},{5,9},{8,12},{9,13},{12,14},{13,15},{14,10},{15,... | collective-permute-start | bytes 602120 | tf_op jit(solution)/shard_map/ppermute | solution.py:329
  17.1 7.8 %collective-permute-start.10 = (bf16[768,128]{1,0:T(8,128)(2,1)S(1)}, bf16[768,128]{1,0:T(8,128)(2,1)S(1)}, u32[]{:S(2)}, u32[]{:S(2)}) collective-permute-start(bf16[768,128]{1,0:T(8,128)(2,1)S(1)} %collective-permute-done.6.refs_2_), channel_id=1, source_target_pairs={{0,2},{1,3},{4,0},{5,1},{8,4},{9,5},{12,8},{13,9},{14,12},{15,13},... | collective-permute-start | bytes 589832 | tf_op jit(solution)/shard_map/ppermute | solution.py:329
  18.7 7.8 %collective-permute-start.11 = (bf16[768,128]{1,0:T(8,128)(2,1)S(1)}, bf16[768,128]{1,0:T(8,128)(2,1)S(1)}, u32[]{:S(2)}, u32[]{:S(2)}) collective-permute-start(bf16[768,128]{1,0:T(8,128)(2,1)S(1)} %collective-permute-done.7.refs_3_), channel_id=1, source_target_pairs={{0,4},{1,5},{4,8},{5,9},{8,12},{9,13},{12,14},{13,15},{14,10},{15,... | collective-permute-start | bytes 589832 | tf_op jit(solution)/shard_map/ppermute | solution.py:329
  19.4 9.8 %collective-permute-start.8 = (bf16[784,128]{1,0:T(8,128)(2,1)S(1)}, bf16[784,128]{1,0:T(8,128)(2,1)S(1)}, u32[]{:S(2)}, u32[]{:S(2)}) collective-permute-start(bf16[784,128]{1,0:T(8,128)(2,1)S(1)} %collective-permute-done.4.refs_0_.refs_4_), channel_id=1, source_target_pairs={{0,2},{1,3},{4,0},{5,1},{8,4},{9,5},{12,8},{13,9},{14,12},{15,13},... | collective-permute-start | bytes 602120 | tf_op jit(solution)/shard_map/ppermute | solution.py:329
  21.4 9.4 %collective-permute-start.9 = (bf16[784,128]{1,0:T(8,128)(2,1)S(1)}, bf16[784,128]{1,0:T(8,128)(2,1)S(1)}, u32[]{:S(2)}, u32[]{:S(2)}) collective-permute-start(bf16[784,128]{1,0:T(8,128)(2,1)S(1)} %collective-permute-done.5.refs_1_.refs_5_), channel_id=1, source_target_pairs={{0,4},{1,5},{4,8},{5,9},{8,12},{9,13},{12,14},{13,15},{14,10},{15,... | collective-permute-start | bytes 602120 | tf_op jit(solution)/shard_map/ppermute | solution.py:329
  26.5 7.7 %collective-permute-start.12 = (bf16[768,128]{1,0:T(8,128)(2,1)S(1)}, bf16[768,128]{1,0:T(8,128)(2,1)S(1)}, u32[]{:S(2)}, u32[]{:S(2)}) collective-permute-start(bf16[768,128]{1,0:T(8,128)(2,1)S(1)} %collective-permute-done.10.refs_2_), channel_id=1, source_target_pairs={{0,2},{1,3},{4,0},{5,1},{8,4},{9,5},{12,8},{13,9},{14,12},{15,13},... | collective-permute-start | bytes 589832 | tf_op jit(solution)/shard_map/ppermute | solution.py:329
  28.1 7.4 %collective-permute-start.13 = (bf16[768,128]{1,0:T(8,128)(2,1)S(1)}, bf16[768,128]{1,0:T(8,128)(2,1)S(1)}, u32[]{:S(2)}, u32[]{:S(2)}) collective-permute-start(bf16[768,128]{1,0:T(8,128)(2,1)S(1)} %collective-permute-done.11.refs_3_), channel_id=1, source_target_pairs={{0,4},{1,5},{4,8},{5,9},{8,12},{9,13},{12,14},{13,15},{14,10},{15,... | collective-permute-start | bytes 589832 | tf_op jit(solution)/shard_map/ppermute | solution.py:329
  29.2 7.5 %collective-permute-start.14 = (bf16[784,128]{1,0:T(8,128)(2,1)S(1)}, bf16[784,128]{1,0:T(8,128)(2,1)S(1)}, u32[]{:S(2)}, u32[]{:S(2)}) collective-permute-start(bf16[784,128]{1,0:T(8,128)(2,1)S(1)} %collective-permute-done.8.refs_0_), channel_id=1, source_target_pairs={{0,2},{1,3},{4,0},{5,1},{8,4},{9,5},{12,8},{13,9},{14,12},{15,13},... | collective-permute-start | bytes 602120 | tf_op jit(solution)/shard_map/ppermute | solution.py:329
  30.8 6.8 %collective-permute-start.15 = (bf16[784,128]{1,0:T(8,128)(2,1)S(1)}, bf16[784,128]{1,0:T(8,128)(2,1)S(1)}, u32[]{:S(2)}, u32[]{:S(2)}) collective-permute-start(bf16[784,128]{1,0:T(8,128)(2,1)S(1)} %collective-permute-done.9.refs_1_), channel_id=1, source_target_pairs={{0,4},{1,5},{4,8},{5,9},{8,12},{9,13},{12,14},{13,15},{14,10},{15,... | collective-permute-start | bytes 602120 | tf_op jit(solution)/shard_map/ppermute | solution.py:329
  36.8 2.5 %collective-permute-start.16 = (bf16[2576,128]{1,0:T(8,128)(2,1)S(1)}, bf16[2576,128]{1,0:T(8,128)(2,1)S(1)}, u32[]{:S(2)}, u32[]{:S(2)}) collective-permute-start(bf16[2576,128]{1,0:T(8,128)(2,1)S(1)} %shard_map.65), channel_id=1, source_target_pairs={{0,1},{1,0},{2,3},{3,2},{4,5},{5,4},{6,7},{7,6},{8,9},{9,8},{10,11... | collective-permute-start | bytes 1978376 | tf_op jit(solution)/shard_map/ppermute | solution.py:329
  37.6 1.6 %collective-permute-start.17 = (bf16[784,128]{1,0:T(8,128)(2,1)S(1)}, bf16[784,128]{1,0:T(8,128)(2,1)S(1)}, u32[]{:S(2)}, u32[]{:S(2)}) collective-permute-start(bf16[784,128]{1,0:T(8,128)(2,1)S(1)} %collective-permute-done.15.refs_1_), channel_id=1, source_target_pairs={{0,1},{1,0},{2,3},{3,2},{4,5},{5,4},{6,7},{7,6},{8,9},{9,8},{10,11... | collective-permute-start | bytes 602120 | tf_op jit(solution)/shard_map/ppermute | solution.py:329

commit v6 on v4

--- a/solution.py
+++ b/solution.py
@@ -14,7 +14,6 @@
 SPLIT = 128.0
 TAIL = 16
 VMEM_LIMIT = 16 * 1024 * 1024
-PARTS = 2
 WEIGHT = 20
 
 
@@ -52,27 +51,26 @@
     )
 
 
-def prep_body(parts, emb_hbm, pos_hbm, a_ref, b_ref, ah_ref, bh_ref, emb_ref, pos_ref, sem):
-    half = pos_ref.shape[1]
-    rows, width = emb_ref.shape
-    size = rows // parts
+def prep_body(sizes, emb_hbm, pos_hbm, a_ref, b_ref, ah_ref, bh_ref, emb_ref, pos_ref, sem):
+    width = emb_ref.shape[1]
+    starts = (0, sizes[0])
     fetch = []
-    for i in range(parts):
-        part = pl.ds(i * size, size)
+    for i, (first, size) in enumerate(zip(starts, sizes)):
+        part = pl.ds(first, size)
         fetch.append(pltpu.make_async_copy(emb_hbm.at[part], emb_ref.at[part], sem.at[i]))
-    last = pltpu.make_async_copy(pos_hbm, pos_ref, sem.at[parts])
+    last = pltpu.make_async_copy(pos_hbm, pos_ref, sem.at[2])
     for copy in (*fetch, last):
         copy.start()
     for i, copy in enumerate(fetch):
         copy.wait()
-        first = i * size
-        whole, alone = (a_ref, ah_ref) if first < half else (b_ref, bh_ref)
+        first, size = starts[i], sizes[i]
+        whole, alone = (a_ref, ah_ref) if i == 0 else (b_ref, bh_ref)
         emb = emb_ref[first : first + size, :]
         unit = emb * lax.rsqrt(jnp.sum(emb * emb, axis=1, keepdims=True) + EPS)
         unit = unit.astype(jnp.bfloat16)
         for at in range(0, width, LANES):
             panel = unit[:, at : at + LANES]
-            row = at // LANES * half + first % half
+            row = at // LANES * size
             alone[row : row + size] = panel
             whole[row : row + size] = panel
     last.wait()
@@ -80,20 +78,21 @@
     high = jnp.floor(pos * (1.0 / SPLIT))
     low = pos - high * SPLIT
     tail = jnp.concatenate(
-        [high[0:1], low[0:1], high[1:2], low[1:2], jnp.zeros((TAIL - 4, half), jnp.float32)],
+        [high[0:1], low[0:1], high[1:2], low[1:2], jnp.zeros((TAIL - 4, LANES), jnp.float32)],
         axis=0,
     ).astype(jnp.bfloat16)
     for ref in (a_ref, b_ref):
-        ref[width // LANES * half :] = tail
-
-
-def rows_of(ref, half):
-    panels = ref.shape[0] // half
-    return jnp.concatenate([ref[i * half : (i + 1) * half] for i in range(panels)], axis=1)
-
-
-def positions_of(ref, half):
-    tail = ref[ref.shape[0] // half * half :].astype(jnp.float32)
+        ref[ref.shape[0] - TAIL :] = tail
+
+
+def rows_of(ref, width):
+    panels = width // LANES
+    size = ref.shape[0] // panels // 16 * 16
+    return jnp.concatenate([ref[i * size : (i + 1) * size] for i in range(panels)], axis=1)
+
+
+def positions_of(ref):
+    tail = ref[ref.shape[0] - TAIL :].astype(jnp.float32)
     return [tail[2 * i : 2 * i + 1] * SPLIT + tail[2 * i + 1 : 2 * i + 2] for i in range(2)]
 
 
@@ -178,18 +177,16 @@
     out_ref[:, width:] = top.astype(out_ref.dtype)
 
 
-def first_body(half, clusters, len_ref, mask_hbm, a_ref, b_ref, sa_ref, sb_ref,
+def first_body(rows, width, clusters, len_ref, mask_hbm, a_ref, b_ref, sa_ref, sb_ref,
                f_ref, g_ref, own_ref, sib_ref, info_ref, feat_ref, ends_ref, mask_ref, sem):
     fetch = pltpu.make_async_copy(mask_hbm, mask_ref, sem.at[0])
     fetch.start()
     ends = ends_of(len_ref, clusters)
-    own = positions_of(a_ref, half)
-    sib = positions_of(sa_ref, half)
+    own = positions_of(a_ref)
+    sib = positions_of(sa_ref)
     pos = jnp.concatenate([column(r) for r in own + sib], axis=0)
     index, start = cluster_parts(pos, ends, clusters)
     count = mask_ref.shape[0]
-    rows = 2 * half
-    width = a_ref.shape[0] // half * LANES
     block = jnp.floor(pos * (1.0 / rows)).astype(jnp.int32)
     total = pos.shape[0]
     onehot = (block == lax.broadcasted_iota(jnp.int32, (total, count), 1)).astype(jnp.bfloat16)
@@ -208,9 +205,9 @@
     feat_ref[...] = feat
     info_ref[0] = jnp.broadcast_to(pos, (total, LANES))
     info_ref[1] = jnp.broadcast_to(start, (total, LANES))
-    keys = jnp.concatenate([rows_of(r, half) for r in (a_ref, b_ref)], axis=0)
+    keys = jnp.concatenate([rows_of(r, width) for r in (a_ref, b_ref)], axis=0)
     blocks = [(keys, jnp.concatenate(own, axis=1))]
-    blocks += gather_keys((f_ref, g_ref), (((0, 0, 0), (1, 1, 1)),), half)
+    blocks += gather_keys((f_ref, g_ref), ((0, 0, 1, 1),), width)
     state = jnp.concatenate(
         [jnp.zeros((rows, width), jnp.float32), jnp.full((rows, LANES), -1.0, jnp.float32)],
         axis=1,
@@ -222,43 +219,43 @@
     )
     fold(rows, width, state, own_ref, keys, info_ref[:, :rows], feat[:rows], blocks, ends,
          clusters, True)
-    other = jnp.concatenate([rows_of(r, half) for r in (sa_ref, sb_ref)], axis=0)
+    other = jnp.concatenate([rows_of(r, width) for r in (sa_ref, sb_ref)], axis=0)
     fold(rows, width, state, sib_ref, other, info_ref[:, rows:], feat[rows:], blocks, ends,
          clusters)
 
 
-def gather_keys(key_refs, groups, half):
+def gather_keys(key_refs, groups, width):
     out = []
     for group in groups:
-        keys = jnp.concatenate([rows_of(key_refs[r], half) for r, _, _ in group], axis=0)
-        pos = jnp.concatenate(
-            [positions_of(key_refs[p], half)[w] for _, p, w in group], axis=1
-        )
-        out.append((keys, pos))
+        first, second = [rows_of(key_refs[r], width) for r in group[::2]]
+        pos = [jnp.concatenate(positions_of(key_refs[p]), axis=1) for p in group[1::2]]
+        lane = lax.broadcasted_iota(jnp.int32, pos[0].shape, 1)
+        out.append((
+            jnp.concatenate([first, second], axis=0),
+            jnp.where(lane < first.shape[0], pos[0], pos[1]),
+        ))
     return out
 
 
-def middle_body(half, clusters, groups, ends_ref, info_ref, feat_ref, a_ref, b_ref, sa_ref,
+def middle_body(rows, width, clusters, groups, ends_ref, info_ref, feat_ref, a_ref, b_ref, sa_ref,
                 sb_ref, own_in, sib_in, *refs):
     key_refs, (own_ref, sib_ref) = refs[:-2], refs[-2:]
     ends = [ends_ref[c : c + 1, :] for c in range(clusters - 1)]
-    rows, width = 2 * half, a_ref.shape[0] // half * LANES
-    blocks = gather_keys(key_refs, groups, half)
+    blocks = gather_keys(key_refs, groups, width)
     for i, state_in, state_out, pair in (
         (0, own_in, own_ref, (a_ref, b_ref)), (1, sib_in, sib_ref, (sa_ref, sb_ref))
     ):
-        query = jnp.concatenate([rows_of(r, half) for r in pair], axis=0)
+        query = jnp.concatenate([rows_of(r, width) for r in pair], axis=0)
         part = slice(i * rows, (i + 1) * rows)
         fold(rows, width, state_in[...], state_out, query, info_ref[:, part], feat_ref[part],
              blocks, ends, clusters)
 
 
-def late_body(half, clusters, ends_ref, info_ref, feat_ref, a_ref, b_ref, own_in, *refs):
+def late_body(rows, width, clusters, ends_ref, info_ref, feat_ref, a_ref, b_ref, own_in, *refs):
     key_refs, own_ref = refs[:-1], refs[-1]
     ends = [ends_ref[c : c + 1, :] for c in range(clusters - 1)]
-    rows, width = 2 * half, a_ref.shape[0] // half * LANES
-    blocks = gather_keys(key_refs, (((0, 0, 0), (1, 1, 1)),), half)
-    query = jnp.concatenate([rows_of(r, half) for r in (a_ref, b_ref)], axis=0)
+    blocks = gather_keys(key_refs, ((0, 0, 1, 1),), width)
+    query = jnp.concatenate([rows_of(r, width) for r in (a_ref, b_ref)], axis=0)
     fold(rows, width, own_in[...], own_ref, query, info_ref[:, :rows], feat_ref[:rows],
          blocks, ends, clusters)
 
@@ -271,23 +268,23 @@
     out_ref[panels * rows : panels * rows + f_ref.shape[0]] = f_ref[...]
 
 
-def last_body(half, clusters, ends_ref, info_ref, feat_ref, a_ref, b_ref, own_in, got_ref,
+def last_body(rows, width, clusters, ends_ref, info_ref, feat_ref, a_ref, b_ref, own_in, got_ref,
               far_ref, dir_ref, out_top):
     ends = [ends_ref[c : c + 1, :] for c in range(clusters - 1)]
-    rows, width = 2 * half, a_ref.shape[0] // half * LANES
-    query = jnp.concatenate([rows_of(r, half) for r in (a_ref, b_ref)], axis=0)
+    query = jnp.concatenate([rows_of(r, width) for r in (a_ref, b_ref)], axis=0)
     panels = width // LANES
     parts = [got_ref[i * rows : (i + 1) * rows].astype(jnp.float32) for i in range(panels + 1)]
     acc = own_in[:, :width] + jnp.concatenate(parts[:panels], axis=1)
     top = jnp.maximum(own_in[:, width:], jnp.sum(parts[panels], axis=1, keepdims=True))
     key_refs = [got_ref.at[pl.ds((panels + 1) * rows, a_ref.shape[0])], far_ref]
-    for keys, pos in gather_keys(key_refs, (((0, 0, 0), (1, 1, 1)),), half):
+    for keys, pos in gather_keys(key_refs, ((0, 0, 1, 1),), width):
         acc, top = attend(
             rows, query, info_ref[0, :rows], info_ref[1, :rows], feat_ref[:rows], acc, top, keys,
             pos, ends, clusters, False,
         )
     scale = math.sqrt(width) * lax.rsqrt(jnp.sum(acc * acc, axis=1, keepdims=True) + EPS)
     dir_ref[...] = (acc * scale).astype(jnp.bfloat16)
+    half = rows // 2
     best = jnp.max(top, axis=1, keepdims=True)
     eye = lax.broadcasted_iota(jnp.int32, (half, half), 0) == lax.broadcasted_iota(
         jnp.int32, (half, half), 1
@@ -325,15 +322,17 @@
     def f32(*s):
         return jax.ShapeDtypeStruct(s, jnp.float32)
 
-    full = width // LANES * half + TAIL
+    sizes = (rows // 2, rows - rows // 2)
+    alone = [width // LANES * n for n in sizes]
+    full = alone[0] + TAIL
     wide = width + LANES
     state = f32(rows, wide)
     a, b, ah, bh = call(
-        functools.partial(prep_body, PARTS),
-        [bf(full, LANES)] * 2 + [bf(full - TAIL, LANES)] * 2, [HB, HB],
+        functools.partial(prep_body, sizes),
+        [bf(n + TAIL, LANES) for n in alone] + [bf(n, LANES) for n in alone], [HB, HB],
         scratch=[
             pltpu.VMEM((rows, width), jnp.float32), pltpu.VMEM((2, half), jnp.int32),
-            pltpu.SemaphoreType.DMA((PARTS + 1,)),
+            pltpu.SemaphoreType.DMA((3,)),
         ],
     )(in_hbm(embeddings), in_hbm(dest_pos.reshape(2, half)))
 
@@ -342,7 +341,7 @@
     sa, sb = move(a, sibling), move(b, sibling)
     work = 8 * rows * rows * width * WEIGHT
     own, sib, info, feat, ends = call(
-        functools.partial(first_body, half, clusters),
+        functools.partial(first_body, rows, width, clusters),
         [state, state, f32(2, 2 * rows, LANES), bf(2 * rows, count * clusters),
          f32(-(-clusters // 8) * 8, rows)],
         [SM, HB] + [VM] * 6, work,
@@ -351,23 +350,23 @@
 
     def middle(own, sib, keys, groups, work, sent=state):
         return call(
-            functools.partial(middle_body, half, clusters, groups), [state, sent],
+            functools.partial(middle_body, rows, width, clusters, groups), [state, sent],
             [VM] * (9 + len(keys)), work, aliases={7: 0, 8: 1} if sent is state else {7: 0},
         )(ends, info, feat, a, b, sa, sb, own, sib, *keys)
 
-    both = ((0, 0, 0), (1, 1, 1))
+    both = (0, 0, 1, 1)
     for step in range(1, steps):
         f, g = lead[-1]
         lead.append((move(f, ahead), move(g, back)))
         if step > 1:
             own, sib = middle(
-                own, sib, (*lead[-2], *follow[-2], *lead[-3]), (((2, 4, 1), (3, 5, 0)), both),
+                own, sib, (*lead[-2], *follow[-2], *lead[-3]), ((3, 5, 2, 4), both),
                 work,
             )
         if step < steps - 1:
             f, g = follow[-1]
             follow.append((move(after(f, own), ahead), move(after(g, own), back)))
-    own, sib = middle(own, sib, (*lead[-2], *follow[-1]), (((2, 0, 1), (3, 1, 0)),), 1,
+    own, sib = middle(own, sib, (*lead[-2], *follow[-1]), ((3, 1, 2, 0),), 1,
                       bf(rows, wide))
     stacked = wide // LANES * rows + -(-full // 16) * 16
     joined = call(join_body, [bf(stacked, LANES)], [VM, VM])(sib, lead[-1][0])[0]
@@ -375,10 +374,10 @@
     far = move(after(lead[-1][1], own), sibling)
     shared = (ends, info, feat, a, b)
     own = call(
-        functools.partial(late_body, half, clusters), [state], [VM] * 8, work, aliases={5: 0},
+        functools.partial(late_body, rows, width, clusters), [state], [VM] * 8, work, aliases={5: 0},
     )(*shared, own, *lead[-1])[0]
     out_dir, out_top = call(
-        functools.partial(last_body, half, clusters),
+        functools.partial(last_body, rows, width, clusters),
         [bf(rows), f32(2, half)], [VM] * 8,
     )(*shared, own, got, far)
     return out_top.reshape(rows), out_dir

time: 40.9 us -> 40.9 us (level)
  no operation moved by 1% of the time
where the time goes in v6:
time: 40.9 us; the launch traced here: 40.8 us
  starting transfers between devices  15.5 us (38%)
  waiting for transfers between devices  13.4 us (33%)
  Pallas kernels  11.1 us (27%)
  between operations  0.73 us (2%)
    ppermute x18, starting transfers between devices, move(): return lax.ppermute(x, 'blk', perm)  15.5 us
    ppermute x18, waiting for transfers between devices, move(): return lax.ppermute(x, 'blk', perm)  13.4 us
    pallas_call x3, Pallas kernels, middle(): call(functools.partial(middle_body, rows, width, clusters, groups), [stat...  4.73 us
    pallas_call x1, Pallas kernels, per_device(): call(functools.partial(first_body, rows, width, clusters), [state, state,...  2.77 us
    pallas_call x1, Pallas kernels, per_device(): call(functools.partial(last_body, rows, width, clusters), [bf(rows), f32(...  1.51 us
    pallas_call x1, Pallas kernels, per_device(): call(functools.partial(prep_body, sizes), [bf(n + TAIL, LANES) for n in a...  1.28 us
  transfers between devices with their start and end apart: 18, of which 10 were waited for; matrix products, arithmetic and copies ran while one was open for 0% of the time, Pallas kernels for 20%

profile of v6, /device:TPU:0, one launch (start us, length us, event | category | flops | bytes accessed | tf_op | source)
XLA Modules:
  0.0 40.8 jit_solution(3847538218638657427)
XLA Ops:
  0.6 1.3 %shard_map.59 = (bf16[784,128]{1,0:T(8,128)(2,1)S(1)}, bf16[784,128]{1,0:T(8,128)(2,1)S(1)}, bf16[768,128]{1,0:T(8,128)(2,1)S(1)}, bf16[768,128]{1,0:T(8,128)(2,1)S(1)}) custom-call(f32[256,768]{1,0:T(8,128)} %emb_hbm.1, s32[2,128]{1,0:T(2,128)} %bitcast.2), custom_call_target="tpu_custom_call" | custom-call | flops 1 | bytes 1 | tf_op jit(solution)/shard_map/pallas_call | solution.py:330
  1.9 0.5 %collective-permute-start = (bf16[784,128]{1,0:T(8,128)(2,1)S(1)}, bf16[784,128]{1,0:T(8,128)(2,1)S(1)}, u32[]{:S(2)}, u32[]{:S(2)}) collective-permute-start(bf16[784,128]{1,0:T(8,128)(2,1)S(1)} %get-tuple-element.24.a_ref), channel_id=1, source_target_pairs={{0,1},{1,0},{2,3},{3,2},{4,5},{5,4},{6,7},{7,6},{8,9},{9,8},{10,11... | collective-permute-start | bytes 602120 | tf_op jit(solution)/shard_map/ppermute | solution.py:317
  2.4 2.6 %collective-permute-start.2 = (bf16[784,128]{1,0:T(8,128)(2,1)S(1)}, bf16[784,128]{1,0:T(8,128)(2,1)S(1)}, u32[]{:S(2)}, u32[]{:S(2)}) collective-permute-start(bf16[784,128]{1,0:T(8,128)(2,1)S(1)} %get-tuple-element.24.a_ref), channel_id=1, source_target_pairs={{0,2},{1,3},{4,0},{5,1},{8,4},{9,5},{12,8},{13,9},{14,12},{15,13},... | collective-permute-start | bytes 602120 | tf_op jit(solution)/shard_map/ppermute | solution.py:317
  5.0 0.1 collective-permute-start.3
  5.3 1.9 %collective-permute-start.7 = (bf16[768,128]{1,0:T(8,128)(2,1)S(1)}, bf16[768,128]{1,0:T(8,128)(2,1)S(1)}, u32[]{:S(2)}, u32[]{:S(2)}) collective-permute-start(bf16[768,128]{1,0:T(8,128)(2,1)S(1)} %get-tuple-element.32), channel_id=1, source_target_pairs={{0,4},{1,5},{4,8},{5,9},{8,12},{9,13},{12,14},{13,15},{14,10},{15,... | collective-permute-start | bytes 589832 | tf_op jit(solution)/shard_map/ppermute | solution.py:317
  7.1 0.2 collective-permute-start.6
  7.3 3.6 %collective-permute-done.2.f_ref.refs_4_ = bf16[784,128]{1,0:T(8,128)(2,1)S(1)} collective-permute-done((bf16[784,128]{1,0:T(8,128)(2,1)S(1)}, bf16[784,128]{1,0:T(8,128)(2,1)S(1)}, u32[]{:S(2)}, u32[]{:S(2)}) %collective-permute-start.2) | collective-permute-done | bytes 200736 | tf_op jit(solution)/shard_map/ppermute | solution.py:317
  10.9 1.9 %collective-permute-start.4 = (bf16[784,128]{1,0:T(8,128)(2,1)S(1)}, bf16[784,128]{1,0:T(8,128)(2,1)S(1)}, u32[]{:S(2)}, u32[]{:S(2)}) collective-permute-start(bf16[784,128]{1,0:T(8,128)(2,1)S(1)} %collective-permute-done.2.f_ref.refs_4_), channel_id=1, source_target_pairs={{0,2},{1,3},{4,0},{5,1},{8,4},{9,5},{12,8},{13,9},{14,12},{15,13},... | collective-permute-start | bytes 602120 | tf_op jit(solution)/shard_map/ppermute | solution.py:317
  12.9 0.1 collective-permute-start.5
  13.0 2.8 %shard_map.60 = (f32[256,896]{1,0:T(8,128)S(1)}, f32[256,896]{1,0:T(8,128)S(1)}, f32[2,512,128]{2,1,0:T(8,128)S(1)}, bf16[512,64]{1,0:T(8,128)(2,1)S(1)}, f32[8,256]{1,0:T(8,128)S(1)}) custom-call(s32[4]{0:T(128)S(1)} %copy-done.1, s32[16,16]{1,0:T(8,128)S(1)} %copy-done, bf16[784,128]{1,0:T(8,128)(2,1)S(1)} %get-tuple-element.24.a_ref, ...), custom_call_target="tpu_custom_call" | custom-call | flops 8053063680 | bytes 1 | tf_op jit(solution)/shard_map/pallas_call | solution.py:343
  15.8 1.3 %collective-permute-done.7.refs_3_ = bf16[768,128]{1,0:T(8,128)(2,1)S(1)} collective-permute-done((bf16[768,128]{1,0:T(8,128)(2,1)S(1)}, bf16[768,128]{1,0:T(8,128)(2,1)S(1)}, u32[]{:S(2)}, u32[]{:S(2)}) %collective-permute-start.7) | collective-permute-done | bytes 196640 | tf_op jit(solution)/shard_map/ppermute | solution.py:317
  17.1 1.6 %collective-permute-start.10 = (bf16[768,128]{1,0:T(8,128)(2,1)S(1)}, bf16[768,128]{1,0:T(8,128)(2,1)S(1)}, u32[]{:S(2)}, u32[]{:S(2)}) collective-permute-start(bf16[768,128]{1,0:T(8,128)(2,1)S(1)} %collective-permute-done.6.refs_2_), channel_id=1, source_target_pairs={{0,2},{1,3},{4,0},{5,1},{8,4},{9,5},{12,8},{13,9},{14,12},{15,13},... | collective-permute-start | bytes 589832 | tf_op jit(solution)/shard_map/ppermute | solution.py:317
  18.7 0.4 %collective-permute-start.11 = (bf16[768,128]{1,0:T(8,128)(2,1)S(1)}, bf16[768,128]{1,0:T(8,128)(2,1)S(1)}, u32[]{:S(2)}, u32[]{:S(2)}) collective-permute-start(bf16[768,128]{1,0:T(8,128)(2,1)S(1)} %collective-permute-done.7.refs_3_), channel_id=1, source_target_pairs={{0,4},{1,5},{4,8},{5,9},{8,12},{9,13},{12,14},{13,15},{14,10},{15,... | collective-permute-start | bytes 589832 | tf_op jit(solution)/shard_map/ppermute | solution.py:317
  19.1 0.3 collective-permute-done.4.refs_0_.refs_4_
  19.4 1.9 %collective-permute-start.8 = (bf16[784,128]{1,0:T(8,128)(2,1)S(1)}, bf16[784,128]{1,0:T(8,128)(2,1)S(1)}, u32[]{:S(2)}, u32[]{:S(2)}) collective-permute-start(bf16[784,128]{1,0:T(8,128)(2,1)S(1)} %collective-permute-done.4.refs_0_.refs_4_), channel_id=1, source_target_pairs={{0,2},{1,3},{4,0},{5,1},{8,4},{9,5},{12,8},{13,9},{14,12},{15,13},... | collective-permute-start | bytes 602120 | tf_op jit(solution)/shard_map/ppermute | solution.py:317
  21.4 0.1 collective-permute-start.9
  21.5 1.8 %shard_map.61 = (f32[256,896]{1,0:T(8,128)S(1)}, f32[256,896]{1,0:T(8,128)S(1)}) custom-call(f32[8,256]{1,0:T(8,128)S(1)} %get-tuple-element.26.ends_ref, f32[2,512,128]{2,1,0:T(8,128)S(1)} %get-tuple-element.27.info_ref, bf16[512,64]{1,0:T(8,128)(2,1)S(1)} %get-tuple-element.28.feat_ref, ...), custom_call_target="tpu_custom_call", output_to_operand_aliasing={{0}: (7, {}), {1}: (8, {})} | custom-call | flops 8053063680 | bytes 1 | tf_op jit(solution)/shard_map/pallas_call | solution.py:352
  23.2 1.7 %collective-permute-done.10.refs_2_ = bf16[768,128]{1,0:T(8,128)(2,1)S(1)} collective-permute-done((bf16[768,128]{1,0:T(8,128)(2,1)S(1)}, bf16[768,128]{1,0:T(8,128)(2,1)S(1)}, u32[]{:S(2)}, u32[]{:S(2)}) %collective-permute-start.10) | collective-permute-done | bytes 196640 | tf_op jit(solution)/shard_map/ppermute | solution.py:317
  24.9 1.6 %collective-permute-done.11.refs_3_ = bf16[768,128]{1,0:T(8,128)(2,1)S(1)} collective-permute-done((bf16[768,128]{1,0:T(8,128)(2,1)S(1)}, bf16[768,128]{1,0:T(8,128)(2,1)S(1)}, u32[]{:S(2)}, u32[]{:S(2)}) %collective-permute-start.11) | collective-permute-done | bytes 196640 | tf_op jit(solution)/shard_map/ppermute | solution.py:317
  26.5 1.6 %collective-permute-start.12 = (bf16[768,128]{1,0:T(8,128)(2,1)S(1)}, bf16[768,128]{1,0:T(8,128)(2,1)S(1)}, u32[]{:S(2)}, u32[]{:S(2)}) collective-permute-start(bf16[768,128]{1,0:T(8,128)(2,1)S(1)} %collective-permute-done.10.refs_2_), channel_id=1, source_target_pairs={{0,2},{1,3},{4,0},{5,1},{8,4},{9,5},{12,8},{13,9},{14,12},{15,13},... | collective-permute-start | bytes 589832 | tf_op jit(solution)/shard_map/ppermute | solution.py:317
  28.1 0.4 %collective-permute-start.13 = (bf16[768,128]{1,0:T(8,128)(2,1)S(1)}, bf16[768,128]{1,0:T(8,128)(2,1)S(1)}, u32[]{:S(2)}, u32[]{:S(2)}) collective-permute-start(bf16[768,128]{1,0:T(8,128)(2,1)S(1)} %collective-permute-done.11.refs_3_), channel_id=1, source_target_pairs={{0,4},{1,5},{4,8},{5,9},{8,12},{9,13},{12,14},{13,15},{14,10},{15,... | collective-permute-start | bytes 589832 | tf_op jit(solution)/shard_map/ppermute | solution.py:317
  28.5 0.7 %collective-permute-done.8.refs_0_ = bf16[784,128]{1,0:T(8,128)(2,1)S(1)} collective-permute-done((bf16[784,128]{1,0:T(8,128)(2,1)S(1)}, bf16[784,128]{1,0:T(8,128)(2,1)S(1)}, u32[]{:S(2)}, u32[]{:S(2)}) %collective-permute-start.8) | collective-permute-done | bytes 200736 | tf_op jit(solution)/shard_map/ppermute | solution.py:317
  29.2 1.6 %collective-permute-start.14 = (bf16[784,128]{1,0:T(8,128)(2,1)S(1)}, bf16[784,128]{1,0:T(8,128)(2,1)S(1)}, u32[]{:S(2)}, u32[]{:S(2)}) collective-permute-start(bf16[784,128]{1,0:T(8,128)(2,1)S(1)} %collective-permute-done.8.refs_0_), channel_id=1, source_target_pairs={{0,2},{1,3},{4,0},{5,1},{8,4},{9,5},{12,8},{13,9},{14,12},{15,13},... | collective-permute-start | bytes 602120 | tf_op jit(solution)/shard_map/ppermute | solution.py:317
  30.8 0.4 %collective-permute-start.15 = (bf16[784,128]{1,0:T(8,128)(2,1)S(1)}, bf16[784,128]{1,0:T(8,128)(2,1)S(1)}, u32[]{:S(2)}, u32[]{:S(2)}) collective-permute-start(bf16[784,128]{1,0:T(8,128)(2,1)S(1)} %collective-permute-done.9.refs_1_), channel_id=1, source_target_pairs={{0,4},{1,5},{4,8},{5,9},{8,12},{9,13},{12,14},{13,15},{14,10},{15,... | collective-permute-start | bytes 602120 | tf_op jit(solution)/shard_map/ppermute | solution.py:317
  31.2 1.8 %shard_map.62 = (f32[256,896]{1,0:T(8,128)S(1)}, f32[256,896]{1,0:T(8,128)S(1)}) custom-call(f32[8,256]{1,0:T(8,128)S(1)} %get-tuple-element.26.ends_ref, f32[2,512,128]{2,1,0:T(8,128)S(1)} %get-tuple-element.27.info_ref, bf16[512,64]{1,0:T(8,128)(2,1)S(1)} %get-tuple-element.28.feat_ref, ...), custom_call_target="tpu_custom_call", output_to_operand_aliasing={{0}: (7, {}), {1}: (8, {})} | custom-call | flops 8053063680 | bytes 1 | tf_op jit(solution)/shard_map/pallas_call | solution.py:352
  33.0 1.2 %collective-permute-done.12.refs_2_ = bf16[768,128]{1,0:T(8,128)(2,1)S(1)} collective-permute-done((bf16[768,128]{1,0:T(8,128)(2,1)S(1)}, bf16[768,128]{1,0:T(8,128)(2,1)S(1)}, u32[]{:S(2)}, u32[]{:S(2)}) %collective-permute-start.12) | collective-permute-done | bytes 196640 | tf_op jit(solution)/shard_map/ppermute | solution.py:317
  34.2 1.3 %collective-permute-done.13.refs_3_ = bf16[768,128]{1,0:T(8,128)(2,1)S(1)} collective-permute-done((bf16[768,128]{1,0:T(8,128)(2,1)S(1)}, bf16[768,128]{1,0:T(8,128)(2,1)S(1)}, u32[]{:S(2)}, u32[]{:S(2)}) %collective-permute-start.13) | collective-permute-done | bytes 196640 | tf_op jit(solution)/shard_map/ppermute | solution.py:317
  35.5 1.2 %shard_map.63 = (f32[256,896]{1,0:T(8,128)S(1)}, bf16[256,896]{1,0:T(8,128)(2,1)S(1)}) custom-call(f32[8,256]{1,0:T(8,128)S(1)} %get-tuple-element.26.ends_ref, f32[2,512,128]{2,1,0:T(8,128)S(1)} %get-tuple-element.27.info_ref, bf16[512,64]{1,0:T(8,128)(2,1)S(1)} %get-tuple-element.28.feat_ref, ...), custom_call_target="tpu_custom_call", output_to_operand_aliasing={{0}: (7, {})} | custom-call | flops 1 | bytes 1 | tf_op jit(solution)/shard_map/pallas_call | solution.py:352
  36.9 0.7 %collective-permute-done.15.refs_1_ = bf16[784,128]{1,0:T(8,128)(2,1)S(1)} collective-permute-done((bf16[784,128]{1,0:T(8,128)(2,1)S(1)}, bf16[784,128]{1,0:T(8,128)(2,1)S(1)}, u32[]{:S(2)}, u32[]{:S(2)}) %collective-permute-start.15) | collective-permute-done | bytes 200736 | tf_op jit(solution)/shard_map/ppermute | solution.py:317
  37.6 0.7 %shard_map.64.own_in = f32[256,896]{1,0:T(8,128)S(1)} custom-call(f32[8,256]{1,0:T(8,128)S(1)} %get-tuple-element.26.ends_ref, f32[2,512,128]{2,1,0:T(8,128)S(1)} %get-tuple-element.27.info_ref, bf16[512,64]{1,0:T(8,128)(2,1)S(1)} %get-tuple-element.28.feat_ref, bf16[784,128]{1,0:T(8,128)(2,1)S(1)} %get-tuple-element.24.a_ref, ...), custom_call_target="tpu_custom_call", output_to_operand_aliasing={{}: (5, {})} | custom-call | flops 8053063680 | bytes 1 | tf_op jit(solution)/shard_map/pallas_call | solution.py:376
  38.4 0.9 %collective-permute-done.17.far_ref = bf16[784,128]{1,0:T(8,128)(2,1)S(1)} collective-permute-done((bf16[784,128]{1,0:T(8,128)(2,1)S(1)}, bf16[784,128]{1,0:T(8,128)(2,1)S(1)}, u32[]{:S(2)}, u32[]{:S(2)}) %collective-permute-start.17) | collective-permute-done | bytes 200736 | tf_op jit(solution)/shard_map/ppermute | solution.py:317
  39.3 1.5 %shard_map.66 = (bf16[256,768]{1,0:T(8,128)(2,1)}, f32[2,128]{1,0:T(2,128)}) custom-call(f32[8,256]{1,0:T(8,128)S(1)} %get-tuple-element.26.ends_ref, f32[2,512,128]{2,1,0:T(8,128)S(1)} %get-tuple-element.27.info_ref, bf16[512,64]{1,0:T(8,128)(2,1)S(1)} %get-tuple-element.28.feat_ref, bf16[784,128]{1,0:T(8,128)(2,1)S(1)} %get-tuple-element.24.a_ref, ...), custom_call_target="tpu_custom_call" | custom-call | flops 1 | bytes 1 | tf_op jit(solution)/shard_map/pallas_call | solution.py:379
  (16 shorter events, 0.4 us)
Async XLA Ops:
  0.6 12.4 %copy-start = (s32[16,16]{1,0:T(8,128)S(1)}, s32[16,16]{1,0:T(8,128)}, u32[]{:S(2)}) copy-start(s32[16,16]{1,0:T(8,128)} %mask_hbm.1) | copy-start | bytes 3076
  1.9 5.2 %collective-permute-start = (bf16[784,128]{1,0:T(8,128)(2,1)S(1)}, bf16[784,128]{1,0:T(8,128)(2,1)S(1)}, u32[]{:S(2)}, u32[]{:S(2)}) collective-permute-start(bf16[784,128]{1,0:T(8,128)(2,1)S(1)} %get-tuple-element.24.a_ref), channel_id=1, source_target_pairs={{0,1},{1,0},{2,3},{3,2},{4,5},{5,4},{6,7},{7,6},{8,9},{9,8},{10,11... | collective-permute-start | bytes 602120 | tf_op jit(solution)/shard_map/ppermute | solution.py:317
  2.4 8.5 %collective-permute-start.2 = (bf16[784,128]{1,0:T(8,128)(2,1)S(1)}, bf16[784,128]{1,0:T(8,128)(2,1)S(1)}, u32[]{:S(2)}, u32[]{:S(2)}) collective-permute-start(bf16[784,128]{1,0:T(8,128)(2,1)S(1)} %get-tuple-element.24.a_ref), channel_id=1, source_target_pairs={{0,2},{1,3},{4,0},{5,1},{8,4},{9,5},{12,8},{13,9},{14,12},{15,13},... | collective-permute-start | bytes 602120 | tf_op jit(solution)/shard_map/ppermute | solution.py:317
  5.0 7.8 %collective-permute-start.3 = (bf16[784,128]{1,0:T(8,128)(2,1)S(1)}, bf16[784,128]{1,0:T(8,128)(2,1)S(1)}, u32[]{:S(2)}, u32[]{:S(2)}) collective-permute-start(bf16[784,128]{1,0:T(8,128)(2,1)S(1)} %get-tuple-element.25.b_ref), channel_id=1, source_target_pairs={{0,4},{1,5},{4,8},{5,9},{8,12},{9,13},{12,14},{13,15},{14,10},{15,... | collective-permute-start | bytes 602120 | tf_op jit(solution)/shard_map/ppermute | solution.py:317
  5.2 7.8 %collective-permute-start.1 = (bf16[784,128]{1,0:T(8,128)(2,1)S(1)}, bf16[784,128]{1,0:T(8,128)(2,1)S(1)}, u32[]{:S(2)}, u32[]{:S(2)}) collective-permute-start(bf16[784,128]{1,0:T(8,128)(2,1)S(1)} %get-tuple-element.25.b_ref), channel_id=1, source_target_pairs={{0,1},{1,0},{2,3},{3,2},{4,5},{5,4},{6,7},{7,6},{8,9},{9,8},{10,11... | collective-permute-start | bytes 602120 | tf_op jit(solution)/shard_map/ppermute | solution.py:317
  5.3 7.7 %copy-start.1 = (s32[4]{0:T(128)S(1)}, s32[4]{0:T(128)}, u32[]{:S(2)}) copy-start(s32[4]{0:T(128)} %len_ref.1) | copy-start | bytes 52
  5.3 11.8 %collective-permute-start.7 = (bf16[768,128]{1,0:T(8,128)(2,1)S(1)}, bf16[768,128]{1,0:T(8,128)(2,1)S(1)}, u32[]{:S(2)}, u32[]{:S(2)}) collective-permute-start(bf16[768,128]{1,0:T(8,128)(2,1)S(1)} %get-tuple-element.32), channel_id=1, source_target_pairs={{0,4},{1,5},{4,8},{5,9},{8,12},{9,13},{12,14},{13,15},{14,10},{15,... | collective-permute-start | bytes 589832 | tf_op jit(solution)/shard_map/ppermute | solution.py:317
  7.1 10.0 %collective-permute-start.6 = (bf16[768,128]{1,0:T(8,128)(2,1)S(1)}, bf16[768,128]{1,0:T(8,128)(2,1)S(1)}, u32[]{:S(2)}, u32[]{:S(2)}) collective-permute-start(bf16[768,128]{1,0:T(8,128)(2,1)S(1)} %get-tuple-element.31), channel_id=1, source_target_pairs={{0,2},{1,3},{4,0},{5,1},{8,4},{9,5},{12,8},{13,9},{14,12},{15,13},... | collective-permute-start | bytes 589832 | tf_op jit(solution)/shard_map/ppermute | solution.py:317
  10.9 8.5 %collective-permute-start.4 = (bf16[784,128]{1,0:T(8,128)(2,1)S(1)}, bf16[784,128]{1,0:T(8,128)(2,1)S(1)}, u32[]{:S(2)}, u32[]{:S(2)}) collective-permute-start(bf16[784,128]{1,0:T(8,128)(2,1)S(1)} %collective-permute-done.2.f_ref.refs_4_), channel_id=1, source_target_pairs={{0,2},{1,3},{4,0},{5,1},{8,4},{9,5},{12,8},{13,9},{14,12},{15,13},... | collective-permute-start | bytes 602120 | tf_op jit(solution)/shard_map/ppermute | solution.py:317
  12.9 8.5 %collective-permute-start.5 = (bf16[784,128]{1,0:T(8,128)(2,1)S(1)}, bf16[784,128]{1,0:T(8,128)(2,1)S(1)}, u32[]{:S(2)}, u32[]{:S(2)}) collective-permute-start(bf16[784,128]{1,0:T(8,128)(2,1)S(1)} %collective-permute-done.3.g_ref.refs_5_), channel_id=1, source_target_pairs={{0,4},{1,5},{4,8},{5,9},{8,12},{9,13},{12,14},{13,15},{14,10},{15,... | collective-permute-start | bytes 602120 | tf_op jit(solution)/shard_map/ppermute | solution.py:317
  17.1 7.8 %collective-permute-start.10 = (bf16[768,128]{1,0:T(8,128)(2,1)S(1)}, bf16[768,128]{1,0:T(8,128)(2,1)S(1)}, u32[]{:S(2)}, u32[]{:S(2)}) collective-permute-start(bf16[768,128]{1,0:T(8,128)(2,1)S(1)} %collective-permute-done.6.refs_2_), channel_id=1, source_target_pairs={{0,2},{1,3},{4,0},{5,1},{8,4},{9,5},{12,8},{13,9},{14,12},{15,13},... | collective-permute-start | bytes 589832 | tf_op jit(solution)/shard_map/ppermute | solution.py:317
  18.7 7.8 %collective-permute-start.11 = (bf16[768,128]{1,0:T(8,128)(2,1)S(1)}, bf16[768,128]{1,0:T(8,128)(2,1)S(1)}, u32[]{:S(2)}, u32[]{:S(2)}) collective-permute-start(bf16[768,128]{1,0:T(8,128)(2,1)S(1)} %collective-permute-done.7.refs_3_), channel_id=1, source_target_pairs={{0,4},{1,5},{4,8},{5,9},{8,12},{9,13},{12,14},{13,15},{14,10},{15,... | collective-permute-start | bytes 589832 | tf_op jit(solution)/shard_map/ppermute | solution.py:317
  19.4 9.8 %collective-permute-start.8 = (bf16[784,128]{1,0:T(8,128)(2,1)S(1)}, bf16[784,128]{1,0:T(8,128)(2,1)S(1)}, u32[]{:S(2)}, u32[]{:S(2)}) collective-permute-start(bf16[784,128]{1,0:T(8,128)(2,1)S(1)} %collective-permute-done.4.refs_0_.refs_4_), channel_id=1, source_target_pairs={{0,2},{1,3},{4,0},{5,1},{8,4},{9,5},{12,8},{13,9},{14,12},{15,13},... | collective-permute-start | bytes 602120 | tf_op jit(solution)/shard_map/ppermute | solution.py:317
  21.4 9.4 %collective-permute-start.9 = (bf16[784,128]{1,0:T(8,128)(2,1)S(1)}, bf16[784,128]{1,0:T(8,128)(2,1)S(1)}, u32[]{:S(2)}, u32[]{:S(2)}) collective-permute-start(bf16[784,128]{1,0:T(8,128)(2,1)S(1)} %collective-permute-done.5.refs_1_.refs_5_), channel_id=1, source_target_pairs={{0,4},{1,5},{4,8},{5,9},{8,12},{9,13},{12,14},{13,15},{14,10},{15,... | collective-permute-start | bytes 602120 | tf_op jit(solution)/shard_map/ppermute | solution.py:317
  26.5 7.7 %collective-permute-start.12 = (bf16[768,128]{1,0:T(8,128)(2,1)S(1)}, bf16[768,128]{1,0:T(8,128)(2,1)S(1)}, u32[]{:S(2)}, u32[]{:S(2)}) collective-permute-start(bf16[768,128]{1,0:T(8,128)(2,1)S(1)} %collective-permute-done.10.refs_2_), channel_id=1, source_target_pairs={{0,2},{1,3},{4,0},{5,1},{8,4},{9,5},{12,8},{13,9},{14,12},{15,13},... | collective-permute-start | bytes 589832 | tf_op jit(solution)/shard_map/ppermute | solution.py:317
  28.1 7.4 %collective-permute-start.13 = (bf16[768,128]{1,0:T(8,128)(2,1)S(1)}, bf16[768,128]{1,0:T(8,128)(2,1)S(1)}, u32[]{:S(2)}, u32[]{:S(2)}) collective-permute-start(bf16[768,128]{1,0:T(8,128)(2,1)S(1)} %collective-permute-done.11.refs_3_), channel_id=1, source_target_pairs={{0,4},{1,5},{4,8},{5,9},{8,12},{9,13},{12,14},{13,15},{14,10},{15,... | collective-permute-start | bytes 589832 | tf_op jit(solution)/shard_map/ppermute | solution.py:317
  29.2 7.5 %collective-permute-start.14 = (bf16[784,128]{1,0:T(8,128)(2,1)S(1)}, bf16[784,128]{1,0:T(8,128)(2,1)S(1)}, u32[]{:S(2)}, u32[]{:S(2)}) collective-permute-start(bf16[784,128]{1,0:T(8,128)(2,1)S(1)} %collective-permute-done.8.refs_0_), channel_id=1, source_target_pairs={{0,2},{1,3},{4,0},{5,1},{8,4},{9,5},{12,8},{13,9},{14,12},{15,13},... | collective-permute-start | bytes 602120 | tf_op jit(solution)/shard_map/ppermute | solution.py:317
  30.8 6.8 %collective-permute-start.15 = (bf16[784,128]{1,0:T(8,128)(2,1)S(1)}, bf16[784,128]{1,0:T(8,128)(2,1)S(1)}, u32[]{:S(2)}, u32[]{:S(2)}) collective-permute-start(bf16[784,128]{1,0:T(8,128)(2,1)S(1)} %collective-permute-done.9.refs_1_), channel_id=1, source_target_pairs={{0,4},{1,5},{4,8},{5,9},{8,12},{9,13},{12,14},{13,15},{14,10},{15,... | collective-permute-start | bytes 602120 | tf_op jit(solution)/shard_map/ppermute | solution.py:317
  36.8 2.5 %collective-permute-start.16 = (bf16[2576,128]{1,0:T(8,128)(2,1)S(1)}, bf16[2576,128]{1,0:T(8,128)(2,1)S(1)}, u32[]{:S(2)}, u32[]{:S(2)}) collective-permute-start(bf16[2576,128]{1,0:T(8,128)(2,1)S(1)} %shard_map.65), channel_id=1, source_target_pairs={{0,1},{1,0},{2,3},{3,2},{4,5},{5,4},{6,7},{7,6},{8,9},{9,8},{10,11... | collective-permute-start | bytes 1978376 | tf_op jit(solution)/shard_map/ppermute | solution.py:317
  37.6 1.6 %collective-permute-start.17 = (bf16[784,128]{1,0:T(8,128)(2,1)S(1)}, bf16[784,128]{1,0:T(8,128)(2,1)S(1)}, u32[]{:S(2)}, u32[]{:S(2)}) collective-permute-start(bf16[784,128]{1,0:T(8,128)(2,1)S(1)} %collective-permute-done.15.refs_1_), channel_id=1, source_target_pairs={{0,1},{1,0},{2,3},{3,2},{4,5},{5,4},{6,7},{7,6},{8,9},{9,8},{10,11... | collective-permute-start | bytes 602120 | tf_op jit(solution)/shard_map/ppermute | solution.py:317
